TPU v7x, 32 devices: a whole 2x2x4 slice. The times are simulated.
32 devices in a mesh: shard: 4 (over y, core), ctx: 2 (over x), tp: 4 (over z).
Axes of the slice: x: 2, y: 2, z: 4, core: 2. Of those that a mesh axis runs over, the one named last changes fastest.
Arguments:
- tokens: bfloat16 [2, 4, 2048, 768], P(None, 'shard', 'ctx'), may hold values from -6 to 6
- segments: int32 [2, 4, 2048], P(None, 'shard', 'ctx'), may hold values from 0 to 5, never falling along the last dimension, each value on 1 to 800 neighbouring positions
- query_weight: bfloat16 [768, 768], P(('shard', 'ctx'), 'tp'), may hold values from -0.21875 to 0.21875
- key_weight: bfloat16 [768, 768], P(('shard', 'ctx'), 'tp'), may hold values from -0.21875 to 0.21875
- value_weight: bfloat16 [768, 768], P(('shard', 'ctx'), 'tp'), may hold values from -0.21875 to 0.21875
- output_weight: bfloat16 [768, 768], P('tp', ('shard', 'ctx')), may hold values from -1.75 to 1.75
- attn_gain: bfloat16 [768], P(('shard', 'ctx')), may hold values from 0.5 to 1.5
- attn_shift: bfloat16 [768], P(('shard', 'ctx')), may hold values from -3 to 3
- inner_weight: bfloat16 [768, 3072], P(('shard', 'ctx'), 'tp'), may hold values from -0.21875 to 0.21875
- outer_weight: bfloat16 [3072, 768], P('tp', ('shard', 'ctx')), may hold values from -0.21875 to 0.21875
- ffn_gain: bfloat16 [768], P(('shard', 'ctx')), may hold values from 0.5 to 1.5
- ffn_shift: bfloat16 [768], P(('shard', 'ctx')), may hold values from -3 to 3
- proj_weight: bfloat16 [768, 128], P(('shard', 'ctx')), may hold values from -0.21875 to 0.21875
- grad_embed: bfloat16 [2, 4, 2048, 128], P(None, 'shard', 'ctx'), may hold values from -48 to 48
Outputs:
- embeddings: float32 [2, 4, 2048, 128], P(None, 'shard', ('ctx', 'tp'))
- grad_tokens: float32 [2, 4, 2048, 768], P(None, 'shard', 'ctx', 'tp')
- query_grad: float32 [768, 768], P(('shard', 'ctx'), 'tp')
- key_grad: float32 [768, 768], P(('shard', 'ctx'), 'tp')
- value_grad: float32 [768, 768], P(('shard', 'ctx'), 'tp')
- output_grad: float32 [768, 768], P('tp', ('shard', 'ctx'))
- attn_gain_grad: float32 [768], P(('shard', 'ctx'))
- attn_shift_grad: float32 [768], P(('shard', 'ctx'))
- inner_grad: float32 [768, 3072], P(('shard', 'ctx'), 'tp')
- outer_grad: float32 [3072, 768], P('tp', ('shard', 'ctx'))
- ffn_gain_grad: float32 [768], P(('shard', 'ctx'))
- ffn_shift_grad: float32 [768], P(('shard', 'ctx'))
- proj_grad: float32 [768, 128], P(('shard', 'ctx'))
Inputs may be any that keep to these rules, and one draw needn't show every extreme that they name: `segments`: within each sequence the document numbers never fall; each of the 6 documents spans 1 to 800 tokens and one spans exactly 800.
All inputs are finite; a program needn't handle non-finite values.
Results may differ from a plain program's by a relative error of at most 0.02.
Values may be sent and summed in bfloat16 or wider, within the bound.
No kernel may reach another device: no remote copies, remote signals or barrier semaphores. Data moves between devices by JAX's collectives and lax.ppermute only.
A program may use at most 192 MiB of HBM per device.

v0:
```python
import functools

import jax
import jax.numpy as jnp
from jax import lax
from jax.sharding import PartitionSpec as P

DH = 64


eps_norm = 1e-12
eps_unit = 1e-06
mask_fill = -1e30


def plain_dot(first_op, second_op):
    return jnp.dot(first_op, second_op, preferred_element_type=jnp.float32)


def cross_rows(first_op, second_op):
    return lax.dot_general(
        first_op, second_op, (((0,), (0,)), ((), ())), preferred_element_type=jnp.float32
    )


def cross_cols(first_op, second_op):
    return lax.dot_general(
        first_op, second_op, (((1,), (1,)), ((), ())), preferred_element_type=jnp.float32
    )


def norm_forward(hidden, gain_vec, offset):
    row_mean = jnp.mean(hidden, axis=-1, keepdims=True)
    centred = hidden - row_mean
    variance = jnp.mean(centred * centred, axis=-1, keepdims=True)
    inv_std = lax.rsqrt(variance + eps_norm)
    normed = centred * inv_std
    return (normed * gain_vec + offset, normed, inv_std)


def norm_backward(grad_out, normed, inv_std, gain_vec):
    scaled = grad_out * gain_vec
    grad_in = inv_std * (
        scaled
        - jnp.mean(scaled, axis=-1, keepdims=True)
        - normed * jnp.mean(scaled * normed, axis=-1, keepdims=True)
    )
    return (grad_in, jnp.sum(grad_out * normed, axis=0), jnp.sum(grad_out, axis=0))


def fetch_weights(
    query_weight,
    key_weight,
    value_weight,
    output_weight,
    attn_gain,
    attn_shift,
    inner_weight,
    outer_weight,
    ffn_gain,
    ffn_shift,
    proj_weight,
):
    return (
        lax.all_gather(query_weight, ("shard", "ctx"), axis=0, tiled=True),
        lax.all_gather(key_weight, ("shard", "ctx"), axis=0, tiled=True),
        lax.all_gather(value_weight, ("shard", "ctx"), axis=0, tiled=True),
        lax.all_gather(output_weight, ("shard", "ctx"), axis=1, tiled=True),
        lax.all_gather(attn_gain, ("shard", "ctx"), axis=0, tiled=True),
        lax.all_gather(attn_shift, ("shard", "ctx"), axis=0, tiled=True),
        lax.all_gather(inner_weight, ("shard", "ctx"), axis=0, tiled=True),
        lax.all_gather(outer_weight, ("shard", "ctx"), axis=1, tiled=True),
        lax.all_gather(ffn_gain, ("shard", "ctx"), axis=0, tiled=True),
        lax.all_gather(ffn_shift, ("shard", "ctx"), axis=0, tiled=True),
        lax.all_gather(proj_weight, ("shard", "ctx"), axis=0, tiled=True),
    )


def per_device(
    tokens,
    segments,
    query_weight,
    key_weight,
    value_weight,
    output_weight,
    attn_gain,
    attn_shift,
    inner_weight,
    outer_weight,
    ffn_gain,
    ffn_shift,
    proj_weight,
    grad_embed,
):
    micro_count = tokens.shape[0]
    seq_count = tokens.shape[1]
    local_len = tokens.shape[2]
    model_width = tokens.shape[3]
    head_cols = query_weight.shape[1]
    heads_here = head_cols // DH
    tok_rows = seq_count * local_len
    block_rows = min(512, local_len)
    per_seq = local_len // block_rows
    block_count = seq_count * per_seq
    score_scale = DH ** (-0.5)
    tp_index = lax.axis_index("tp")
    tp_count = lax.axis_size("tp")
    own_len = local_len // tp_count
    own_start = tp_index * own_len

    def own_rows(flat):
        width = flat.shape[-1]
        return lax.dynamic_slice_in_dim(
            flat.reshape(seq_count, local_len, width), own_start, own_len, 1
        ).reshape(seq_count * own_len, width)

    def as_blocks(flat):
        return flat.reshape(seq_count, -1, flat.shape[-1])

    weight_args = (
        query_weight,
        key_weight,
        value_weight,
        output_weight,
        attn_gain,
        attn_shift,
        inner_weight,
        outer_weight,
        ffn_gain,
        ffn_shift,
        proj_weight,
    )
    grad_totals = None
    embed_list = []
    grad_list = []
    for step_index in range(micro_count):
        gathered = fetch_weights(*weight_args)
        (
            query_full,
            key_full,
            value_full,
            output_full,
            gain_one,
            shift_one,
            inner_full,
            outer_full,
            gain_two,
            shift_two,
            proj_full,
        ) = gathered
        gain_one = gain_one.astype(jnp.float32)
        shift_one = shift_one.astype(jnp.float32)
        gain_two = gain_two.astype(jnp.float32)
        shift_two = shift_two.astype(jnp.float32)
        tok_low = tokens[step_index].reshape(tok_rows, model_width)
        tok_high = tok_low.astype(jnp.float32)
        queries = plain_dot(tok_low, query_full).astype(jnp.bfloat16)
        keys_here = plain_dot(tok_low, key_full).astype(jnp.bfloat16)
        values_here = plain_dot(tok_low, value_full).astype(jnp.bfloat16)
        packed = jnp.concatenate([keys_here, values_here], axis=1).reshape(
            seq_count, local_len, 2 * head_cols
        )
        seg_local = segments[step_index].astype(jnp.bfloat16)
        kv_all, seg_keys_all = (
            lax.all_gather(packed, "ctx", axis=1, tiled=True),
            lax.all_gather(seg_local, "ctx", axis=1, tiled=True),
        )
        full_len = kv_all.shape[1]
        query_seq = queries.reshape(seq_count, local_len, head_cols)

        def block_scores(block_index):
            seq_id = block_index // per_seq
            row_start = block_index % per_seq * block_rows
            query_blk = lax.dynamic_slice_in_dim(
                lax.dynamic_index_in_dim(query_seq, seq_id, 0, False), row_start, block_rows, 0
            )
            kv_seq = lax.dynamic_index_in_dim(kv_all, seq_id, 0, False)
            keys_seq = kv_seq[:, :head_cols].reshape(full_len, heads_here, DH)
            values_seq = kv_seq[:, head_cols:].reshape(full_len, heads_here, DH)
            seg_keys = lax.dynamic_index_in_dim(seg_keys_all, seq_id, 0, False)
            seg_rows = lax.dynamic_slice_in_dim(
                lax.dynamic_index_in_dim(seg_local, seq_id, 0, False), row_start, block_rows, 0
            )
            heads_q = query_blk.reshape(block_rows, heads_here, DH)
            scores = (
                jnp.einsum("qhd,khd->hqk", heads_q, keys_seq, preferred_element_type=jnp.float32)
                * score_scale
            )
            scores = jnp.where((seg_rows[:, None] == seg_keys[None, :])[None], scores, mask_fill)
            return (scores, heads_q, keys_seq, values_seq, seq_id)

        def forward_block(block_index):
            scores, heads_q, keys_seq, values_seq, seq_id = block_scores(block_index)
            row_top = jnp.max(scores, axis=-1, keepdims=True)
            shifted = jnp.exp(scores - row_top)
            denominator = jnp.sum(shifted, axis=-1, keepdims=True)
            probs_low = (shifted / denominator).astype(jnp.bfloat16)
            mixed_blk = jnp.einsum(
                "hqk,khd->qhd", probs_low, values_seq, preferred_element_type=jnp.float32
            )
            return (
                mixed_blk.astype(jnp.bfloat16).reshape(block_rows, head_cols),
                (row_top + jnp.log(denominator))[..., 0],
            )

        mixed_blocks, lse_blocks = lax.map(forward_block, jnp.arange(block_count))
        mixed = mixed_blocks.reshape(tok_rows, head_cols)
        attn_partial = plain_dot(mixed, output_full)
        tok_own = own_rows(tok_high)
        attn_own = lax.psum_scatter(
            as_blocks(attn_partial), "tp", scatter_dimension=1, tiled=True
        ).reshape(-1, model_width)
        first_own, normed_one, inv_one = norm_forward(tok_own + attn_own, gain_one, shift_one)
        first_low = lax.all_gather(
            as_blocks(first_own.astype(jnp.bfloat16)), "tp", axis=1, tiled=True
        ).reshape(tok_rows, model_width)
        pre_act = plain_dot(first_low, inner_full)
        gelu_value, gelu_pull = jax.vjp(functools.partial(jax.nn.gelu, approximate=False), pre_act)
        activated = gelu_value.astype(jnp.bfloat16)
        ffn_partial = plain_dot(activated, outer_full)
        ffn_own = (
            lax.psum_scatter(
                as_blocks(ffn_partial).astype(jnp.bfloat16), "tp", scatter_dimension=1, tiled=True
            )
            .astype(jnp.float32)
            .reshape(-1, model_width)
        )
        second, normed_two, inv_two = norm_forward(first_own + ffn_own, gain_two, shift_two)
        second_low = second.astype(jnp.bfloat16)
        projected = plain_dot(second_low, proj_full)
        inv_norm = lax.rsqrt(jnp.sum(projected * projected, axis=-1, keepdims=True) + eps_unit)
        embedding = projected * inv_norm
        embed_list.append(embedding)
        cot_high = own_rows(grad_embed[step_index].reshape(tok_rows, -1).astype(jnp.float32))
        radial = jnp.sum(cot_high * embedding, axis=-1, keepdims=True)
        grad_projected = (inv_norm * (cot_high - embedding * radial)).astype(jnp.bfloat16)
        proj_part = cross_rows(second_low, grad_projected)
        grad_second = cross_cols(grad_projected, proj_full)
        grad_h2, gain_two_part, shift_two_part = norm_backward(
            grad_second, normed_two, inv_two, gain_two
        )
        grad_ffn = lax.all_gather(
            as_blocks(grad_h2.astype(jnp.bfloat16)), "tp", axis=1, tiled=True
        ).reshape(tok_rows, model_width)
        outer_part = cross_rows(activated, grad_ffn)
        grad_act = cross_cols(grad_ffn, outer_full)
        (grad_pre,) = gelu_pull(grad_act)
        grad_pre = grad_pre.astype(jnp.bfloat16)
        inner_part = cross_rows(first_low, grad_pre)
        hidden_own = (
            lax.psum_scatter(
                as_blocks(cross_cols(grad_pre, inner_full)).astype(jnp.bfloat16),
                "tp",
                scatter_dimension=1,
                tiled=True,
            )
            .astype(jnp.float32)
            .reshape(-1, model_width)
        )
        grad_first = grad_h2 + hidden_own
        grad_h1, gain_one_part, shift_one_part = norm_backward(
            grad_first, normed_one, inv_one, gain_one
        )
        grad_attn = lax.all_gather(
            as_blocks(grad_h1.astype(jnp.bfloat16)), "tp", axis=1, tiled=True
        ).reshape(tok_rows, model_width)
        output_part = cross_rows(mixed, grad_attn)
        grad_mixed = cross_cols(grad_attn, output_full).astype(jnp.bfloat16)
        grad_mixed_blocks = grad_mixed.reshape(block_count, block_rows, heads_here, DH)

        def backward_block(kv_acc, inputs):
            block_index, grad_blk, lse_blk = inputs
            scores, heads_q, keys_seq, values_seq, seq_id = block_scores(block_index)
            probs = jnp.exp(scores - lse_blk[..., None])
            grad_probs = jnp.einsum(
                "qhd,khd->hqk", grad_blk, values_seq, preferred_element_type=jnp.float32
            )
            value_part = jnp.einsum(
                "hqk,qhd->khd",
                probs.astype(jnp.bfloat16),
                grad_blk,
                preferred_element_type=jnp.float32,
            )
            row_delta = jnp.sum(probs * grad_probs, axis=-1, keepdims=True)
            grad_scores = (probs * (grad_probs - row_delta)).astype(jnp.bfloat16)
            query_part = (
                jnp.einsum(
                    "hqk,khd->qhd", grad_scores, keys_seq, preferred_element_type=jnp.float32
                )
                * score_scale
            )
            key_part = (
                jnp.einsum("hqk,qhd->khd", grad_scores, heads_q, preferred_element_type=jnp.float32)
                * score_scale
            )
            combined = jnp.concatenate(
                [key_part.reshape(full_len, head_cols), value_part.reshape(full_len, head_cols)],
                axis=1,
            )
            current = lax.dynamic_index_in_dim(kv_acc, seq_id, 0, False)
            kv_acc = lax.dynamic_update_index_in_dim(kv_acc, current + combined, seq_id, 0)
            return (kv_acc, query_part.reshape(block_rows, head_cols).astype(jnp.bfloat16))

        kv_start = jnp.zeros((seq_count, full_len, 2 * head_cols), jnp.float32)
        kv_grads, query_blocks = lax.scan(
            backward_block, kv_start, (jnp.arange(block_count), grad_mixed_blocks, lse_blocks)
        )
        kv_local = lax.psum_scatter(
            kv_grads.astype(jnp.bfloat16), "ctx", scatter_dimension=1, tiled=True
        )
        grad_queries = query_blocks.reshape(tok_rows, head_cols)
        grad_keys = kv_local[:, :, :head_cols].reshape(tok_rows, head_cols)
        grad_values = kv_local[:, :, head_cols:].reshape(tok_rows, head_cols)
        query_part_w = cross_rows(tok_low, grad_queries)
        key_part_w = cross_rows(tok_low, grad_keys)
        value_part_w = cross_rows(tok_low, grad_values)
        input_part = (
            cross_cols(grad_queries, query_full)
            + cross_cols(grad_keys, key_full)
            + cross_cols(grad_values, value_full)
        )
        input_seq = input_part.reshape(seq_count, local_len, model_width)
        own_part = lax.dynamic_slice_in_dim(input_seq, own_start, own_len, 1) + as_blocks(grad_h1)
        input_seq = lax.dynamic_update_slice_in_dim(input_seq, own_part, own_start, 1)
        grad_tok = lax.psum_scatter(
            input_seq.reshape(tok_rows, model_width).astype(jnp.bfloat16),
            "tp",
            scatter_dimension=1,
            tiled=True,
        ).astype(jnp.float32)
        grad_list.append(grad_tok)
        new_terms = (
            query_part_w,
            key_part_w,
            value_part_w,
            output_part,
            gain_one_part,
            shift_one_part,
            inner_part,
            outer_part,
            gain_two_part,
            shift_two_part,
            proj_part,
        )
        if grad_totals is None:
            grad_totals = new_terms
        else:
            grad_totals = tuple(
                (old_term + new_term for old_term, new_term in zip(grad_totals, new_terms))
            )
    (
        query_acc,
        key_acc,
        value_acc,
        output_acc,
        gain_one_acc,
        shift_one_acc,
        inner_acc,
        outer_acc,
        gain_two_acc,
        shift_two_acc,
        proj_acc,
    ) = grad_totals
    gain_one_acc, shift_one_acc, gain_two_acc, shift_two_acc, proj_acc = (
        lax.psum(gain_one_acc.astype(jnp.bfloat16), "tp").astype(jnp.float32),
        lax.psum(shift_one_acc.astype(jnp.bfloat16), "tp").astype(jnp.float32),
        lax.psum(gain_two_acc.astype(jnp.bfloat16), "tp").astype(jnp.float32),
        lax.psum(shift_two_acc.astype(jnp.bfloat16), "tp").astype(jnp.float32),
        lax.psum(proj_acc.astype(jnp.bfloat16), "tp").astype(jnp.float32),
    )
    reduced = (
        lax.psum_scatter(query_acc, ("shard", "ctx"), scatter_dimension=0, tiled=True),
        lax.psum_scatter(key_acc, ("shard", "ctx"), scatter_dimension=0, tiled=True),
        lax.psum_scatter(value_acc, ("shard", "ctx"), scatter_dimension=0, tiled=True),
        lax.psum_scatter(output_acc, ("shard", "ctx"), scatter_dimension=1, tiled=True),
        lax.psum_scatter(gain_one_acc, ("shard", "ctx"), scatter_dimension=0, tiled=True),
        lax.psum_scatter(shift_one_acc, ("shard", "ctx"), scatter_dimension=0, tiled=True),
        lax.psum_scatter(inner_acc, ("shard", "ctx"), scatter_dimension=0, tiled=True),
        lax.psum_scatter(outer_acc, ("shard", "ctx"), scatter_dimension=1, tiled=True),
        lax.psum_scatter(gain_two_acc, ("shard", "ctx"), scatter_dimension=0, tiled=True),
        lax.psum_scatter(shift_two_acc, ("shard", "ctx"), scatter_dimension=0, tiled=True),
        lax.psum_scatter(proj_acc, ("shard", "ctx"), scatter_dimension=0, tiled=True),
    )
    embeddings = jnp.stack(embed_list).reshape(micro_count, seq_count, own_len, -1)
    grad_tokens = jnp.stack(grad_list).reshape(micro_count, seq_count, local_len, -1)
    return (
        embeddings,
        grad_tokens,
        reduced[0],
        reduced[1],
        reduced[2],
        reduced[3],
        reduced[4],
        reduced[5],
        reduced[6],
        reduced[7],
        reduced[8],
        reduced[9],
        reduced[10],
    )


def solution(mesh):
    placed = (
        P(None, "shard", "ctx", None),
        P(None, "shard", "ctx"),
        P(("shard", "ctx"), "tp"),
        P(("shard", "ctx"), "tp"),
        P(("shard", "ctx"), "tp"),
        P("tp", ("shard", "ctx")),
        P(("shard", "ctx")),
        P(("shard", "ctx")),
        P(("shard", "ctx"), "tp"),
        P("tp", ("shard", "ctx")),
        P(("shard", "ctx")),
        P(("shard", "ctx")),
        P(("shard", "ctx"), None),
        P(None, "shard", "ctx", None),
    )
    return jax.shard_map(
        per_device,
        mesh=mesh,
        in_specs=placed,
        out_specs=(
            P(None, "shard", ("ctx", "tp"), None),
            P(None, "shard", "ctx", "tp"),
            P(("shard", "ctx"), "tp"),
            P(("shard", "ctx"), "tp"),
            P(("shard", "ctx"), "tp"),
            P("tp", ("shard", "ctx")),
            P(("shard", "ctx")),
            P(("shard", "ctx")),
            P(("shard", "ctx"), "tp"),
            P("tp", ("shard", "ctx")),
            P(("shard", "ctx")),
            P(("shard", "ctx")),
            P(("shard", "ctx"), None),
        ),
        check_vma=False,
    )
```

profile of v0, /device:TPU:1, one launch (start us, length us, event | category | flops | bytes accessed | tf_op | source)
XLA Modules:
  0.0 1203.9 jit_solution(17850336290348110757)
XLA Ops:
  8.1 18.7 %all_gather.77 = bf16[768,192]{1,0:T(8,128)(2,1)S(1)} all-gather(bf16[96,192]{1,0:T(8,128)(2,1)} %param.26), channel_id=1, replica_groups=mesh['shard'=4,'ctx'=2,'tp'=4] {'shard','ctx'}, dimensions={0}, use_global_device_ids=true | all-gather | bytes 331776 | tf_op jit(solution)/shard_map/all_gather | solution.py:67
  26.8 16.5 %all_gather.76 = bf16[768,192]{1,0:T(8,128)(2,1)S(1)} all-gather(bf16[96,192]{1,0:T(8,128)(2,1)} %param.25), channel_id=1, replica_groups=mesh['shard'=4,'ctx'=2,'tp'=4] {'shard','ctx'}, dimensions={0}, use_global_device_ids=true | all-gather | bytes 331776 | tf_op jit(solution)/shard_map/all_gather | solution.py:66
  50.7 18.6 %all_gather.75 = bf16[768,192]{1,0:T(8,128)(2,1)S(1)} all-gather(bf16[96,192]{1,0:T(8,128)(2,1)} %param.24), channel_id=1, replica_groups=mesh['shard'=4,'ctx'=2,'tp'=4] {'shard','ctx'}, dimensions={0}, use_global_device_ids=true | all-gather | bytes 331776 | tf_op jit(solution)/shard_map/all_gather | solution.py:65
  76.0 17.0 %all_gather.79 = bf16[192,768]{0,1:T(8,128)(2,1)S(1)} all-gather(bf16[192,96]{0,1:T(8,128)(2,1)S(1)} %copy.50), channel_id=1, replica_groups=mesh['shard'=4,'ctx'=2,'tp'=4] {'shard','ctx'}, dimensions={1}, use_global_device_ids=true | all-gather | bytes 331776 | tf_op jit(solution)/shard_map/all_gather | solution.py:68
  96.6 48.6 %while.59 = (s32[]{:T(128)}, bf16[2,512,192]{1,2,0:T(8,128)(2,1)S(1)}, f32[2,3,512]{2,1,0:T(4,128)S(1)}, s32[2]{0:T(128)S(1)}, bf16[1,1024]{1,0:T(2,128)(2,1)S(1...) while((s32[]{:T(128)}, ...), condition=%wide.region_14.15_spmd, body=%wide.region_11.14_spmd.sunk | while | flops 844200448 | bytes 47912252 | solution.py:206
  148.6 48.8 %while.58 = (s32[]{:T(128)}, bf16[2,512,192]{1,2,0:T(8,128)(2,1)S(1)}, f32[2,3,512]{2,1,0:T(4,128)S(1)}, s32[2]{0:T(128)S(1)}, bf16[1,1024]{1,0:T(2,128)(2,1)S(1...) while((s32[]{:T(128)}, ...), condition=%wide.region_3.4_spmd, body=%wide.region_0.3_spmd.sunk | while | flops 844200448 | bytes 47912252 | solution.py:206
  205.9 14.0 %all-reduce.9 = (bf16[768]{0:T(1024)(128)(2,1)S(1)}, bf16[768]{0:T(1024)(128)(2,1)S(1)}, bf16[768]{0:T(1024)(128)(2,1)S(1)}, bf16[768]{0:T(1024)(128)(2,1)S(1)}) all-reduce(bf16[768]{0:T(1024)(128)(2,1)S(1)} %dynamic-update-slice.1, bf16[768]{0:T(1024)(128)(2,1)S(1)} %dynamic-update-slice, ...), channel_id=1, replica_groups=mesh['shard'=4,'ctx'=2,'tp'=4] {'shard','ctx'}, use_global_device_ids=true, to_apply=%add.1 | all-reduce | flops 3072 | bytes 12288
  221.6 50.0 %reduce-scatter.30.cloned.1.call-done = f32[1,256,768]{2,1,0:T(8,128)} async-done(((f32[1,1024,768]{2,1,0:T(8,128)}), f32[1,256,768]{2,1,0:T(8,128)}) %reduce-scatter.30.cloned.1.call-update) | async-done | bytes 786448 | tf_op jit(solution)/shard_map/reduce_scatter | solution.py:210
  277.6 35.0 %all-gather.25.cloned.1.call-done = bf16[1,1024,768]{2,1,0:T(8,128)(2,1)} async-done(((bf16[1,256,768]{2,1,0:T(8,128)(2,1)}), bf16[1,1024,768]{2,1,0:T(8,128)(2,1)}) %all-gather.25.cloned.1.call-update) | async-done | bytes 1572880 | tf_op jit(solution)/shard_map/all_gather | solution.py:214
  312.6 11.0 multiply_convert_fusion.2
  323.7 14.4 %all-gather.23.cloned.1.call-done = bf16[768,768]{0,1:T(8,128)(2,1)} async-done(((bf16[768,96]{0,1:T(8,128)(2,1)}), bf16[768,768]{0,1:T(8,128)(2,1)}) %all-gather.23.cloned.1.call-update) | async-done | bytes 1179664 | tf_op jit(solution)/shard_map/all_gather | solution.py:72
  342.4 33.3 %all-gather.19.cloned.1.call-done = bf16[1,1024,768]{2,1,0:T(8,128)(2,1)} async-done(((bf16[1,256,768]{2,1,0:T(8,128)(2,1)}), bf16[1,1024,768]{2,1,0:T(8,128)(2,1)}) %all-gather.19.cloned.1.call-update) | async-done | bytes 1572880 | tf_op jit(solution)/shard_map/all_gather | solution.py:214
  375.7 10.8 multiply_convert_fusion.3
  392.2 18.2 %all_gather.87 = bf16[768,128]{1,0:T(8,128)(2,1)S(1)} all-gather(bf16[96,128]{1,0:T(8,128)(2,1)S(1)} %copy-done.74), channel_id=1, replica_groups=mesh['shard'=4,'ctx'=2,'tp'=4] {'shard','ctx'}, dimensions={0}, use_global_device_ids=true | all-gather | bytes 221184 | tf_op jit(solution)/shard_map/all_gather | solution.py:75
  412.3 37.1 %reduce-scatter.32.cloned.1.call-done = bf16[1,256,768]{2,1,0:T(8,128)(2,1)} async-done(((bf16[1,1024,768]{2,1,0:T(8,128)(2,1)}), bf16[1,256,768]{2,1,0:T(8,128)(2,1)}) %reduce-scatter.32.cloned.1.call-update) | async-done | bytes 393232 | tf_op jit(solution)/shard_map/reduce_scatter | solution.py:222
  459.8 33.6 %all-gather.31.cloned.1.call-done = bf16[1024,768]{1,0:T(8,128)(2,1)} async-done(((bf16[256,768]{1,0:T(8,128)(2,1)}), bf16[1024,768]{1,0:T(8,128)(2,1)}) %all-gather.31.cloned.1.call-update) | async-done | bytes 1572880 | tf_op jit(solution)/shard_map/all_gather | solution.py:242
  502.9 44.5 %all-gather.35.cloned.1.call-done = bf16[1024,768]{1,0:T(8,128)(2,1)} async-done(((bf16[256,768]{1,0:T(8,128)(2,1)}), bf16[1024,768]{1,0:T(8,128)(2,1)}) %all-gather.35.cloned.1.call-update) | async-done | bytes 1572880 | tf_op jit(solution)/shard_map/all_gather | solution.py:242
  559.1 34.0 %reduce-scatter.42.cloned.1.call-done = bf16[1,256,768]{2,1,0:T(8,128)(2,1)} async-done(((bf16[1,1024,768]{2,1,0:T(8,128)(2,1)}), bf16[1,256,768]{2,1,0:T(8,128)(2,1)}) %reduce-scatter.42.cloned.1.call-update) | async-done | bytes 393232 | tf_op jit(solution)/shard_map/reduce_scatter | solution.py:251
  600.3 32.0 %all-gather.33.cloned.1.call-done = bf16[1024,768]{1,0:T(8,128)(2,1)} async-done(((bf16[256,768]{1,0:T(8,128)(2,1)}), bf16[1024,768]{1,0:T(8,128)(2,1)}) %all-gather.33.cloned.1.call-update) | async-done | bytes 1572880 | tf_op jit(solution)/shard_map/all_gather | solution.py:264
  636.2 82.0 %while.60 = (s32[]{:T(128)}, f32[1,2048,384]{1,2,0:T(8,128)}, bf16[2,512,192]{1,2,0:T(8,128)(2,1)}, s32[2]{0:T(128)S(1)}, bf16[1,1024,192]{1,2,0:T(8,128)(2,1)S(...) while((s32[]{:T(128)}, f32[1,2048,384]{1,2,0:T(8,128)}, ...), condition=%wide.region_30.31_spmd.clone, body=%wide.region_28.30_spmd.clone.sunk | while | flops 2064448000 | bytes 228061488 | solution.py:305
  649.6 8.6 multiply_reduce_fusion.22
  690.2 8.5 multiply_reduce_fusion.22
  725.8 82.1 %while.61 = (s32[]{:T(128)}, f32[1,2048,384]{1,2,0:T(8,128)}, bf16[2,512,192]{1,2,0:T(8,128)(2,1)}, s32[2]{0:T(128)S(1)}, bf16[1,1024,192]{1,2,0:T(8,128)(2,1)S(...) while((s32[]{:T(128)}, f32[1,2048,384]{1,2,0:T(8,128)}, ...), condition=%wide.region_41.42_spmd.clone, body=%wide.region_39.41_spmd.clone.sunk | while | flops 2064448000 | bytes 228061488 | solution.py:305
  879.0 9.1 all-reduce.10
  888.1 28.9 %all-reduce.8 = (f32[768]{0:T(1024)S(1)}, f32[768]{0:T(1024)S(1)}, f32[768]{0:T(1024)S(1)}, f32[768]{0:T(1024)S(1)}) all-reduce(bf16[768]{0:T(1024)(128)(2,1)S(1)} %get-tuple-element.742, bf16[768]{0:T(1024)(128)(2,1)S(1)} %get-tuple-element.743, ...), channel_id=24, replica_groups=mesh['shard'=4,'ctx'=2,'tp'=4] {'shard','ctx'}, use_global_device_ids=true, to_apply=%region_51.52.clone | all-reduce | flops 3072 | bytes 18432
  922.2 27.7 %reduce-scatter.54.cloned.1.call-done = bf16[192,1024]{1,0:T(8,128)(2,1)} async-done(((bf16[768,1024]{1,0:T(8,128)(2,1)}), bf16[192,1024]{1,0:T(8,128)(2,1)}) %reduce-scatter.54.cloned.1.call-update) | async-done | bytes 393232
  953.0 33.1 %reduce-scatter.50.cloned.1.call-done = f32[96,128]{1,0:T(8,128)} async-done(((f32[768,128]{1,0:T(8,128)}), f32[96,128]{1,0:T(8,128)}) %reduce-scatter.50.cloned.1.call-update) | async-done | bytes 49168 | tf_op jit(solution)/shard_map/reduce_scatter | solution.py:382
  986.2 47.3 %reduce-scatter.48.cloned.1.call-done = f32[768,96]{0,1:T(8,128)} async-done(((f32[768,768]{0,1:T(8,128)}), f32[768,96]{0,1:T(8,128)}) %reduce-scatter.48.cloned.1.call-update) | async-done | bytes 294928 | tf_op jit(solution)/shard_map/reduce_scatter | solution.py:379
  1033.4 46.3 %reduce-scatter.46.cloned.1.call-done = f32[96,768]{1,0:T(8,128)} async-done(((f32[768,768]{1,0:T(8,128)}), f32[96,768]{1,0:T(8,128)}) %reduce-scatter.46.cloned.1.call-update) | async-done | bytes 294928 | tf_op jit(solution)/shard_map/reduce_scatter | solution.py:378
  1079.7 38.6 %reduce-scatter.56.cloned.1.call-done = f32[96,192]{1,0:T(8,128)} async-done(((f32[768,192]{1,0:T(8,128)}), f32[96,192]{1,0:T(8,128)}) %reduce-scatter.56.cloned.1.call-update) | async-done | bytes 73744
  1118.3 38.9 %reduce-scatter.60.cloned.1.call-done = f32[96,192]{1,0:T(8,128)} async-done(((f32[768,192]{1,0:T(8,128)}), f32[96,192]{1,0:T(8,128)}) %reduce-scatter.60.cloned.1.call-update) | async-done | bytes 73744
  1157.2 38.9 %reduce-scatter.58.cloned.1.call-done = f32[96,192]{1,0:T(8,128)} async-done(((f32[768,192]{1,0:T(8,128)}), f32[96,192]{1,0:T(8,128)}) %reduce-scatter.58.cloned.1.call-update) | async-done | bytes 73744
  (601 shorter events, 403.4 us)
Async XLA Ops:
  8.0 88.5 %all-gather.29.cloned.1.call-start = ((), (), s32[]{:S(2)}) async-start(), calls=%async_computation.34 | async-start | bytes 2359296 | tf_op jit(solution)/shard_map/all_gather | solution.py:165
  47.3 101.3 %all-gather.27.cloned.1.call-start = ((), (), s32[]{:S(2)}) async-start(), calls=%async_computation.33 | async-start | bytes 2359296 | tf_op jit(solution)/shard_map/all_gather | solution.py:165
  50.6 169.3 %reduce-scatter.34.cloned.1.call-start = ((), (), s32[]{:S(2)}) async-start(), calls=%async_computation.22 | async-start | bytes 3932160 | tf_op jit(solution)/shard_map/reduce_scatter | solution.py:210
  148.3 123.3 %reduce-scatter.30.cloned.1.call-start = ((), (), s32[]{:S(2)}) async-start(), calls=%async_computation.17 | async-start | bytes 3932160 | tf_op jit(solution)/shard_map/reduce_scatter | solution.py:210
  201.1 76.4 %all-gather.21.cloned.1.call-start = ((), (), s32[]{:S(2)}) async-start(), calls=%async_computation.19 | async-start | bytes 1327104 | tf_op jit(solution)/shard_map/all_gather | solution.py:71
  201.8 110.8 %all-gather.25.cloned.1.call-start = ((), (), s32[]{:S(2)}) async-start(), calls=%async_computation.23 | async-start | bytes 1966080 | tf_op jit(solution)/shard_map/all_gather | solution.py:214
  221.4 228.0 %copy-start.65 = (f32[256]{0:T(256)}, f32[256]{0:T(256)S(1)}, u32[]{:S(2)}) copy-start(f32[256]{0:T(256)S(1)} %broadcast_multiply_fusion.9) | copy-start | bytes 3076
  273.1 176.3 %copy-start.67 = (f32[256]{0:T(256)}, f32[256]{0:T(256)S(1)}, u32[]{:S(2)}) copy-start(f32[256]{0:T(256)S(1)} %broadcast_multiply_fusion.11) | copy-start | bytes 3076
  273.3 176.1 %copy-start.69 = (f32[256]{0:T(256)}, f32[256]{0:T(256)S(1)}, u32[]{:S(2)}) copy-start(f32[256]{0:T(256)S(1)} %add_rsqrt_fusion.2) | copy-start | bytes 3076
  273.4 176.0 %copy-start.71 = (f32[256]{0:T(256)}, f32[256]{0:T(256)S(1)}, u32[]{:S(2)}) copy-start(f32[256]{0:T(256)S(1)} %add_rsqrt_fusion.5) | copy-start | bytes 3076
  275.8 62.2 %all-gather.23.cloned.1.call-start = ((), (), s32[]{:S(2)}) async-start(), calls=%async_computation.20 | async-start | bytes 1327104 | tf_op jit(solution)/shard_map/all_gather | solution.py:72
  276.4 99.3 %all-gather.19.cloned.1.call-start = ((), (), s32[]{:S(2)}) async-start(), calls=%async_computation.18 | async-start | bytes 1966080 | tf_op jit(solution)/shard_map/all_gather | solution.py:214
  277.1 135.2 %reduce-scatter.36.cloned.1.call-start = ((), (), s32[]{:S(2)}) async-start(), calls=%async_computation.24 | async-start | bytes 1966080 | tf_op jit(solution)/shard_map/reduce_scatter | solution.py:222
  342.3 107.0 %reduce-scatter.32.cloned.1.call-start = ((), (), s32[]{:S(2)}) async-start(), calls=%async_computation.21 | async-start | bytes 1966080 | tf_op jit(solution)/shard_map/reduce_scatter | solution.py:222
  391.5 101.8 %all-gather.31.cloned.1.call-start = ((), (), s32[]{:S(2)}) async-start(), calls=%async_computation.35 | async-start | bytes 1966080 | tf_op jit(solution)/shard_map/all_gather | solution.py:242
  457.4 90.0 %all-gather.35.cloned.1.call-start = ((), (), s32[]{:S(2)}) async-start(), calls=%async_computation.37 | async-start | bytes 1966080 | tf_op jit(solution)/shard_map/all_gather | solution.py:242
  459.7 97.3 %reduce-scatter.38.cloned.1.call-start = ((), (), s32[]{:S(2)}) async-start(), calls=%async_computation.25 | async-start | bytes 1966080 | tf_op jit(solution)/shard_map/reduce_scatter | solution.py:251
  502.9 90.3 %reduce-scatter.42.cloned.1.call-start = ((), (), s32[]{:S(2)}) async-start(), calls=%async_computation.27 | async-start | bytes 1966080 | tf_op jit(solution)/shard_map/reduce_scatter | solution.py:251
  557.0 75.3 %all-gather.33.cloned.1.call-start = ((), (), s32[]{:S(2)}) async-start(), calls=%async_computation.36 | async-start | bytes 1966080 | tf_op jit(solution)/shard_map/all_gather | solution.py:264
  596.5 125.2 %all-gather.37.cloned.1.call-start = ((), (), s32[]{:S(2)}) async-start(), calls=%async_computation.38 | async-start | bytes 1966080 | tf_op jit(solution)/shard_map/all_gather | solution.py:264
  600.2 220.7 %reduce-scatter.40.cloned.1.call-start = ((), (), s32[]{:S(2)}) async-start(), calls=%async_computation.26 | async-start | bytes 2359296 | tf_op jit(solution)/shard_map/reduce_scatter | solution.py:308
  721.6 115.2 %reduce-scatter.44.cloned.1.call-start = ((), (), s32[]{:S(2)}) async-start(), calls=%async_computation.28 | async-start | bytes 2359296 | tf_op jit(solution)/shard_map/reduce_scatter | solution.py:308
  811.3 35.4 %all-reduce.13.cloned.1.call-start = ((), (), s32[]{:S(2)}) async-start(), calls=%async_computation.31 | async-start | bytes 393216 | tf_op jit(solution)/shard_map/psum | solution.py:369
  814.7 104.6 %reduce-scatter.62.cloned.1.call-start = ((), (), s32[]{:S(2)}) async-start(), calls=%async_computation.44 | async-start | bytes 884736
  820.8 100.1 %reduce-scatter.52.cloned.1.call-start = ((), (), s32[]{:S(2)}) async-start(), calls=%async_computation.39 | async-start | bytes 1966080
  825.9 124.0 %reduce-scatter.54.cloned.1.call-start = ((), (), s32[]{:S(2)}) async-start(), calls=%async_computation.40 | async-start | bytes 1966080
  841.8 144.4 %reduce-scatter.50.cloned.1.call-start = ((), (), s32[]{:S(2)}) async-start(), calls=%async_computation.32 | async-start | bytes 442368 | tf_op jit(solution)/shard_map/reduce_scatter | solution.py:382
  848.4 185.0 %reduce-scatter.48.cloned.1.call-start = ((), (), s32[]{:S(2)}) async-start(), calls=%async_computation.30 | async-start | bytes 2654208 | tf_op jit(solution)/shard_map/reduce_scatter | solution.py:379
  854.7 225.0 %reduce-scatter.46.cloned.1.call-start = ((), (), s32[]{:S(2)}) async-start(), calls=%async_computation.29 | async-start | bytes 2654208 | tf_op jit(solution)/shard_map/reduce_scatter | solution.py:378
  859.9 258.4 %reduce-scatter.56.cloned.1.call-start = ((), (), s32[]{:S(2)}) async-start(), calls=%async_computation.41 | async-start | bytes 884736
  865.1 292.1 %reduce-scatter.60.cloned.1.call-start = ((), (), s32[]{:S(2)}) async-start(), calls=%async_computation.43 | async-start | bytes 884736
  871.2 325.0 %reduce-scatter.58.cloned.1.call-start = ((), (), s32[]{:S(2)}) async-start(), calls=%async_computation.42 | async-start | bytes 884736
  (136 other events, 910.0 us)
Sparse Core Ops, SparseCore 0:
  47.4 28.5 all-gather.28
  78.1 28.1 all-gather.26
  148.4 60.7 reduce-scatter.33
  211.3 60.2 reduce-scatter.29
  503.0 53.5 reduce-scatter.37
  558.7 34.3 reduce-scatter.41
  721.7 25.2 reduce-scatter.39
  811.5 25.3 reduce-scatter.43
  840.0 34.6 reduce-scatter.61
  876.9 35.7 reduce-scatter.51
  915.6 34.2 reduce-scatter.53
  953.6 32.4 reduce-scatter.49
  990.4 42.9 reduce-scatter.47
  1037.2 42.4 reduce-scatter.45
  1083.6 34.6 reduce-scatter.55
  1122.2 34.9 reduce-scatter.59
  1161.1 34.9 reduce-scatter.57
Sparse Core Ops, SparseCore 1:
  203.5 24.9 all-gather.20
  275.9 36.7 all-gather.24
  314.4 23.6 all-gather.22
  339.6 36.1 all-gather.18
  378.0 34.2 reduce-scatter.35
  415.2 34.1 reduce-scatter.31
  457.5 35.7 all-gather.30
  494.8 52.6 all-gather.34
  596.6 35.6 all-gather.32
  633.9 35.8 all-gather.36
  814.8 31.9 all-reduce.12
where the time goes:
time: 1210 us; the launch traced here: 1200 us
  waiting for transfers between devices  602 us (50%)
  matrix products  239 us (20%)
  blocking collectives  148 us (12%)
  other arithmetic  103 us (9%)
  local copies, waits for them, and re-layouts  73.1 us (6%)
  between operations  18.9 us (2%)
  loops' own time  17.1 us (1%)
    unnamed x34, waiting for transfers between devices  146 us
    all_gather x2, waiting for transfers between devices, per_device(): lax.all_gather(as_blocks(grad_h2.astype(jnp.bfloat16)), 'tp', axis=1, til...  78.1 us
    all_gather x2, waiting for transfers between devices, per_device(): lax.all_gather(as_blocks(first_own.astype(jnp.bfloat16)), 'tp', axis=1, t...  68.4 us
    reduce_scatter x2, waiting for transfers between devices, per_device(): lax.psum_scatter(as_blocks(attn_partial), 'tp', scatter_dimension=1, tile...  50 us
    dot_general x8, matrix products, block_scores(): jnp.einsum('qhd,khd->hqk', heads_q, keys_seq, preferred_element_type=jnp....  49.7 us
    reduce_scatter x1, waiting for transfers between devices, per_device(): lax.psum_scatter(outer_acc, ('shard', 'ctx'), scatter_dimension=1, tiled=...  47.3 us
    reduce_scatter x1, waiting for transfers between devices, per_device(): lax.psum_scatter(inner_acc, ('shard', 'ctx'), scatter_dimension=0, tiled=...  46.3 us
    unnamed x2, blocking collectives  42.8 us
  transfers between devices with their start and end apart: 28, of which 19 were waited for; matrix products, arithmetic and copies ran while one was open for 31% of the time, Pallas kernels for 0%

commit v1 on v0

v1 whole, which is shorter than its diff:
```python
import functools

import jax
import jax.numpy as jnp
from jax import lax
from jax.experimental import pallas as pl
from jax.experimental.pallas import tpu as pltpu
from jax.sharding import PartitionSpec as P

DH = 64
SEG_COUNT = 6
SEG_MOST = 800
BQ = 256
BK = 256

eps_norm = 1e-12
eps_unit = 1e-06
mask_fill = -1e30

NN = (((1,), (0,)), ((), ()))
NT = (((1,), (1,)), ((), ()))
TN = (((0,), (0,)), ((), ()))


def dot(first_op, second_op, dims=NN):
    return lax.dot_general(first_op, second_op, dims, preferred_element_type=jnp.float32)


def norm_forward(hidden, gain_vec, offset):
    row_mean = jnp.mean(hidden, axis=-1, keepdims=True)
    centred = hidden - row_mean
    variance = jnp.mean(centred * centred, axis=-1, keepdims=True)
    inv_std = lax.rsqrt(variance + eps_norm)
    normed = centred * inv_std
    return (normed * gain_vec + offset, normed, inv_std)


def norm_backward(grad_out, normed, inv_std, gain_vec):
    scaled = grad_out * gain_vec
    grad_in = inv_std * (
        scaled
        - jnp.mean(scaled, axis=-1, keepdims=True)
        - normed * jnp.mean(scaled * normed, axis=-1, keepdims=True)
    )
    return (grad_in, jnp.sum(grad_out * normed, axis=0), jnp.sum(grad_out, axis=0))


def swap(v, axis, bit):
    count = lax.axis_size(axis)
    return lax.ppermute(v, axis, [(i, i ^ bit) for i in range(count)])


def route(v, target):
    shards, halves, groups = (lax.axis_size(a) for a in ("shard", "ctx", "tp"))

    def flat(s, c, t):
        return (s * halves + c) * groups + t

    pairs = []
    for s in range(shards):
        for c in range(halves):
            for t in range(groups):
                to = target(s, c, t)
                if to is not None:
                    pairs.append((flat(s, c, t), flat(*to)))
    return lax.ppermute(v, ("shard", "ctx", "tp"), pairs)


def row_steps(order):
    shard_bits = lax.axis_size("shard").bit_length() - 1
    named = {"x": [("ctx", 1, 1 + shard_bits)], "core": [("shard", 1, shard_bits)]}
    named["y"] = [("shard", 1 << i, shard_bits - i) for i in range(1, shard_bits)]
    return [step for name in order for step in named[name]]


def my_bit(axis, bit):
    return (lax.axis_index(axis) // bit) % 2


def gather_tree(own, order, with_tp=True):
    shard_bits = lax.axis_size("shard").bit_length() - 1
    cur = own.reshape((1,) * (shard_bits + 2) + own.shape)
    if with_tp:
        t = lax.axis_index("tp")
        parts = [cur] + [swap(cur, "tp", d) for d in range(1, lax.axis_size("tp"))]
        cur = jnp.concatenate([lax.select_n(t ^ j, *parts) for j in range(len(parts))], axis=0)
    for axis, bit, dim in row_steps(order):
        other = swap(cur, axis, bit)
        first = my_bit(axis, bit) == 0
        cur = jnp.concatenate(
            [jnp.where(first, cur, other), jnp.where(first, other, cur)], axis=dim
        )
    return cur.reshape(cur.shape[0], -1, cur.shape[-1])


def scatter_tree(full, order, with_tp=True):
    shard_bits = lax.axis_size("shard").bit_length() - 1
    rows = full.shape[1] // (lax.axis_size("shard") * lax.axis_size("ctx"))
    cur = full.reshape((full.shape[0],) + (2,) * (shard_bits + 1) + (rows, full.shape[-1]))
    steps = row_steps(order)
    for axis, bit, dim in steps:
        mine = my_bit(axis, bit)
        other = swap(lax.dynamic_slice_in_dim(cur, 1 - mine, 1, dim), axis, bit)
        kept = lax.dynamic_slice_in_dim(cur, mine, 1, dim)
        cur = kept.astype(jnp.float32) + other.astype(jnp.float32)
        if with_tp or (axis, bit, dim) != steps[-1]:
            cur = cur.astype(jnp.bfloat16)
    if with_tp:
        t = lax.axis_index("tp")
        parts = [
            swap(lax.dynamic_slice_in_dim(cur, t ^ d, 1, 0), "tp", d)
            for d in range(1, lax.axis_size("tp"))
        ]
        cur = lax.dynamic_slice_in_dim(cur, t, 1, 0).astype(jnp.float32)
        for part in parts:
            cur = cur + part.astype(jnp.float32)
    return cur.reshape(rows, -1)


def two_heads(pair):
    lane = lax.broadcasted_iota(jnp.int32, pair.shape, 1)
    zero = jnp.zeros_like(pair)
    return jnp.concatenate(
        [jnp.where(lane < DH, pair, zero), jnp.where(lane < DH, zero, pair)], axis=0
    )


def fold_heads(wide):
    rows = wide.shape[1] // 2
    both = jnp.concatenate([wide[:DH, :rows], wide[DH:, rows:]], axis=0)
    return both.T


def block_of(meta, i):
    qb = pl.program_id(0)
    here = meta[1, qb]
    is_here = i < here
    kb = jnp.where(is_here, meta[0, qb] + i, meta[2, qb] + (i - here))
    return kb, kb * BK + jnp.where(is_here, meta[4, 0], meta[4, 1])


def key_mask(bounds, base):
    key_pos = lax.broadcasted_iota(jnp.int32, (BK, BQ), 0) + base
    same = (key_pos >= bounds[0:1, :]) & (key_pos < bounds[1:2, :])
    return jnp.concatenate([same, same], axis=1)


def attn_fwd_kernel(meta, q_ref, bounds, k_ref, v_ref, o_ref, lse_ref, acc, top, den):
    qb = pl.program_id(0)
    pairs = q_ref.shape[1] // 128
    acc[...] = jnp.zeros_like(acc)
    top[...] = jnp.full_like(top, mask_fill)
    den[...] = jnp.zeros_like(den)
    queries = [two_heads(q_ref[:, 128 * p : 128 * p + 128]) for p in range(pairs)]

    @pl.loop(0, meta[1, qb] + meta[3, qb])
    def _(i):
        kb, base = block_of(meta, i)
        rows = pl.ds(pl.multiple_of(kb * BK, BK), BK)
        same = key_mask(bounds, base)
        for p in range(pairs):
            cols = slice(128 * p, 128 * p + 128)
            s = dot(k_ref[rows, cols], queries[p], NT)
            s = jnp.where(same, s, mask_fill)
            old = top[p]
            new = jnp.maximum(old, jnp.max(s, axis=0, keepdims=True))
            e = jnp.exp(s - new)
            shrink = jnp.exp(old - new)
            den[p] = den[p] * shrink + jnp.sum(e, axis=0, keepdims=True)
            top[p] = new
            acc[p] = acc[p] * shrink + dot(v_ref[rows, cols], e.astype(jnp.bfloat16), TN)

    for p in range(pairs):
        out = fold_heads(acc[p] / den[p])
        o_ref[:, 128 * p : 128 * p + 128] = out.astype(o_ref.dtype)
        lse_ref[p] = top[p] + jnp.log(den[p])


def attn_bwd_kernel(
    meta, q_ref, do_ref, bounds, lse_ref, delta_ref, k_ref, v_ref, dq_ref, dk_ref, dv_ref, dk_acc, dv_acc, dq_acc
):
    qb = pl.program_id(0)
    pairs = q_ref.shape[1] // 128

    @pl.when(qb == 0)
    def _():
        dk_acc[...] = jnp.zeros_like(dk_acc)
        dv_acc[...] = jnp.zeros_like(dv_acc)

    dq_acc[...] = jnp.zeros_like(dq_acc)
    queries = [two_heads(q_ref[:, 128 * p : 128 * p + 128]) for p in range(pairs)]
    grads = [two_heads(do_ref[:, 128 * p : 128 * p + 128]) for p in range(pairs)]

    @pl.loop(0, meta[1, qb] + meta[3, qb])
    def _(i):
        kb, base = block_of(meta, i)
        rows = pl.ds(pl.multiple_of(kb * BK, BK), BK)
        same = key_mask(bounds, base)
        for p in range(pairs):
            cols = slice(128 * p, 128 * p + 128)
            keys = k_ref[rows, cols]
            s = dot(keys, queries[p], NT)
            probs = jnp.exp(jnp.where(same, s, mask_fill) - lse_ref[p])
            dp = dot(v_ref[rows, cols], grads[p], NT)
            ds = (probs * (dp - delta_ref[p])).astype(jnp.bfloat16)
            dv_acc[rows, cols] += dot(probs.astype(jnp.bfloat16), grads[p])
            dk_acc[rows, cols] += dot(ds, queries[p])
            dq_acc[p] += dot(keys, ds, TN)

    for p in range(pairs):
        out = fold_heads(dq_acc[p]) * (DH**-0.5)
        dq_ref[:, 128 * p : 128 * p + 128] = out.astype(dq_ref.dtype)

    @pl.when(qb == pl.num_programs(0) - 1)
    def _():
        dk_ref[...] = dk_acc[...].astype(dk_ref.dtype)
        dv_ref[...] = dv_acc[...].astype(dv_ref.dtype)


def whole(shape):
    return pl.BlockSpec(shape, lambda i, m: (0,) * len(shape))


def attn_forward(meta, queries, bounds, keys, values):
    rows, width = queries.shape
    span = keys.shape[0]
    pairs = width // 128
    return pl.pallas_call(
        attn_fwd_kernel,
        grid_spec=pltpu.PrefetchScalarGridSpec(
            num_scalar_prefetch=1,
            grid=(rows // BQ,),
            in_specs=[
                pl.BlockSpec((BQ, width), lambda i, m: (i, 0)),
                pl.BlockSpec((2, BQ), lambda i, m: (0, i)),
                whole((span, width)),
                whole((span, width)),
            ],
            out_specs=[
                pl.BlockSpec((BQ, width), lambda i, m: (i, 0)),
                pl.BlockSpec((pairs, 1, 2 * BQ), lambda i, m: (0, 0, i)),
            ],
            scratch_shapes=[
                pltpu.VMEM((pairs, 128, 2 * BQ), jnp.float32),
                pltpu.VMEM((pairs, 1, 2 * BQ), jnp.float32),
                pltpu.VMEM((pairs, 1, 2 * BQ), jnp.float32),
            ],
        ),
        out_shape=[
            jax.ShapeDtypeStruct((rows, width), jnp.bfloat16),
            jax.ShapeDtypeStruct((pairs, 1, 2 * rows), jnp.float32),
        ],
        compiler_params=pltpu.CompilerParams(vmem_limit_bytes=40 * 2**20),
        cost_estimate=pl.CostEstimate(
            flops=8 * rows * span * width // 4, bytes_accessed=8 * 2**20, transcendentals=rows * span * pairs
        ),
        name="attn_fwd",
    )(meta, queries, bounds, keys, values)


def attn_backward(meta, queries, grads, bounds, lse, delta, keys, values):
    rows, width = queries.shape
    span = keys.shape[0]
    pairs = width // 128
    tile = pl.BlockSpec((BQ, width), lambda i, m: (i, 0))
    line = pl.BlockSpec((pairs, 1, 2 * BQ), lambda i, m: (0, 0, i))
    return pl.pallas_call(
        attn_bwd_kernel,
        grid_spec=pltpu.PrefetchScalarGridSpec(
            num_scalar_prefetch=1,
            grid=(rows // BQ,),
            in_specs=[
                tile,
                tile,
                pl.BlockSpec((2, BQ), lambda i, m: (0, i)),
                line,
                line,
                whole((span, width)),
                whole((span, width)),
            ],
            out_specs=[tile, whole((span, width)), whole((span, width))],
            scratch_shapes=[
                pltpu.VMEM((span, width), jnp.float32),
                pltpu.VMEM((span, width), jnp.float32),
                pltpu.VMEM((pairs, 128, 2 * BQ), jnp.float32),
            ],
        ),
        out_shape=[
            jax.ShapeDtypeStruct((rows, width), jnp.bfloat16),
            jax.ShapeDtypeStruct((span, width), jnp.bfloat16),
            jax.ShapeDtypeStruct((span, width), jnp.bfloat16),
        ],
        compiler_params=pltpu.CompilerParams(vmem_limit_bytes=48 * 2**20),
        cost_estimate=pl.CostEstimate(
            flops=20 * rows * span * width // 4, bytes_accessed=12 * 2**20, transcendentals=rows * span * pairs
        ),
        name="attn_bwd",
    )(meta, queries, grads, bounds, lse, delta, keys, values)


def pack_heads(parts):
    return jnp.concatenate([p[:, :128] for p in parts] + [p[:, 128:] for p in parts], axis=1)


def unpack_heads(packed):
    return [
        jnp.concatenate(
            [packed[:, 128 * i : 128 * i + 128], packed[:, 512 + DH * i : 512 + DH * i + DH]], axis=1
        )
        for i in range(4)
    ]


def head_columns(two, i):
    return jnp.concatenate(
        [
            two[0][:, 128 * i : 128 * i + 128],
            two[1][:, 128 * i : 128 * i + 128],
            two[0][:, 512 + DH * i : 512 + DH * i + DH],
            two[1][:, 512 + DH * i : 512 + DH * i + DH],
        ],
        axis=1,
    )


def to_slices(parts):
    first = [p[:, :128] for p in parts] + [p[:, 256 : 256 + DH] for p in parts]
    second = [p[:, 128:256] for p in parts] + [p[:, 256 + DH :] for p in parts]
    return jnp.stack([jnp.concatenate(first, axis=1), jnp.concatenate(second, axis=1)])


def per_device(
    tokens,
    segments,
    query_weight,
    key_weight,
    value_weight,
    output_weight,
    attn_gain,
    attn_shift,
    inner_weight,
    outer_weight,
    ffn_gain,
    ffn_shift,
    proj_weight,
    grad_embed,
):
    length, model_width = tokens.shape[2:]
    half = length // 2
    core = lax.axis_index("shard") % 2
    ctx = lax.axis_index("ctx")
    group = lax.axis_index("tp")
    micro, seat = group // 2, group % 2
    owner = core == seat
    edge = min(SEG_MOST, length)
    bf16, f32 = jnp.bfloat16, jnp.float32

    tok_m = lax.dynamic_index_in_dim(tokens, micro, 0, False)[0]
    seg_m = lax.dynamic_index_in_dim(segments, micro, 0, False)[0]
    cot_m = lax.dynamic_index_in_dim(grad_embed, micro, 0, False)[0]
    tok_here = jnp.where(owner, tok_m, swap(tok_m, "shard", 1))
    seg_here = jnp.where(owner, seg_m, swap(seg_m, "shard", 1))
    seg_far = swap(seg_here, "ctx", 1)
    sent = lax.dynamic_slice_in_dim(tok_m, (1 - ctx) * (length - edge), edge, 0)
    got = route(sent, lambda s, c, t: (s, 1 - c, t) if s % 2 == t % 2 else None)
    got = jnp.where(owner, got, swap(got, "shard", 1))
    tok_far = lax.dynamic_update_slice_in_dim(
        jnp.zeros_like(tok_here), got, ctx * (length - edge), 0
    )
    tok_all = jnp.concatenate([tok_here, tok_far], axis=0)
    cot_sent = swap(lax.dynamic_slice_in_dim(cot_m, (1 - core) * half, half, 0), "shard", 1)
    cot = jnp.where(owner, lax.dynamic_slice_in_dim(cot_m, core * half, half, 0), cot_sent)
    cot = cot.astype(f32)

    heads_own = pack_heads([query_weight, key_weight, value_weight, output_weight.T])
    heads_full = gather_tree(heads_own, ("y", "x", "core"))
    inner_full = gather_tree(inner_weight, ("x", "y", "core"))
    outer_full = gather_tree(outer_weight.T, ("y", "x", "core"))
    proj_full = gather_tree(proj_weight, ("x", "y", "core"), False)[0]
    norms_own = jnp.stack([attn_gain, attn_shift, ffn_gain, ffn_shift], axis=1)
    norms = gather_tree(norms_own, ("x", "y", "core"), False)[0].astype(f32)
    gain_one, shift_one, gain_two, shift_two = (norms[:, i][None, :] for i in range(4))
    two = lax.dynamic_slice_in_dim(heads_full, 2 * core, 2, 0)
    query_w, key_w, value_w, output_w = (head_columns(two, i) for i in range(4))
    output_all = jnp.concatenate([head_columns(heads_full[:2], 3), head_columns(heads_full[2:], 3)], axis=1)

    seg_all = jnp.where(
        ctx == 0, jnp.concatenate([seg_here, seg_far]), jnp.concatenate([seg_far, seg_here])
    )
    upto = [jnp.sum((seg_all <= d).astype(jnp.int32)) for d in range(SEG_COUNT)]
    first = jnp.zeros_like(seg_here)
    last = jnp.full_like(seg_here, upto[0])
    for d in range(1, SEG_COUNT):
        first = jnp.where(seg_here >= d, upto[d - 1], first)
        last = jnp.where(seg_here >= d, upto[d], last)
    bounds = jnp.stack([first, last])
    here, far = ctx * length, (1 - ctx) * length
    low, high = first[::BQ], last[BQ - 1 :: BQ]
    ks = jnp.clip(low - here, 0, length) // BK
    ke = (jnp.clip(high - here, 0, length) + BK - 1) // BK
    rs = jnp.clip(low - far, 0, length) // BK
    re = (jnp.clip(high - far, 0, length) + BK - 1) // BK
    offsets = jnp.zeros_like(ks).at[0].set(here).at[1].set(far - length)
    meta = jnp.stack([ks, ke - ks, rs + length // BK, jnp.maximum(re - rs, 0), offsets])

    queries = (dot(tok_here, query_w).astype(bf16).astype(f32) * DH**-0.5).astype(bf16)
    keys = dot(tok_all, key_w).astype(bf16)
    values = dot(tok_all, value_w).astype(bf16)
    mixed, lse = attn_forward(meta, queries, bounds, keys, values)
    mixed_got = swap(lax.dynamic_slice_in_dim(mixed, (1 - core) * half, half, 0), "shard", 1)
    mixed_kept = lax.dynamic_slice_in_dim(mixed, core * half, half, 0)
    mixed_own = jnp.concatenate(
        [jnp.where(core == 0, mixed_kept, mixed_got), jnp.where(core == 0, mixed_got, mixed_kept)],
        axis=1,
    )
    attn_out = dot(mixed_own, output_all, NT)

    tok_own = lax.dynamic_slice_in_dim(tok_here, core * half, half, 0).astype(f32)
    first_out, normed_one, inv_one = norm_forward(tok_own + attn_out, gain_one, shift_one)
    first_low = first_out.astype(bf16)
    pre_act = jnp.einsum("td,zdf->ztf", first_low, inner_full, preferred_element_type=f32)
    gelu_value, gelu_pull = jax.vjp(functools.partial(jax.nn.gelu, approximate=False), pre_act)
    activated = gelu_value.astype(bf16)
    ffn_out = jnp.einsum("ztf,zdf->td", activated, outer_full, preferred_element_type=f32)
    second, normed_two, inv_two = norm_forward(first_out + ffn_out, gain_two, shift_two)
    second_low = second.astype(bf16)
    projected = dot(second_low, proj_full)
    inv_norm = lax.rsqrt(jnp.sum(projected * projected, axis=-1, keepdims=True) + eps_unit)
    embedding = projected * inv_norm

    radial = jnp.sum(cot * embedding, axis=-1, keepdims=True)
    grad_projected = (inv_norm * (cot - embedding * radial)).astype(bf16)
    proj_part = dot(second_low, grad_projected, TN)
    grad_second = dot(grad_projected, proj_full, NT)
    grad_h2, gain_two_part, shift_two_part = norm_backward(
        grad_second, normed_two, inv_two, gain_two
    )
    grad_ffn = grad_h2.astype(bf16)
    outer_part = jnp.einsum("td,ztf->zdf", grad_ffn, activated, preferred_element_type=f32)
    grad_act = jnp.einsum("td,zdf->ztf", grad_ffn, outer_full, preferred_element_type=f32)
    (grad_pre,) = gelu_pull(grad_act)
    grad_pre = grad_pre.astype(bf16)
    inner_part = jnp.einsum("td,ztf->zdf", first_low, grad_pre, preferred_element_type=f32)
    hidden = jnp.einsum("ztf,zdf->td", grad_pre, inner_full, preferred_element_type=f32)
    grad_h1, gain_one_part, shift_one_part = norm_backward(
        grad_h2 + hidden, normed_one, inv_one, gain_one
    )
    grad_attn_own = grad_h1.astype(bf16)
    other = swap(grad_attn_own, "shard", 1)
    grad_attn = jnp.concatenate(
        [jnp.where(core == 0, grad_attn_own, other), jnp.where(core == 0, other, grad_attn_own)],
        axis=0,
    )
    output_part = dot(grad_attn, mixed, TN)
    grad_mixed = dot(grad_attn, output_w).astype(bf16)

    pairs = mixed.shape[1] // 128
    products = grad_mixed.astype(f32) * mixed.astype(f32)
    delta = jnp.sum(products.reshape(length // BQ, BQ, pairs, 2, DH), axis=-1)
    delta = delta.transpose(2, 0, 3, 1).reshape(pairs, 1, 2 * length)
    grad_q, grad_k, grad_v = attn_backward(
        meta, queries, grad_mixed, bounds, lse, delta, keys, values
    )
    query_part = dot(tok_here, grad_q, TN)
    key_part = dot(tok_all, grad_k, TN)
    value_part = dot(tok_all, grad_v, TN)
    input_all = dot(grad_k, key_w, NT) + dot(grad_v, value_w, NT)
    input_here = input_all[:length] + dot(grad_q, query_w, NT)
    input_far = input_all[length:]

    def halve(full):
        theirs = lax.dynamic_slice_in_dim(full, (1 - core) * half, half, 0).astype(bf16)
        return lax.dynamic_slice_in_dim(full, core * half, half, 0) + swap(
            theirs, "shard", 1
        ).astype(f32)

    from_far = swap(halve(input_far).astype(bf16), "ctx", 1).astype(f32)
    grad_tok = (halve(input_here) + from_far + grad_h1).astype(bf16)
    own_cols = model_width // lax.axis_size("tp")
    col_parts = [grad_tok[:, own_cols * j : own_cols * (j + 1)] for j in range(4)]
    place = 2 * micro + core
    arrived = [
        route(
            lax.select_n(place ^ d, *col_parts),
            lambda s, c, t, d=d: (s - s % 2 + t % 2, c, (2 * (t // 2) + s % 2) ^ d),
        )
        for d in range(4)
    ]
    grad_tokens = jnp.stack([lax.select_n(group ^ j, *arrived) for j in range(4)])
    grad_tokens = grad_tokens.reshape(2, 1, length, own_cols).astype(f32)

    quarter = half // 2
    emb_parts = [embedding[:quarter], embedding[quarter:]]
    emb_got = [
        route(
            lax.select_n(micro ^ d, *emb_parts),
            lambda s, c, t, d=d: (s - s % 2 + t % 2, c, 2 * (s % 2) + ((t // 2) ^ d)),
        )
        for d in range(2)
    ]
    embeddings = jnp.stack([lax.select_n((group % 2) ^ m, *emb_got) for m in range(2)])
    embeddings = embeddings.reshape(2, 1, quarter, -1)

    outer_grad = scatter_tree(outer_part.astype(bf16), ("core", "x", "y")).T
    inner_grad = scatter_tree(inner_part.astype(bf16), ("core", "y", "x"))
    slices = to_slices([query_part, key_part, value_part, output_part]).astype(bf16)
    zero = jnp.zeros_like(slices)
    slices = jnp.concatenate(
        [jnp.where(core == 0, slices, zero), jnp.where(core == 0, zero, slices)], axis=0
    )
    query_grad, key_grad, value_grad, output_grad = unpack_heads(
        scatter_tree(slices, ("core", "x", "y"))
    )
    small = jnp.concatenate(
        [proj_part]
        + [
            v[:, None]
            for v in (gain_one_part, shift_one_part, gain_two_part, shift_two_part)
        ],
        axis=1,
    ).astype(bf16)
    small = scatter_tree(small[None], ("core", "x", "y"), False).astype(bf16)
    parts = [swap(small, "tp", d) for d in range(1, 4)]
    small = small.astype(f32)
    for part in parts:
        small = small + part.astype(f32)
    p_width = proj_part.shape[1]
    return (
        embeddings,
        grad_tokens,
        query_grad,
        key_grad,
        value_grad,
        output_grad.T,
        small[:, p_width],
        small[:, p_width + 1],
        inner_grad,
        outer_grad,
        small[:, p_width + 2],
        small[:, p_width + 3],
        small[:, :p_width],
    )


def solution(mesh):
    rows = ("shard", "ctx")
    placed = (
        P(None, "shard", "ctx", None),
        P(None, "shard", "ctx"),
        P(rows, "tp"),
        P(rows, "tp"),
        P(rows, "tp"),
        P("tp", rows),
        P(rows),
        P(rows),
        P(rows, "tp"),
        P("tp", rows),
        P(rows),
        P(rows),
        P(rows, None),
        P(None, "shard", "ctx", None),
    )
    return jax.shard_map(
        per_device,
        mesh=mesh,
        in_specs=placed,
        out_specs=(
            P(None, "shard", ("ctx", "tp"), None),
            P(None, "shard", "ctx", "tp"),
            P(rows, "tp"),
            P(rows, "tp"),
            P(rows, "tp"),
            P("tp", rows),
            P(rows),
            P(rows),
            P(rows, "tp"),
            P("tp", rows),
            P(rows),
            P(rows),
            P(rows, None),
        ),
        check_vma=False,
    )
```

time: 1210 us -> 474 us (0.39)
  waiting for transfers between devices: 602 us -> 137 us
  matrix products: 239 us -> 63.5 us
  blocking collectives: 148 us -> 0 us
  starting transfers between devices: 2.05 us -> 97.2 us
  other arithmetic: 103 us -> 63.1 us
  Pallas kernels: 0 us -> 37.2 us
  loops' own time: 17.1 us -> 0 us
  between operations: 18.9 us -> 2.89 us
    reduce_scatter x11 -> x0, waiting for transfers between devices: 258 us -> none  [the longest x2 50 us: per_device(): lax.psum_scatter(as_blocks(attn_partial), 'tp', scatter_dimension=1, tile...]
    all_gather x10 -> x0, waiting for transfers between devices: 193 us -> none  [the longest x2 78.1 us: per_device(): lax.all_gather(as_blocks(grad_h2.astype(jnp.bfloat16)), 'tp', axis=1, til...]
    dot_general x70 -> x21, matrix products: 239 us -> 63.5 us  [the longest x15 22 us: dot(): lax.dot_general(first_op, second_op, dims, preferred_element_type=jnp.flo...]
    unnamed x34 -> x0, waiting for transfers between devices: 146 us -> none
    ppermute x0 -> x65, waiting for transfers between devices: none -> 137 us  [the longest x58 133 us: swap(): return lax.ppermute(v, axis, [(i, i ^ bit) for i in range(count)])]
    ppermute x0 -> x65, starting transfers between devices: none -> 97.2 us  [the longest x58 74.7 us: swap(): return lax.ppermute(v, axis, [(i, i ^ bit) for i in range(count)])]
    all_gather x7 -> x0, blocking collectives: 96.2 us -> none  [the longest x1 18.7 us: fetch_weights(): lax.all_gather(value_weight, ('shard', 'ctx'), axis=0, tiled=True)]
    unnamed x2 -> x0, blocking collectives: 42.8 us -> none
  transfers between devices with their start and end apart: 28 -> 65, of which waited for: 19 -> 20; matrix products, arithmetic and copies ran while one was open for 31% -> 33% of each run, Pallas kernels for 0% -> 8%
where the time goes in v1:
time: 474 us; the launch traced here: 467 us
  waiting for transfers between devices  137 us (29%)
  starting transfers between devices  97.2 us (21%)
  local copies, waits for them, and re-layouts  65.7 us (14%)
  matrix products  63.5 us (13%)
  other arithmetic  63.1 us (13%)
  Pallas kernels  37.2 us (8%)
    ppermute x58, waiting for transfers between devices, swap(): return lax.ppermute(v, axis, [(i, i ^ bit) for i in range(count)])  133 us
    ppermute x58, starting transfers between devices, swap(): return lax.ppermute(v, axis, [(i, i ^ bit) for i in range(count)])  74.7 us
    ppermute x7, starting transfers between devices, route(): return lax.ppermute(v, ('shard', 'ctx', 'tp'), pairs)  22.5 us
    dot_general x15, matrix products, dot(): lax.dot_general(first_op, second_op, dims, preferred_element_type=jnp.flo...  22 us
    pallas_call x1, Pallas kernels, attn_backward(): pl.pallas_call(attn_bwd_kernel, grid_spec=pltpu.PrefetchScalarGridSpec(nu...  19.9 us
    dot_general x1, matrix products, per_device(): jnp.einsum('td,zdf->ztf', first_low, inner_full, preferred_element_type=f32)  18.3 us
    pallas_call x1, Pallas kernels, attn_forward(): pl.pallas_call(attn_fwd_kernel, grid_spec=pltpu.PrefetchScalarGridSpec(nu...  17.3 us
    unnamed x171, local copies, waits for them, and re-layouts  14.1 us
  transfers between devices with their start and end apart: 65, of which 20 were waited for; matrix products, arithmetic and copies ran while one was open for 33% of the time, Pallas kernels for 8%

profile of v1, /device:TPU:1, one launch (start us, length us, event | category | flops | bytes accessed | tf_op | source)
XLA Modules:
  0.0 466.9 jit_solution(14138311336430347079)
XLA Ops:
  32.0 3.9 select_select_fusion.16
  48.1 8.1 %collective-permute-done.6 = bf16[4,1,1,1,96,768]{5,4,3,2,1,0:T(8,128)(2,1)S(1)} collective-permute-done((bf16[4,1,1,1,96,768]{5,4,3,2,1,0:T(8,128)(2,1)S(1)}, bf16[4,1,1,1,96,768]{5,4,3,2,1,0:T(8,128)(2,1)S(1)}, u32[]{:S(2)}, u32[]{:S(2)}) %collective-permute-start.6) | collective-permute-done | bytes 589856 | tf_op jit(solution)/shard_map/ppermute | solution.py:50
  60.2 5.8 %collective-permute-start = (bf16[1024,768]{1,0:T(8,128)(2,1)}, bf16[1024,768]{1,0:T(8,128)(2,1)}, u32[]{:S(2)}, u32[]{:S(2)}) collective-permute-start(bf16[1024,768]{1,0:T(8,128)(2,1)} %dynamic-slice_bitcast_fusion), channel_id=1, source_target_pairs={{0,8},{8,0},{16,24},{24,16},{1,9},{9,1},{17,25},{25,17},{2,10},{10... | collective-permute-start | bytes 4718600 | tf_op jit(solution)/shard_map/ppermute | solution.py:50
  66.2 26.5 %collective-permute-done.18 = bf16[4,1,1,1,96,768]{5,4,3,2,1,0:T(8,128)(2,1)S(1)} collective-permute-done((bf16[4,1,1,1,96,768]{5,4,3,2,1,0:T(8,128)(2,1)S(1)}, bf16[4,1,1,1,96,768]{5,4,3,2,1,0:T(8,128)(2,1)S(1)}, u32[]{:S(2)}, u32[]{:S(2)}) %collective-permute-start.18) | collective-permute-done | bytes 589856 | tf_op jit(solution)/shard_map/ppermute | solution.py:50
  97.5 5.5 %collective-permute-done.24 = bf16[4,1,1,1,96,768]{5,4,3,2,1,0:T(8,128)(2,1)S(1)} collective-permute-done((bf16[4,1,1,1,96,768]{5,4,3,2,1,0:T(8,128)(2,1)S(1)}, bf16[4,1,1,1,96,768]{5,4,3,2,1,0:T(8,128)(2,1)S(1)}, u32[]{:S(2)}, u32[]{:S(2)}) %collective-permute-start.24) | collective-permute-done | bytes 589856 | tf_op jit(solution)/shard_map/ppermute | solution.py:50
  103.0 10.8 %collective-permute-start.8 = (bf16[4,2,1,2,96,768]{5,4,3,2,1,0:T(8,128)(2,1)}, bf16[4,2,1,2,96,768]{5,4,3,2,1,0:T(8,128)(2,1)}, u32[]{:S(2)}, u32[]{:S(2)}) collective-permute-start(bf16[4,2,1,2,96,768]{5,4,3,2,1,0:T(8,128)(2,1)} %pad_maximum_fusion.4), channel_id=1, source_target_pairs={{0,8},{8,0},{16,24},{24,16},{1,9},{9,1},{17,25},{25,17},{2,10},{10... | collective-permute-start | bytes 7077896 | tf_op jit(solution)/shard_map/ppermute | solution.py:50
  121.5 6.8 %collective-permute-done.19 = bf16[4,1,1,2,96,768]{5,4,3,2,1,0:T(8,128)(2,1)} collective-permute-done((bf16[4,1,1,2,96,768]{5,4,3,2,1,0:T(8,128)(2,1)}, bf16[4,1,1,2,96,768]{5,4,3,2,1,0:T(8,128)(2,1)}, u32[]{:S(2)}, u32[]{:S(2)}) %collective-permute-start.19) | collective-permute-done | bytes 1179680 | tf_op jit(solution)/shard_map/ppermute | solution.py:50
  131.9 5.7 %collective-permute-start.20 = (bf16[4,2,1,2,96,768]{5,4,3,2,1,0:T(8,128)(2,1)}, bf16[4,2,1,2,96,768]{5,4,3,2,1,0:T(8,128)(2,1)}, u32[]{:S(2)}, u32[]{:S(2)}) collective-permute-start(bf16[4,2,1,2,96,768]{5,4,3,2,1,0:T(8,128)(2,1)} %pad_maximum_fusion.5), channel_id=1, source_target_pairs={{0,8},{8,0},{16,24},{24,16},{1,9},{9,1},{17,25},{25,17},{2,10},{10... | collective-permute-start | bytes 7077896 | tf_op jit(solution)/shard_map/ppermute | solution.py:50
  137.5 5.7 %collective-permute-done.25 = bf16[4,2,1,1,96,768]{5,4,3,2,1,0:T(8,128)(2,1)} collective-permute-done((bf16[4,2,1,1,96,768]{5,4,3,2,1,0:T(8,128)(2,1)}, bf16[4,2,1,1,96,768]{5,4,3,2,1,0:T(8,128)(2,1)}, u32[]{:S(2)}, u32[]{:S(2)}) %collective-permute-start.25) | collective-permute-done | bytes 1179680 | tf_op jit(solution)/shard_map/ppermute | solution.py:50
  164.1 17.3 %attn_fwd.1 = (bf16[1024,384]{1,0:T(8,128)(2,1)S(1)}, f32[3,1,2048]{2,1,0:T(1,128)S(1)}) custom-call(s32[5,4]{1,0:T(8,128)S(1)} %stack.83.meta, bf16[1024,384]{1,0:T(8,128)(2,1)S(1)} %multiply_convert_fusion.q_ref, s32[2,1024]{1,0:T(2,128)S(1)} %pad_add_fusion.bounds, bf16[2048,384]{1,0:T(8,128)(2,1)S(1)} %convolution_convert_fusion.3.k_ref, ...), custom_call_target="tpu_custom_call" | custom-call | flops 1610612736 | bytes 8388608 | tf_op jit(solution)/shard_map/attn_fwd/pallas_call | solution.py:228
  183.5 3.3 concatenate.151
  186.9 3.7 broadcast_select_fusion.3
  194.6 18.3 %fusion.9 = (bf16[4,512,768]{1,2,0:T(8,128)(2,1)S(1)}, f32[4,512,768]{1,2,0:T(8,128)S(1)}, f32[4,768,512]{2,1,0:T(8,128)}) fusion(bf16[4,768,768]{2,1,0:T(8,128)(2,1)S(1)} %bitcast.242, f32[512,768]{1,0:T(8,128)S(1)} %get-tuple-element.246, f32[768]{0:T(1024)S(1)} %copy-done.70, f32[768]{0:T(1024)S(1)} %copy-done.64, f32[512]{0:T(512)S(1)} %add_rsqrt_fusion.2, ...), kind=kOutput, calls=%fused_computation.26 | convolution fusion | flops 2520121344 | bytes 22030336 | tf_op jit(solution)/shard_map/td,zdf->ztf/dot_general | solution.py:421
  222.0 4.3 convolution_convert_fusion
  226.4 6.8 %fusion.6 = bf16[4,512,768]{1,2,0:T(8,128)(2,1)S(1)} fusion(f32[4,512,768]{1,2,0:T(8,128)S(1)} %get-tuple-element.113, f32[4,768,512]{2,1,0:T(8,128)} %get-tuple-element.247, bf16[4,768,768]{2,1,0:T(8,128)(2,1)S(1)} %bitcast.245, f32[512,768]{1,0:T(8,128)S(1)} %subtract_multiply_fusion.1), kind=kOutput, calls=%fused_computation.18 | convolution fusion | flops 2438332416 | bytes 22020096 | tf_op jit(solution)/shard_map/td,zdf->ztf/dot_general | solution.py:440
  233.2 4.3 multiply_reduce_fusion.1
  237.5 4.7 %convolution_convert_fusion.1 = bf16[4,768,768]{1,2,0:T(8,128)(2,1)} fusion(bf16[4,512,768]{1,2,0:T(8,128)(2,1)S(1)} %fusion.6, f32[512,768]{1,0:T(8,128)S(1)} %get-tuple-element.246, f32[768]{0:T(1024)S(1)} %copy-done.70, f32[768]{0:T(1024)S(1)} %copy-done.64, f32[512]{0:T(512)S(1)} %add_rsqrt_fusion.2, f32[512]{0:T(512)S(1)} %broadcast_multiply_fusion.6), kind=kOutput, calls=%fused_computation.53 | convolution fusion | flops 2420244480 | bytes 9447424 | tf_op jit(solution)/shard_map/td,ztf->zdf/dot_general | solution.py:443
  243.0 11.5 %collective-permute-start.31 = (f32[256,128]{0,1:T(8,128)}, f32[256,128]{0,1:T(8,128)S(1)}, u32[]{:S(2)}, u32[]{:S(2)}) collective-permute-start(f32[256,128]{0,1:T(8,128)} %get-tuple-element.227), channel_id=1, source_target_pairs={{0,1},{1,9},{2,0},{3,8},{4,5},{5,13},{6,4},{7,12},{8,3},{9,11},{10... | collective-permute-start | bytes 393224 | tf_op jit(solution)/shard_map/ppermute | solution.py:66
  263.9 3.5 fusion.64
  269.9 3.3 constant_dynamic-slice_fusion.5
  296.4 19.9 %attn_bwd.1 = (bf16[1024,384]{1,0:T(8,128)(2,1)S(1)}, bf16[2048,384]{1,0:T(8,128)(2,1)S(1)}, bf16[2048,384]{1,0:T(8,128)(2,1)S(1)}) custom-call(s32[5,4]{1,0:T(8,128)S(1)} %stack.83.meta, bf16[1024,384]{1,0:T(8,128)(2,1)S(1)} %multiply_convert_fusion.q_ref, bf16[1024,384]{1,0:T(8,128)(2,1)S(1)} %copy-done.3, s32[2,1024]{1,0:T(2,128)S(1)} %pad_add_fusion.bounds, ...), custom_call_target="tpu_custom_call" | custom-call | flops 4026531840 | bytes 12582912 | tf_op jit(solution)/shard_map/attn_bwd/pallas_call | solution.py:267
  331.3 3.4 fusion.51
  342.7 5.5 %collective-permute-start.36 = (bf16[512,768]{1,0:T(8,128)(2,1)S(1)}, bf16[512,768]{1,0:T(8,128)(2,1)S(1)}, u32[]{:S(2)}, u32[]{:S(2)}) collective-permute-start(bf16[512,768]{1,0:T(8,128)(2,1)S(1)} %add_convert_fusion.7), channel_id=1, source_target_pairs={{0,4},{4,0},{1,5},{5,1},{2,6},{6,2},{3,7},{7,3},{8,12},{12,8},{9,1... | collective-permute-start | bytes 2359304 | tf_op jit(solution)/shard_map/ppermute | solution.py:50
  354.9 11.3 %collective-permute-done.36 = bf16[512,768]{1,0:T(8,128)(2,1)S(1)} collective-permute-done((bf16[512,768]{1,0:T(8,128)(2,1)S(1)}, bf16[512,768]{1,0:T(8,128)(2,1)S(1)}, u32[]{:S(2)}, u32[]{:S(2)}) %collective-permute-start.36) | collective-permute-done | bytes 786464 | tf_op jit(solution)/shard_map/ppermute | solution.py:50
  373.6 17.7 %collective-permute-done.60 = bf16[4,2,1,1,96,768]{5,4,3,2,1,0:T(8,128)(2,1)S(1)} collective-permute-done((bf16[4,2,1,1,96,768]{5,4,3,2,1,0:T(8,128)(2,1)S(1)}, bf16[4,2,1,1,96,768]{5,4,3,2,1,0:T(8,128)(2,1)S(1)}, u32[]{:S(2)}, u32[]{:S(2)}) %collective-permute-start.60) | collective-permute-done | bytes 1179680 | tf_op jit(solution)/shard_map/ppermute | solution.py:50
  395.8 4.4 collective-permute-done.39
  406.3 4.8 %collective-permute-done.61 = bf16[4,1,1,1,96,768]{5,4,3,2,1,0:T(8,128)(2,1)} collective-permute-done((bf16[4,1,1,1,96,768]{5,4,3,2,1,0:T(8,128)(2,1)}, bf16[4,1,1,1,96,768]{5,4,3,2,1,0:T(8,128)(2,1)}, u32[]{:S(2)}, u32[]{:S(2)}) %collective-permute-start.61) | collective-permute-done | bytes 589856 | tf_op jit(solution)/shard_map/ppermute | solution.py:50
  415.1 8.7 %collective-permute-done.42 = bf16[4,2,1,1,96,768]{5,4,3,2,1,0:T(8,128)(2,1)} collective-permute-done((bf16[4,2,1,1,96,768]{5,4,3,2,1,0:T(8,128)(2,1)}, bf16[4,2,1,1,96,768]{5,4,3,2,1,0:T(8,128)(2,1)}, u32[]{:S(2)}, u32[]{:S(2)}) %collective-permute-start.42) | collective-permute-done | bytes 1179680 | tf_op jit(solution)/shard_map/ppermute | solution.py:50
  425.5 9.0 %collective-permute-done.55 = bf16[4,1,1,1,96,768]{5,4,3,2,1,0:T(8,128)(2,1)S(1)} collective-permute-done((bf16[4,1,1,1,96,768]{5,4,3,2,1,0:T(8,128)(2,1)S(1)}, bf16[4,1,1,1,96,768]{5,4,3,2,1,0:T(8,128)(2,1)S(1)}, u32[]{:S(2)}, u32[]{:S(2)}) %collective-permute-start.55) | collective-permute-done | bytes 589856 | tf_op jit(solution)/shard_map/ppermute | solution.py:50
  439.7 4.0 collective-permute-done.56
  443.7 13.6 %collective-permute-done.57 = bf16[1,1,1,1,96,768]{5,4,3,2,1,0:T(8,128)(2,1)S(1)} collective-permute-done((bf16[1,1,1,1,96,768]{5,4,3,2,1,0:T(8,128)(2,1)S(1)}, bf16[1,1,1,1,96,768]{5,4,3,2,1,0:T(8,128)(2,1)S(1)}, u32[]{:S(2)}, u32[]{:S(2)}) %collective-permute-start.57) | collective-permute-done | bytes 147488 | tf_op jit(solution)/shard_map/ppermute | solution.py:50
  458.1 5.4 %collective-permute-done.45 = bf16[1,1,1,1,96,768]{5,4,3,2,1,0:T(8,128)(2,1)S(1)} collective-permute-done((bf16[1,1,1,1,96,768]{5,4,3,2,1,0:T(8,128)(2,1)S(1)}, bf16[1,1,1,1,96,768]{5,4,3,2,1,0:T(8,128)(2,1)S(1)}, u32[]{:S(2)}, u32[]{:S(2)}) %collective-permute-start.45) | collective-permute-done | bytes 147488 | tf_op jit(solution)/shard_map/ppermute | solution.py:50
  (461 shorter events, 196.7 us)
Async XLA Ops:
  6.1 34.3 %collective-permute-start.4 = (bf16[1,1,1,1,96,768]{5,4,3,2,1,0:T(8,128)(2,1)S(1)}, bf16[1,1,1,1,96,768]{5,4,3,2,1,0:T(8,128)(2,1)S(1)}, u32[]{:S(2)}, u32[]{:S(2)}) collective-permute-start(bf16[1,1,1,1,96,768]{5,4,3,2,1,0:T(8,128)(2,1)S(1)} %bitcast.258), channel_id=1, source_target_pairs={{0,2},{1,3},{2,0},{3,1},{4,6},{5,7},{6,4},{7,5},{8,10},{9,11},{10,... | collective-permute-start | bytes 442376 | tf_op jit(solution)/shard_map/ppermute | solution.py:50
  9.3 31.1 %collective-permute-start.5 = (bf16[1,1,1,1,96,768]{5,4,3,2,1,0:T(8,128)(2,1)S(1)}, bf16[1,1,1,1,96,768]{5,4,3,2,1,0:T(8,128)(2,1)S(1)}, u32[]{:S(2)}, u32[]{:S(2)}) collective-permute-start(bf16[1,1,1,1,96,768]{5,4,3,2,1,0:T(8,128)(2,1)S(1)} %bitcast.259), channel_id=1, source_target_pairs={{0,3},{1,2},{2,1},{3,0},{4,7},{5,6},{6,5},{7,4},{8,11},{9,10},{10,... | collective-permute-start | bytes 442376 | tf_op jit(solution)/shard_map/ppermute | solution.py:50
  10.4 30.4 %collective-permute-start.3 = (bf16[1,1,1,1,96,768]{5,4,3,2,1,0:T(8,128)(2,1)S(1)}, bf16[1,1,1,1,96,768]{5,4,3,2,1,0:T(8,128)(2,1)S(1)}, u32[]{:S(2)}, u32[]{:S(2)}) collective-permute-start(bf16[1,1,1,1,96,768]{5,4,3,2,1,0:T(8,128)(2,1)S(1)} %bitcast.260), channel_id=1, source_target_pairs={{0,1},{1,0},{2,3},{3,2},{4,5},{5,4},{6,7},{7,6},{8,9},{9,8},{10,11... | collective-permute-start | bytes 442376 | tf_op jit(solution)/shard_map/ppermute | solution.py:50
  22.7 22.0 %collective-permute-start.16 = (bf16[1,1,1,1,96,768]{5,4,3,2,1,0:T(8,128)(2,1)S(1)}, bf16[1,1,1,1,96,768]{5,4,3,2,1,0:T(8,128)(2,1)S(1)}, u32[]{:S(2)}, u32[]{:S(2)}) collective-permute-start(bf16[1,1,1,1,96,768]{5,4,3,2,1,0:T(8,128)(2,1)S(1)} %bitcast.263), channel_id=1, source_target_pairs={{0,2},{1,3},{2,0},{3,1},{4,6},{5,7},{6,4},{7,5},{8,10},{9,11},{10,... | collective-permute-start | bytes 442376 | tf_op jit(solution)/shard_map/ppermute | solution.py:50
  56.4 38.0 %collective-permute-start.7 = (bf16[4,2,1,1,96,768]{5,4,3,2,1,0:T(8,128)(2,1)S(1)}, bf16[4,2,1,1,96,768]{5,4,3,2,1,0:T(8,128)(2,1)S(1)}, u32[]{:S(2)}, u32[]{:S(2)}) collective-permute-start(bf16[4,2,1,1,96,768]{5,4,3,2,1,0:T(8,128)(2,1)S(1)} %pad_maximum_fusion.9), channel_id=1, source_target_pairs={{0,4},{4,0},{1,5},{5,1},{2,6},{6,2},{3,7},{7,3},{8,12},{12,8},{9,1... | collective-permute-start | bytes 3538952 | tf_op jit(solution)/shard_map/ppermute | solution.py:50
  57.8 35.0 %collective-permute-start.18 = (bf16[4,1,1,1,96,768]{5,4,3,2,1,0:T(8,128)(2,1)S(1)}, bf16[4,1,1,1,96,768]{5,4,3,2,1,0:T(8,128)(2,1)S(1)}, u32[]{:S(2)}, u32[]{:S(2)}) collective-permute-start(bf16[4,1,1,1,96,768]{5,4,3,2,1,0:T(8,128)(2,1)S(1)} %pad_maximum_fusion.19), channel_id=1, source_target_pairs={{0,4},{4,0},{1,5},{5,1},{2,6},{6,2},{3,7},{7,3},{8,12},{12,8},{9,1... | collective-permute-start | bytes 1769480 | tf_op jit(solution)/shard_map/ppermute | solution.py:50
  58.5 60.4 %collective-permute-start.9 = (bf16[800,768]{1,0:T(8,128)(2,1)}, bf16[800,768]{1,0:T(8,128)(2,1)}, u32[]{:S(2)}, u32[]{:S(2)}) collective-permute-start(bf16[800,768]{1,0:T(8,128)(2,1)} %dynamic-slice_bitcast_fusion.1), channel_id=1, source_target_pairs={{0,4},{2,6},{4,0},{6,2},{9,13},{11,15},{13,9},{15,11},{16,20},{18,... | collective-permute-start | bytes 3686408 | tf_op jit(solution)/shard_map/ppermute | solution.py:66
  60.2 59.0 %collective-permute-start = (bf16[1024,768]{1,0:T(8,128)(2,1)}, bf16[1024,768]{1,0:T(8,128)(2,1)}, u32[]{:S(2)}, u32[]{:S(2)}) collective-permute-start(bf16[1024,768]{1,0:T(8,128)(2,1)} %dynamic-slice_bitcast_fusion), channel_id=1, source_target_pairs={{0,8},{8,0},{16,24},{24,16},{1,9},{9,1},{17,25},{25,17},{2,10},{10... | collective-permute-start | bytes 4718600 | tf_op jit(solution)/shard_map/ppermute | solution.py:50
  66.0 49.3 %collective-permute-start.29 = (bf16[1,2,1,2,96,128]{5,4,3,2,1,0:T(8,128)(2,1)S(1)}, bf16[1,2,1,2,96,128]{5,4,3,2,1,0:T(8,128)(2,1)S(1)}, u32[]{:S(2)}, u32[]{:S(2)}) collective-permute-start(bf16[1,2,1,2,96,128]{5,4,3,2,1,0:T(8,128)(2,1)S(1)} %pad_maximum_fusion.22), channel_id=1, source_target_pairs={{0,8},{8,0},{16,24},{24,16},{1,9},{9,1},{17,25},{25,17},{2,10},{10... | collective-permute-start | bytes 294920 | tf_op jit(solution)/shard_map/ppermute | solution.py:50
  94.5 33.8 %collective-permute-start.19 = (bf16[4,1,1,2,96,768]{5,4,3,2,1,0:T(8,128)(2,1)}, bf16[4,1,1,2,96,768]{5,4,3,2,1,0:T(8,128)(2,1)}, u32[]{:S(2)}, u32[]{:S(2)}) collective-permute-start(bf16[4,1,1,2,96,768]{5,4,3,2,1,0:T(8,128)(2,1)} %pad_maximum_fusion.10), channel_id=1, source_target_pairs={{0,16},{8,24},{16,0},{24,8},{1,17},{9,25},{17,1},{25,9},{2,18},{10... | collective-permute-start | bytes 3538952 | tf_op jit(solution)/shard_map/ppermute | solution.py:50
  103.0 45.3 %collective-permute-start.8 = (bf16[4,2,1,2,96,768]{5,4,3,2,1,0:T(8,128)(2,1)}, bf16[4,2,1,2,96,768]{5,4,3,2,1,0:T(8,128)(2,1)}, u32[]{:S(2)}, u32[]{:S(2)}) collective-permute-start(bf16[4,2,1,2,96,768]{5,4,3,2,1,0:T(8,128)(2,1)} %pad_maximum_fusion.4), channel_id=1, source_target_pairs={{0,8},{8,0},{16,24},{24,16},{1,9},{9,1},{17,25},{25,17},{2,10},{10... | collective-permute-start | bytes 7077896 | tf_op jit(solution)/shard_map/ppermute | solution.py:50
  115.3 27.9 %collective-permute-start.25 = (bf16[4,2,1,1,96,768]{5,4,3,2,1,0:T(8,128)(2,1)}, bf16[4,2,1,1,96,768]{5,4,3,2,1,0:T(8,128)(2,1)}, u32[]{:S(2)}, u32[]{:S(2)}) collective-permute-start(bf16[4,2,1,1,96,768]{5,4,3,2,1,0:T(8,128)(2,1)} %pad_maximum_fusion.11), channel_id=1, source_target_pairs={{0,4},{4,0},{1,5},{5,1},{2,6},{6,2},{3,7},{7,3},{8,12},{12,8},{9,1... | collective-permute-start | bytes 3538952 | tf_op jit(solution)/shard_map/ppermute | solution.py:50
  118.9 98.6 %collective-permute-start.32 = (bf16[512,128]{0,1:T(8,128)(2,1)}, bf16[512,128]{0,1:T(8,128)(2,1)}, u32[]{:S(2)}, u32[]{:S(2)}) collective-permute-start(bf16[512,128]{0,1:T(8,128)(2,1)} %bitcast.269), channel_id=1, source_target_pairs={{0,8},{8,0},{16,24},{24,16},{1,9},{9,1},{17,25},{25,17},{2,10},{10... | collective-permute-start | bytes 393224 | tf_op jit(solution)/shard_map/ppermute | solution.py:50
  119.2 28.5 %collective-permute-start.10 = (bf16[800,768]{1,0:T(8,128)(2,1)}, bf16[800,768]{1,0:T(8,128)(2,1)S(1)}, u32[]{:S(2)}, u32[]{:S(2)}) collective-permute-start(bf16[800,768]{1,0:T(8,128)(2,1)} %collective-permute-done.9), channel_id=1, source_target_pairs={{0,8},{8,0},{16,24},{24,16},{1,9},{9,1},{17,25},{25,17},{2,10},{10... | collective-permute-start | bytes 3686408 | tf_op jit(solution)/shard_map/ppermute | solution.py:50
  131.9 54.9 %collective-permute-start.20 = (bf16[4,2,1,2,96,768]{5,4,3,2,1,0:T(8,128)(2,1)}, bf16[4,2,1,2,96,768]{5,4,3,2,1,0:T(8,128)(2,1)}, u32[]{:S(2)}, u32[]{:S(2)}) collective-permute-start(bf16[4,2,1,2,96,768]{5,4,3,2,1,0:T(8,128)(2,1)} %pad_maximum_fusion.5), channel_id=1, source_target_pairs={{0,8},{8,0},{16,24},{24,16},{1,9},{9,1},{17,25},{25,17},{2,10},{10... | collective-permute-start | bytes 7077896 | tf_op jit(solution)/shard_map/ppermute | solution.py:50
  146.9 39.9 %collective-permute-start.26 = (bf16[4,2,1,2,96,768]{5,4,3,2,1,0:T(8,128)(2,1)}, bf16[4,2,1,2,96,768]{5,4,3,2,1,0:T(8,128)(2,1)}, u32[]{:S(2)}, u32[]{:S(2)}) collective-permute-start(bf16[4,2,1,2,96,768]{5,4,3,2,1,0:T(8,128)(2,1)} %pad_maximum_fusion.6), channel_id=1, source_target_pairs={{0,8},{8,0},{16,24},{24,16},{1,9},{9,1},{17,25},{25,17},{2,10},{10... | collective-permute-start | bytes 7077896 | tf_op jit(solution)/shard_map/ppermute | solution.py:50
  243.0 31.1 %collective-permute-start.31 = (f32[256,128]{0,1:T(8,128)}, f32[256,128]{0,1:T(8,128)S(1)}, u32[]{:S(2)}, u32[]{:S(2)}) collective-permute-start(f32[256,128]{0,1:T(8,128)} %get-tuple-element.227), channel_id=1, source_target_pairs={{0,1},{1,9},{2,0},{3,8},{4,5},{5,13},{6,4},{7,12},{8,3},{9,11},{10... | collective-permute-start | bytes 393224 | tf_op jit(solution)/shard_map/ppermute | solution.py:66
  273.2 75.0 %collective-permute-start.59 = (bf16[4,2,1,2,96,768]{5,4,3,2,1,0:T(8,128)(2,1)}, bf16[4,2,1,2,96,768]{5,4,3,2,1,0:T(8,128)(2,1)}, u32[]{:S(2)}, u32[]{:S(2)}) collective-permute-start(bf16[4,2,1,2,96,768]{5,4,3,2,1,0:T(8,128)(2,1)} %constant_dynamic-slice_fusion.5), channel_id=1, source_target_pairs={{0,8},{8,0},{16,24},{24,16},{1,9},{9,1},{17,25},{25,17},{2,10},{10... | collective-permute-start | bytes 7077896 | tf_op jit(solution)/shard_map/ppermute | solution.py:50
  282.0 69.1 %collective-permute-start.53 = (bf16[4,2,1,2,96,768]{5,4,3,2,1,0:T(8,128)(2,1)}, bf16[4,2,1,2,96,768]{5,4,3,2,1,0:T(8,128)(2,1)}, u32[]{:S(2)}, u32[]{:S(2)}) collective-permute-start(bf16[4,2,1,2,96,768]{5,4,3,2,1,0:T(8,128)(2,1)} %constant_dynamic-slice_fusion.11), channel_id=1, source_target_pairs={{0,8},{8,0},{16,24},{24,16},{1,9},{9,1},{17,25},{25,17},{2,10},{10... | collective-permute-start | bytes 7077896 | tf_op jit(solution)/shard_map/ppermute | solution.py:50
  339.0 30.8 %collective-permute-start.41 = (bf16[4,2,1,2,96,768]{5,4,3,2,1,0:T(8,128)(2,1)S(1)}, bf16[4,2,1,2,96,768]{5,4,3,2,1,0:T(8,128)(2,1)S(1)}, u32[]{:S(2)}, u32[]{:S(2)}) collective-permute-start(bf16[4,2,1,2,96,768]{5,4,3,2,1,0:T(8,128)(2,1)S(1)} %fusion.22), channel_id=1, source_target_pairs={{0,8},{8,0},{16,24},{24,16},{1,9},{9,1},{17,25},{25,17},{2,10},{10... | collective-permute-start | bytes 7077896 | tf_op jit(solution)/shard_map/ppermute | solution.py:50
  342.7 23.5 %collective-permute-start.36 = (bf16[512,768]{1,0:T(8,128)(2,1)S(1)}, bf16[512,768]{1,0:T(8,128)(2,1)S(1)}, u32[]{:S(2)}, u32[]{:S(2)}) collective-permute-start(bf16[512,768]{1,0:T(8,128)(2,1)S(1)} %add_convert_fusion.7), channel_id=1, source_target_pairs={{0,4},{4,0},{1,5},{5,1},{2,6},{6,2},{3,7},{7,3},{8,12},{12,8},{9,1... | collective-permute-start | bytes 2359304 | tf_op jit(solution)/shard_map/ppermute | solution.py:50
  350.8 40.6 %collective-permute-start.60 = (bf16[4,2,1,1,96,768]{5,4,3,2,1,0:T(8,128)(2,1)S(1)}, bf16[4,2,1,1,96,768]{5,4,3,2,1,0:T(8,128)(2,1)S(1)}, u32[]{:S(2)}, u32[]{:S(2)}) collective-permute-start(bf16[4,2,1,1,96,768]{5,4,3,2,1,0:T(8,128)(2,1)S(1)} %constant_dynamic-slice_fusion.4), channel_id=1, source_target_pairs={{0,4},{4,0},{1,5},{5,1},{2,6},{6,2},{3,7},{7,3},{8,12},{12,8},{9,1... | collective-permute-start | bytes 3538952 | tf_op jit(solution)/shard_map/ppermute | solution.py:50
  354.8 49.4 %collective-permute-start.54 = (bf16[4,1,1,2,96,768]{5,4,3,2,1,0:T(8,128)(2,1)}, bf16[4,1,1,2,96,768]{5,4,3,2,1,0:T(8,128)(2,1)}, u32[]{:S(2)}, u32[]{:S(2)}) collective-permute-start(bf16[4,1,1,2,96,768]{5,4,3,2,1,0:T(8,128)(2,1)} %constant_dynamic-slice_fusion.10), channel_id=1, source_target_pairs={{0,16},{8,24},{16,0},{24,8},{1,17},{9,25},{17,1},{25,9},{2,18},{10... | collective-permute-start | bytes 3538952 | tf_op jit(solution)/shard_map/ppermute | solution.py:50
  366.9 28.6 %collective-permute-start.38 = (bf16[512,192]{1,0:T(8,128)(2,1)S(1)}, bf16[512,192]{1,0:T(8,128)(2,1)S(1)}, u32[]{:S(2)}, u32[]{:S(2)}) collective-permute-start(bf16[512,192]{1,0:T(8,128)(2,1)S(1)} %get-tuple-element.174), channel_id=1, source_target_pairs={{0,1},{1,9},{2,3},{3,11},{4,5},{5,13},{6,7},{7,15},{8,0},{9,8},{10... | collective-permute-start | bytes 589832 | tf_op jit(solution)/shard_map/ppermute | solution.py:66
  367.7 28.1 %collective-permute-start.37 = (bf16[512,192]{1,0:T(8,128)(2,1)S(1)}, bf16[512,192]{1,0:T(8,128)(2,1)S(1)}, u32[]{:S(2)}, u32[]{:S(2)}) collective-permute-start(bf16[512,192]{1,0:T(8,128)(2,1)S(1)} %get-tuple-element.175), channel_id=1, source_target_pairs={{0,0},{1,8},{2,2},{3,10},{4,4},{5,12},{6,6},{7,14},{8,1},{9,9},{10... | collective-permute-start | bytes 589832 | tf_op jit(solution)/shard_map/ppermute | solution.py:66
  369.8 26.0 %collective-permute-start.40 = (bf16[512,192]{1,0:T(8,128)(2,1)S(1)}, bf16[512,192]{1,0:T(8,128)(2,1)S(1)}, u32[]{:S(2)}, u32[]{:S(2)}) collective-permute-start(bf16[512,192]{1,0:T(8,128)(2,1)S(1)} %get-tuple-element.176), channel_id=1, source_target_pairs={{0,3},{1,11},{2,1},{3,9},{4,7},{5,15},{6,5},{7,13},{8,2},{9,10},{1... | collective-permute-start | bytes 589832 | tf_op jit(solution)/shard_map/ppermute | solution.py:66
  395.5 28.3 %collective-permute-start.42 = (bf16[4,2,1,1,96,768]{5,4,3,2,1,0:T(8,128)(2,1)}, bf16[4,2,1,1,96,768]{5,4,3,2,1,0:T(8,128)(2,1)}, u32[]{:S(2)}, u32[]{:S(2)}) collective-permute-start(bf16[4,2,1,1,96,768]{5,4,3,2,1,0:T(8,128)(2,1)} %constant_dynamic-slice_fusion.19), channel_id=1, source_target_pairs={{0,4},{4,0},{1,5},{5,1},{2,6},{6,2},{3,7},{7,3},{8,12},{12,8},{9,1... | collective-permute-start | bytes 3538952 | tf_op jit(solution)/shard_map/ppermute | solution.py:50
  405.9 28.6 %collective-permute-start.55 = (bf16[4,1,1,1,96,768]{5,4,3,2,1,0:T(8,128)(2,1)S(1)}, bf16[4,1,1,1,96,768]{5,4,3,2,1,0:T(8,128)(2,1)S(1)}, u32[]{:S(2)}, u32[]{:S(2)}) collective-permute-start(bf16[4,1,1,1,96,768]{5,4,3,2,1,0:T(8,128)(2,1)S(1)} %constant_dynamic-slice_fusion.9), channel_id=1, source_target_pairs={{0,4},{4,0},{1,5},{5,1},{2,6},{6,2},{3,7},{7,3},{8,12},{12,8},{9,1... | collective-permute-start | bytes 1769480 | tf_op jit(solution)/shard_map/ppermute | solution.py:50
  412.4 22.4 %collective-permute-start.62 = (bf16[1,1,1,1,96,768]{5,4,3,2,1,0:T(8,128)(2,1)S(1)}, bf16[1,1,1,1,96,768]{5,4,3,2,1,0:T(8,128)(2,1)S(1)}, u32[]{:S(2)}, u32[]{:S(2)}) collective-permute-start(bf16[1,1,1,1,96,768]{5,4,3,2,1,0:T(8,128)(2,1)S(1)} %get-tuple-element.178), channel_id=1, source_target_pairs={{0,1},{1,0},{2,3},{3,2},{4,5},{5,4},{6,7},{7,6},{8,9},{9,8},{10,11... | collective-permute-start | bytes 442376 | tf_op jit(solution)/shard_map/ppermute | solution.py:50
  412.4 22.4 %collective-permute-start.64 = (bf16[1,1,1,1,96,768]{5,4,3,2,1,0:T(8,128)(2,1)S(1)}, bf16[1,1,1,1,96,768]{5,4,3,2,1,0:T(8,128)(2,1)S(1)}, u32[]{:S(2)}, u32[]{:S(2)}) collective-permute-start(bf16[1,1,1,1,96,768]{5,4,3,2,1,0:T(8,128)(2,1)S(1)} %get-tuple-element.179), channel_id=1, source_target_pairs={{0,3},{1,2},{2,1},{3,0},{4,7},{5,6},{6,5},{7,4},{8,11},{9,10},{10,... | collective-permute-start | bytes 442376 | tf_op jit(solution)/shard_map/ppermute | solution.py:50
  413.4 24.1 %collective-permute-start.63 = (bf16[1,1,1,1,96,768]{5,4,3,2,1,0:T(8,128)(2,1)S(1)}, bf16[1,1,1,1,96,768]{5,4,3,2,1,0:T(8,128)(2,1)S(1)}, u32[]{:S(2)}, u32[]{:S(2)}) collective-permute-start(bf16[1,1,1,1,96,768]{5,4,3,2,1,0:T(8,128)(2,1)S(1)} %get-tuple-element.180), channel_id=1, source_target_pairs={{0,2},{1,3},{2,0},{3,1},{4,6},{5,7},{6,4},{7,5},{8,10},{9,11},{10,... | collective-permute-start | bytes 442376 | tf_op jit(solution)/shard_map/ppermute | solution.py:50
  434.9 22.4 %collective-permute-start.57 = (bf16[1,1,1,1,96,768]{5,4,3,2,1,0:T(8,128)(2,1)S(1)}, bf16[1,1,1,1,96,768]{5,4,3,2,1,0:T(8,128)(2,1)S(1)}, u32[]{:S(2)}, u32[]{:S(2)}) collective-permute-start(bf16[1,1,1,1,96,768]{5,4,3,2,1,0:T(8,128)(2,1)S(1)} %get-tuple-element.183), channel_id=1, source_target_pairs={{0,2},{1,3},{2,0},{3,1},{4,6},{5,7},{6,4},{7,5},{8,10},{9,11},{10,... | collective-permute-start | bytes 442376 | tf_op jit(solution)/shard_map/ppermute | solution.py:50
  (113 other events, 877.0 us)

commit v2 on v1

v2 whole, which is shorter than its diff:
```python
import functools

import jax
import jax.numpy as jnp
from jax import lax
from jax.experimental import pallas as pl
from jax.experimental.pallas import tpu as pltpu
from jax.sharding import PartitionSpec as P

DH = 64
SEG_COUNT = 6
SEG_MOST = 800
BQ = 256
BK = 256
VMEM_MIB = 48

eps_norm = 1e-12
eps_unit = 1e-06
mask_fill = -1e30

NN = (((1,), (0,)), ((), ()))
NT = (((1,), (1,)), ((), ()))
TN = (((0,), (0,)), ((), ()))


def dot(first_op, second_op, dims=NN):
    return lax.dot_general(first_op, second_op, dims, preferred_element_type=jnp.float32)


def tie(*values):
    return lax.optimization_barrier(values)


def after(value, *others):
    return lax.optimization_barrier((value, *others))[0]


def after_all(done, *values):
    return lax.optimization_barrier((done, *values))[1:]


def swap(v, axis, bit):
    count = lax.axis_size(axis)
    return lax.ppermute(v, axis, [(i, i ^ bit) for i in range(count)])


def route(v, target):
    shards, halves, groups = (lax.axis_size(a) for a in ("shard", "ctx", "tp"))

    def flat(s, c, t):
        return (s * halves + c) * groups + t

    pairs = []
    for s in range(shards):
        for c in range(halves):
            for t in range(groups):
                to = target(s, c, t)
                if to is not None:
                    pairs.append((flat(s, c, t), flat(*to)))
    return lax.ppermute(v, ("shard", "ctx", "tp"), pairs)


def shard_bits():
    return lax.axis_size("shard").bit_length() - 1


def steps_of(name):
    bits = shard_bits()
    if name == "x":
        return [("ctx", 1, bits)]
    return [("shard", 1 << i, bits - 1 - i) for i in range(1, bits)]


def my_bit(axis, bit):
    return (lax.axis_index(axis) // bit) % 2


def gather_tp_start(own):
    return [
        route(
            own,
            lambda s, c, t, d=d: (s - s % 2 + t // 2, c, (2 * (s % 2) + t % 2) ^ d),
        )
        for d in range(4)
    ]


def gather_tp_finish(parts):
    t = lax.axis_index("tp")
    dim = shard_bits() - 1
    shape = (1,) * dim + (1, 1) + parts[0].shape
    return [
        jnp.concatenate(
            [lax.select_n(t ^ (2 * j + s), *parts).reshape(shape) for j in range(2)], axis=dim
        )
        for s in range(2)
    ]


def join(cur, other, axis, bit, dim):
    first = my_bit(axis, bit) == 0
    return jnp.concatenate([jnp.where(first, cur, other), jnp.where(first, other, cur)], axis=dim)


def gather_start(cur, name):
    axis, bit, _ = steps_of(name)[0]
    return swap(cur, axis, bit)


def gather_finish(cur, other, name):
    first, *rest = steps_of(name)
    cur = join(cur, other, *first)
    for axis, bit, dim in rest:
        cur = join(cur, swap(cur, axis, bit), axis, bit, dim)
    return cur


def flat_rows(cur):
    return cur.reshape(-1, cur.shape[-1])


def split_rows(full):
    rows = full.shape[-2] // (lax.axis_size("shard") * lax.axis_size("ctx"))
    return full.reshape(full.shape[:-2] + (2,) * (shard_bits() + 1) + (rows, full.shape[-1]))


def scatter_start(cur, name):
    axis, bit, dim = steps_of(name)[0]
    return swap(lax.dynamic_slice_in_dim(cur, 1 - my_bit(axis, bit), 1, dim), axis, bit)


def scatter_finish(cur, other, name):
    first, *rest = steps_of(name)
    kept = lax.dynamic_slice_in_dim(cur, my_bit(*first[:2]), 1, first[2])
    cur = (kept.astype(jnp.float32) + other.astype(jnp.float32)).astype(jnp.bfloat16)
    for axis, bit, dim in rest:
        mine = my_bit(axis, bit)
        other = swap(lax.dynamic_slice_in_dim(cur, 1 - mine, 1, dim), axis, bit)
        kept = lax.dynamic_slice_in_dim(cur, mine, 1, dim)
        cur = (kept.astype(jnp.float32) + other.astype(jnp.float32)).astype(jnp.bfloat16)
    return cur


def scatter_tp_start(first, second):
    z = lax.axis_index("tp")
    blocks = [lax.index_in_dim(s, j, s.ndim - 4, False) for j in range(2) for s in (first, second)]
    return [
        route(
            lax.select_n(z ^ d, *blocks),
            lambda s, c, t, d=d: (s - s % 2 + ((t ^ d) >> 1), c, 2 * (s % 2) + ((t ^ d) & 1)),
        )
        for d in range(4)
    ]


def sum_all(parts):
    total = parts[0].astype(jnp.float32)
    for part in parts[1:]:
        total = total + part.astype(jnp.float32)
    return total


def two_heads(pair):
    lane = lax.broadcasted_iota(jnp.int32, pair.shape, 1)
    zero = jnp.zeros_like(pair)
    return jnp.concatenate(
        [jnp.where(lane < DH, pair, zero), jnp.where(lane < DH, zero, pair)], axis=0
    )


def fold_heads(wide):
    rows = wide.shape[1] // 2
    both = jnp.concatenate([wide[:DH, :rows], wide[DH:, rows:]], axis=0)
    return both.T


def document(ends, start, stop, most):
    low, high = start * 0, start * 0 + most
    for d in range(SEG_COUNT):
        low = jnp.maximum(low, jnp.where(ends[d] <= start, ends[d], 0))
        high = jnp.minimum(high, jnp.where(ends[d] > stop, ends[d], most))
    return low, high


def key_blocks(ends, qb, span):
    length = span // 2
    here = ends[SEG_COUNT]
    far = length - here
    start = here + qb * BQ
    low, high = document(ends, start, start + BQ - 1, span)
    first = jnp.clip(low - here, 0, length) // BK
    count = (jnp.clip(high - here, 0, length) + (BK - 1)) // BK - first
    first_far = jnp.clip(low - far, 0, length) // BK
    count_far = (jnp.clip(high - far, 0, length) + (BK - 1)) // BK - first_far
    count_far = jnp.maximum(count_far, 0)

    def block(i):
        is_here = i < count
        kb = jnp.where(is_here, first + i, length // BK + first_far + (i - count))
        return kb, kb * BK + jnp.where(is_here, here, far - length)

    return count + count_far, block


def query_bounds(ends, qb, span):
    pos = ends[SEG_COUNT] + qb * BQ + lax.broadcasted_iota(jnp.int32, (1, BQ), 1)
    return document(ends, pos, pos, span)


def key_mask(bounds, base):
    key_pos = lax.broadcasted_iota(jnp.int32, (BK, BQ), 0) + base
    same = (key_pos >= bounds[0]) & (key_pos < bounds[1])
    return jnp.concatenate([same, same], axis=1)


def attn_fwd_kernel(first_block, ends, q_ref, k_ref, v_ref, o_ref, lse_ref, acc, top, den):
    span = k_ref.shape[0]
    qb = pl.program_id(0) + first_block
    pairs = q_ref.shape[1] // 128
    acc[...] = jnp.zeros_like(acc)
    top[...] = jnp.full_like(top, mask_fill)
    den[...] = jnp.zeros_like(den)
    queries = [two_heads(q_ref[:, 128 * p : 128 * p + 128]) for p in range(pairs)]
    bounds = query_bounds(ends, qb, span)
    count, block = key_blocks(ends, qb, span)

    @pl.loop(0, count)
    def _(i):
        kb, base = block(i)
        rows = pl.ds(pl.multiple_of(kb * BK, BK), BK)
        same = key_mask(bounds, base)
        for p in range(pairs):
            cols = slice(128 * p, 128 * p + 128)
            s = dot(k_ref[rows, cols], queries[p], NT)
            s = jnp.where(same, s, mask_fill)
            old = top[p]
            new = jnp.maximum(old, jnp.max(s, axis=0, keepdims=True))
            e = jnp.exp(s - new)
            shrink = jnp.exp(old - new)
            den[p] = den[p] * shrink + jnp.sum(e, axis=0, keepdims=True)
            top[p] = new
            acc[p] = acc[p] * shrink + dot(v_ref[rows, cols], e.astype(jnp.bfloat16), TN)

    for p in range(pairs):
        out = fold_heads(acc[p] / den[p])
        o_ref[:, 128 * p : 128 * p + 128] = out.astype(o_ref.dtype)
        lse_ref[p] = top[p] + jnp.log(den[p])


def row_sums(grads, outs):
    prod = (grads.astype(jnp.float32) * outs.astype(jnp.float32)).T
    return jnp.concatenate(
        [jnp.sum(prod[:DH], axis=0, keepdims=True), jnp.sum(prod[DH:], axis=0, keepdims=True)],
        axis=1,
    )


def attn_bwd_kernel(
    ends,
    q_ref,
    do_ref,
    o_low,
    o_high,
    lse_low,
    lse_high,
    k_ref,
    v_ref,
    dq_ref,
    dk_ref,
    dv_ref,
    dk_acc,
    dv_acc,
    dq_acc,
):
    span = k_ref.shape[0]
    qb = pl.program_id(0)
    is_low = qb < pl.num_programs(0) // 2
    pairs = q_ref.shape[1] // 128
    cols = [slice(128 * p, 128 * p + 128) for p in range(pairs)]

    @pl.when(qb == 0)
    def _():
        dk_acc[...] = jnp.zeros_like(dk_acc)
        dv_acc[...] = jnp.zeros_like(dv_acc)

    dq_acc[...] = jnp.zeros_like(dq_acc)
    outs = jnp.where(is_low, o_low[...], o_high[...])
    lses = jnp.where(is_low, lse_low[...], lse_high[...])
    queries = [two_heads(q_ref[:, c]) for c in cols]
    grads = [two_heads(do_ref[:, c]) for c in cols]
    deltas = [row_sums(do_ref[:, c], outs[:, c]) for c in cols]
    bounds = query_bounds(ends, qb, span)
    count, block = key_blocks(ends, qb, span)

    @pl.loop(0, count)
    def _(i):
        kb, base = block(i)
        rows = pl.ds(pl.multiple_of(kb * BK, BK), BK)
        same = key_mask(bounds, base)
        for p, c in enumerate(cols):
            keys = k_ref[rows, c]
            s = dot(keys, queries[p], NT)
            probs = jnp.exp(jnp.where(same, s, mask_fill) - lses[p])
            dp = dot(v_ref[rows, c], grads[p], NT)
            ds = (probs * (dp - deltas[p])).astype(jnp.bfloat16)
            dv_acc[rows, c] += dot(probs.astype(jnp.bfloat16), grads[p])
            dk_acc[rows, c] += dot(ds, queries[p])
            dq_acc[p] += dot(keys, ds, TN)

    for p, c in enumerate(cols):
        dq_ref[:, c] = (fold_heads(dq_acc[p]) * (DH**-0.5)).astype(dq_ref.dtype)

    @pl.when(qb == pl.num_programs(0) - 1)
    def _():
        dk_ref[...] = dk_acc[...].astype(dk_ref.dtype)
        dv_ref[...] = dv_acc[...].astype(dv_ref.dtype)


def params(mib):
    return pltpu.CompilerParams(vmem_limit_bytes=mib * 2**20)


def cost(seconds):
    return pl.CostEstimate(flops=int(seconds * 1.15e15), bytes_accessed=2**20, transcendentals=0)


def attn_forward(ends, first_block, queries, keys, values):
    rows, width = queries.shape
    span = keys.shape[0]
    pairs = width // 128
    every = pl.BlockSpec((span, width), lambda i, e: (0, 0))
    return pl.pallas_call(
        functools.partial(attn_fwd_kernel, first_block),
        grid_spec=pltpu.PrefetchScalarGridSpec(
            num_scalar_prefetch=1,
            grid=(rows // BQ // 2,),
            in_specs=[
                pl.BlockSpec((BQ, width), lambda i, e: (i + first_block, 0)),
                every,
                every,
            ],
            out_specs=[
                pl.BlockSpec((BQ, width), lambda i, e: (i, 0)),
                pl.BlockSpec((pairs, 1, 2 * BQ), lambda i, e: (0, 0, i)),
            ],
            scratch_shapes=[
                pltpu.VMEM((pairs, 128, 2 * BQ), jnp.float32),
                pltpu.VMEM((pairs, 1, 2 * BQ), jnp.float32),
                pltpu.VMEM((pairs, 1, 2 * BQ), jnp.float32),
            ],
        ),
        out_shape=[
            jax.ShapeDtypeStruct((rows // 2, width), jnp.bfloat16),
            jax.ShapeDtypeStruct((pairs, 1, rows), jnp.float32),
        ],
        compiler_params=params(VMEM_MIB),
        cost_estimate=cost(10e-6),
        name="attn_fwd",
    )(ends, queries, keys, values)


def attn_backward(ends, queries, grads, mixed, lse, keys, values):
    rows, width = queries.shape
    span = keys.shape[0]
    pairs = width // 128
    half = rows // BQ // 2
    tile = pl.BlockSpec((BQ, width), lambda i, e: (i, 0))
    low = pl.BlockSpec((BQ, width), lambda i, e: (jnp.minimum(i, half - 1), 0))
    high = pl.BlockSpec((BQ, width), lambda i, e: (jnp.maximum(i - half, 0), 0))
    low_line = pl.BlockSpec((pairs, 1, 2 * BQ), lambda i, e: (0, 0, jnp.minimum(i, half - 1)))
    high_line = pl.BlockSpec((pairs, 1, 2 * BQ), lambda i, e: (0, 0, jnp.maximum(i - half, 0)))
    every = pl.BlockSpec((span, width), lambda i, e: (0, 0))
    return pl.pallas_call(
        attn_bwd_kernel,
        grid_spec=pltpu.PrefetchScalarGridSpec(
            num_scalar_prefetch=1,
            grid=(rows // BQ,),
            in_specs=[tile, tile, low, high, low_line, high_line, every, every],
            out_specs=[tile, every, every],
            scratch_shapes=[
                pltpu.VMEM((span, width), jnp.float32),
                pltpu.VMEM((span, width), jnp.float32),
                pltpu.VMEM((pairs, 128, 2 * BQ), jnp.float32),
            ],
        ),
        out_shape=[
            jax.ShapeDtypeStruct((rows, width), jnp.bfloat16),
            jax.ShapeDtypeStruct((span, width), jnp.bfloat16),
            jax.ShapeDtypeStruct((span, width), jnp.bfloat16),
        ],
        compiler_params=params(VMEM_MIB),
        cost_estimate=cost(25e-6),
        name="attn_bwd",
    )(ends, queries, grads, *mixed, *lse, keys, values)


def full_spec(shape):
    return pl.BlockSpec(shape, lambda i: (0,) * len(shape))


def rows_spec(rows, cols):
    return pl.BlockSpec((rows, cols), lambda i: (i, 0))


def pack_kernel(q_ref, k_ref, v_ref, out_ref):
    parts = [q_ref[...], k_ref[...], v_ref[...]]
    for i, part in enumerate(parts):
        out_ref[:, 128 * i : 128 * i + 128] = part[:, :128]
    thirds = [p[:, 128:] for p in parts]
    thirds.append(jnp.zeros_like(thirds[0]))
    out_ref[:, 384:512] = jnp.concatenate(thirds[:2], axis=1)
    out_ref[:, 512:640] = jnp.concatenate(thirds[2:], axis=1)


def pack_heads(*parts):
    return pl.pallas_call(
        pack_kernel,
        out_shape=jax.ShapeDtypeStruct((parts[0].shape[0], 640), parts[0].dtype),
        compiler_params=params(8),
        cost_estimate=cost(1e-6),
        name="pack_heads",
    )(*parts)


def qkv_kernel(x_ref, a_ref, b_ref, q_ref, k_ref, v_ref, wq_ref, wk_ref, wv_ref):
    step = pl.program_id(0)

    @pl.when(step == 0)
    def _():
        for i, out in enumerate((wq_ref, wk_ref, wv_ref)):
            lo = 384 + DH * i
            out[:, :128] = a_ref[:, 128 * i : 128 * i + 128]
            out[:, 128:256] = b_ref[:, 128 * i : 128 * i + 128]
            out[:, 256:] = jnp.concatenate([a_ref[:, lo : lo + DH], b_ref[:, lo : lo + DH]], axis=1)

    x = x_ref[...]
    k_ref[...] = dot(x, wk_ref[...]).astype(k_ref.dtype)
    v_ref[...] = dot(x, wv_ref[...]).astype(v_ref.dtype)

    @pl.when(step < pl.num_programs(0) // 2)
    def _():
        q = dot(x, wq_ref[...]).astype(jnp.bfloat16).astype(jnp.float32)
        q_ref[...] = (q * DH**-0.5).astype(q_ref.dtype)


def project(tok_all, w_a, w_b):
    span, width = tok_all.shape
    block = 512
    steps = span // block
    cols = 384
    low = jnp.bfloat16
    return pl.pallas_call(
        qkv_kernel,
        grid=(steps,),
        in_specs=[rows_spec(block, width), full_spec(w_a.shape), full_spec(w_b.shape)],
        out_specs=[
            pl.BlockSpec((block, cols), lambda i: (jnp.minimum(i, steps // 2 - 1), 0)),
            rows_spec(block, cols),
            rows_spec(block, cols),
        ]
        + [full_spec((width, cols))] * 3,
        out_shape=[
            jax.ShapeDtypeStruct((span // 2, cols), low),
            jax.ShapeDtypeStruct((span, cols), low),
            jax.ShapeDtypeStruct((span, cols), low),
        ]
        + [jax.ShapeDtypeStruct((width, cols), low)] * 3,
        compiler_params=params(VMEM_MIB),
        cost_estimate=cost(6e-6),
        name="qkv",
    )(tok_all, w_a, w_b)


def attn_out_kernel(low_ref, high_ref, a_ref, b_ref, part_ref, ow_ref, proj_ref, norms_ref):
    step = pl.program_id(0)

    @pl.when(step == 0)
    def _():
        ow_ref[:, :128] = a_ref[:, :128]
        ow_ref[:, 128:256] = b_ref[:, :128]
        ow_ref[:, 256:] = jnp.concatenate([a_ref[:, 128:192], b_ref[:, 128:192]], axis=1)
        proj_ref[...] = a_ref[:, 192:320]
        turned = a_ref[:, 256:384].astype(jnp.float32).T
        norms_ref[...] = turned[64:72]

    mixed = jnp.where(step < pl.num_programs(0) // 2, low_ref[...], high_ref[...])
    part_ref[...] = dot(mixed, ow_ref[...], NT).astype(part_ref.dtype)


def attn_out(mixed, w_a, w_b):
    half, cols = mixed[0].shape
    width = w_a.shape[0]
    block = 256
    per = half // block
    low = jnp.bfloat16
    third = pl.BlockSpec((width, 384), lambda i: (0, 2))
    return pl.pallas_call(
        attn_out_kernel,
        grid=(2 * per,),
        in_specs=[
            pl.BlockSpec((block, cols), lambda i: (jnp.minimum(i, per - 1), 0)),
            pl.BlockSpec((block, cols), lambda i: (jnp.maximum(i - per, 0), 0)),
            third,
            third,
        ],
        out_specs=[
            rows_spec(block, width),
            full_spec((width, cols)),
            full_spec((width, 128)),
            full_spec((8, width)),
        ],
        out_shape=[
            jax.ShapeDtypeStruct((2 * half, width), low),
            jax.ShapeDtypeStruct((width, cols), low),
            jax.ShapeDtypeStruct((width, 128), low),
            jax.ShapeDtypeStruct((8, width), jnp.float32),
        ],
        compiler_params=params(VMEM_MIB),
        cost_estimate=cost(3e-6),
        name="attn_out",
    )(*mixed, w_a, w_b)


def normalize(hidden):
    row_mean = jnp.mean(hidden, axis=-1, keepdims=True)
    centred = hidden - row_mean
    variance = jnp.mean(centred * centred, axis=-1, keepdims=True)
    inv_std = lax.rsqrt(variance + eps_norm)
    return centred * inv_std, inv_std


def norm_backward(grad_out, normed, inv_std, gain):
    scaled = grad_out * gain
    return inv_std * (
        scaled
        - jnp.mean(scaled, axis=-1, keepdims=True)
        - normed * jnp.mean(scaled * normed, axis=-1, keepdims=True)
    )


def wide(ref):
    return ref[...].astype(jnp.float32)


def first_norm_kernel(x_ref, mine_ref, got_ref, norms, normed_ref, inv_ref, low_ref, turned_ref):
    normed, inv = normalize(wide(x_ref) + (wide(mine_ref) + wide(got_ref)))
    normed_ref[...] = normed
    inv_ref[...] = jnp.broadcast_to(inv, inv_ref.shape)
    low = (normed * norms[0:1, :] + norms[1:2, :]).astype(jnp.bfloat16)
    low_ref[...] = low
    turned_ref[...] = low.T


def first_norm(tok, mine, got, norms):
    rows, width = tok.shape
    block = 256
    tile = rows_spec(block, width)
    return pl.pallas_call(
        first_norm_kernel,
        grid=(rows // block,),
        in_specs=[tile, tile, tile, full_spec(norms.shape)],
        out_specs=[
            tile,
            rows_spec(block, 128),
            tile,
            pl.BlockSpec((width, block), lambda i: (0, i)),
        ],
        out_shape=[
            jax.ShapeDtypeStruct((rows, width), jnp.float32),
            jax.ShapeDtypeStruct((rows, 128), jnp.float32),
            jax.ShapeDtypeStruct((rows, width), jnp.bfloat16),
            jax.ShapeDtypeStruct((width, rows), jnp.bfloat16),
        ],
        compiler_params=params(VMEM_MIB),
        cost_estimate=cost(3e-6),
        name="first_norm",
    )(tok, mine, got, norms)


def gelu_parts(v):
    e = jnp.exp(v * v * -0.5)
    t = 1.0 / (1.0 + (0.3275911 * 0.5**0.5) * jnp.abs(v))
    poly = 0.5 * 1.061405429
    for c in (-1.453152027, 1.421413741, -0.284496736, 0.254829592):
        poly = poly * t + 0.5 * c
    upper = poly * t * e
    cdf = jnp.where(v >= 0, 1.0 - upper, upper)
    return v * cdf, cdf + v * e * 0.3989422804014327


def ffn_in_kernel(x_ref, a_ref, b_ref, act_ref, slope_ref):
    def work(w_ref):
        for r in range(0, x_ref.shape[0], 256):
            rows = slice(r, r + 256)
            act, slope = gelu_parts(dot(x_ref[rows, :], w_ref[...]))
            act_ref[rows, :] = act.astype(act_ref.dtype)
            slope_ref[rows, :] = slope.astype(slope_ref.dtype)

    first = pl.program_id(0) < pl.num_programs(0) // 2
    pl.when(first)(lambda: work(a_ref))
    pl.when(jnp.logical_not(first))(lambda: work(b_ref))


def ffn_in(x, w_a, w_b, hidden):
    rows, width = x.shape
    cols = 384
    per = hidden // cols
    out = pl.BlockSpec((rows, cols), lambda i: (0, i))
    shape = jax.ShapeDtypeStruct((rows, 2 * hidden), jnp.bfloat16)
    return pl.pallas_call(
        ffn_in_kernel,
        grid=(2 * per,),
        in_specs=[
            full_spec((rows, width)),
            pl.BlockSpec((width, cols), lambda i: (0, jnp.minimum(i, per - 1))),
            pl.BlockSpec((width, cols), lambda i: (0, jnp.maximum(i - per, 0))),
        ],
        out_specs=[out, out],
        out_shape=[shape, shape],
        compiler_params=params(VMEM_MIB),
        cost_estimate=cost(10e-6),
        name="ffn_in",
    )(x, w_a, w_b)


def ffn_out_kernel(act_ref, a_ref, b_ref, out_ref):
    hidden = a_ref.shape[1]
    part = dot(act_ref[:, :hidden], a_ref[...], NT) + dot(act_ref[:, hidden:], b_ref[...], NT)
    out_ref[...] = part.astype(out_ref.dtype)


def ffn_out(act, w_a, w_b):
    rows = act.shape[0]
    width = w_a.shape[0]
    block = 256
    return pl.pallas_call(
        ffn_out_kernel,
        grid=(rows // block,),
        in_specs=[rows_spec(block, act.shape[1]), full_spec(w_a.shape), full_spec(w_b.shape)],
        out_specs=rows_spec(block, width),
        out_shape=jax.ShapeDtypeStruct((rows, width), jnp.bfloat16),
        compiler_params=params(VMEM_MIB),
        cost_estimate=cost(3e-6),
        name="ffn_out",
    )(act, w_a, w_b)


def middle_kernel(
    normed_ref, mine_ref, got_ref, norms, proj_ref, cot_ref, emb_ref, gh2_ref, low_ref, turned_ref, pg_ref, vec_ref
):
    step = pl.program_id(0)
    first = normed_ref[...] * norms[0:1, :] + norms[1:2, :]
    normed, inv = normalize(first + (wide(mine_ref) + wide(got_ref)))
    second = (normed * norms[2:3, :] + norms[3:4, :]).astype(jnp.bfloat16)
    projected = dot(second, proj_ref[...])
    inv_norm = lax.rsqrt(jnp.sum(projected * projected, axis=-1, keepdims=True) + eps_unit)
    embedding = projected * inv_norm
    emb_ref[...] = embedding
    cot = wide(cot_ref)
    radial = jnp.sum(cot * embedding, axis=-1, keepdims=True)
    grad_projected = (inv_norm * (cot - embedding * radial)).astype(jnp.bfloat16)
    grad_second = dot(grad_projected, proj_ref[...], NT)
    grad = norm_backward(grad_second, normed, inv, norms[2:3, :])
    gh2_ref[...] = grad
    low = grad.astype(jnp.bfloat16)
    low_ref[...] = low
    turned_ref[...] = low.T

    @pl.when(step == 0)
    def _():
        pg_ref[...] = jnp.zeros_like(pg_ref)
        vec_ref[...] = jnp.zeros_like(vec_ref)

    pg_ref[...] += dot(second, grad_projected, TN)
    vec_ref[0:1, :] += jnp.sum(grad_second * normed, axis=0, keepdims=True)
    vec_ref[1:2, :] += jnp.sum(grad_second, axis=0, keepdims=True)


def middle(normed, mine, got, norms, proj, cot):
    rows, width = normed.shape
    p_width = proj.shape[1]
    block = 256
    tile = rows_spec(block, width)
    return pl.pallas_call(
        middle_kernel,
        grid=(rows // block,),
        in_specs=[
            tile,
            tile,
            tile,
            full_spec(norms.shape),
            full_spec(proj.shape),
            rows_spec(block, p_width),
        ],
        out_specs=[
            rows_spec(block, p_width),
            tile,
            tile,
            pl.BlockSpec((width, block), lambda i: (0, i)),
            full_spec((width, p_width)),
            full_spec((8, width)),
        ],
        out_shape=[
            jax.ShapeDtypeStruct((rows, p_width), jnp.float32),
            jax.ShapeDtypeStruct((rows, width), jnp.float32),
            jax.ShapeDtypeStruct((rows, width), jnp.bfloat16),
            jax.ShapeDtypeStruct((width, rows), jnp.bfloat16),
            jax.ShapeDtypeStruct((width, p_width), jnp.float32),
            jax.ShapeDtypeStruct((8, width), jnp.float32),
        ],
        compiler_params=params(VMEM_MIB),
        cost_estimate=cost(5e-6),
        name="middle",
    )(normed, mine, got, norms, proj, cot)


def back_outer_kernel(g_ref, gt_ref, act_ref, slope_ref, a_ref, b_ref, wga_ref, wgb_ref, gpre_ref):
    def work(w_ref, wg_ref):
        wg_ref[...] = dot(gt_ref[...], act_ref[...]).astype(wg_ref.dtype)
        for r in range(0, g_ref.shape[0], 256):
            rows = slice(r, r + 256)
            grad = dot(g_ref[rows, :], w_ref[...]) * slope_ref[rows, :].astype(jnp.float32)
            gpre_ref[rows, :] = grad.astype(gpre_ref.dtype)

    first = pl.program_id(0) < pl.num_programs(0) // 2
    pl.when(first)(lambda: work(a_ref, wga_ref))
    pl.when(jnp.logical_not(first))(lambda: work(b_ref, wgb_ref))


def back_outer(grad, grad_t, act, slope, w_a, w_b):
    rows, width = grad.shape
    hidden = w_a.shape[1]
    cols = 384
    per = hidden // cols
    tile = pl.BlockSpec((rows, cols), lambda i: (0, i))
    mat_a = pl.BlockSpec((width, cols), lambda i: (0, jnp.minimum(i, per - 1)))
    mat_b = pl.BlockSpec((width, cols), lambda i: (0, jnp.maximum(i - per, 0)))
    shape = jax.ShapeDtypeStruct((width, hidden), jnp.bfloat16)
    return pl.pallas_call(
        back_outer_kernel,
        grid=(2 * per,),
        in_specs=[full_spec((rows, width)), full_spec((width, rows)), tile, tile, mat_a, mat_b],
        out_specs=[mat_a, mat_b, tile],
        out_shape=[shape, shape, jax.ShapeDtypeStruct(act.shape, jnp.bfloat16)],
        compiler_params=params(VMEM_MIB),
        cost_estimate=cost(9e-6),
        name="back_outer",
    )(grad, grad_t, act, slope, w_a, w_b)


def back_inner_kernel(xt_ref, gpre_ref, a_ref, b_ref, wga_ref, wgb_ref, out_ref, acc):
    step = pl.program_id(0)

    @pl.when(step == 0)
    def _():
        acc[...] = jnp.zeros_like(acc)

    def work(w_ref, wg_ref):
        wg_ref[...] = dot(xt_ref[...], gpre_ref[...]).astype(wg_ref.dtype)
        acc[...] += dot(gpre_ref[...], w_ref[...], NT)

    first = step < pl.num_programs(0) // 2
    pl.when(first)(lambda: work(a_ref, wga_ref))
    pl.when(jnp.logical_not(first))(lambda: work(b_ref, wgb_ref))

    @pl.when(step == pl.num_programs(0) - 1)
    def _():
        out_ref[...] = acc[...].astype(out_ref.dtype)


def back_inner(x_t, grad_pre, w_a, w_b, hidden):
    width, rows = x_t.shape
    cols = 384
    per = hidden // cols
    mat_a = pl.BlockSpec((width, cols), lambda i: (0, jnp.minimum(i, per - 1)))
    mat_b = pl.BlockSpec((width, cols), lambda i: (0, jnp.maximum(i - per, 0)))
    shape = jax.ShapeDtypeStruct((width, hidden), jnp.bfloat16)
    return pl.pallas_call(
        back_inner_kernel,
        grid=(2 * per,),
        in_specs=[
            full_spec((width, rows)),
            pl.BlockSpec((rows, cols), lambda i: (0, i)),
            mat_a,
            mat_b,
        ],
        out_specs=[mat_a, mat_b, full_spec((rows, width))],
        out_shape=[shape, shape, jax.ShapeDtypeStruct((rows, width), jnp.bfloat16)],
        scratch_shapes=[pltpu.VMEM((rows, width), jnp.float32)],
        compiler_params=params(VMEM_MIB),
        cost_estimate=cost(9e-6),
        name="back_inner",
    )(x_t, grad_pre, w_a, w_b)


def first_back_kernel(
    mine_ref,
    got_ref,
    gh2_ref,
    normed_ref,
    inv_ref,
    norms,
    ow_ref,
    low_ref,
    high_ref,
    pg_ref,
    vec2_ref,
    gh1_ref,
    gmix_ref,
    og_ref,
    small_ref,
    og_acc,
    vec,
):
    step = pl.program_id(0)
    steps = pl.num_programs(0)

    @pl.when(step == 0)
    def _():
        og_acc[...] = jnp.zeros_like(og_acc)
        vec[...] = jnp.zeros_like(vec)
        vec[2:4, :] = vec2_ref[0:2, :]

    grad = gh2_ref[...] + (wide(mine_ref) + wide(got_ref))
    normed = normed_ref[...]
    vec[0:1, :] += jnp.sum(grad * normed, axis=0, keepdims=True)
    vec[1:2, :] += jnp.sum(grad, axis=0, keepdims=True)
    grad_h1 = norm_backward(grad, normed, inv_ref[:, 0:1], norms[0:1, :])
    gh1_ref[...] = grad_h1
    low = grad_h1.astype(jnp.bfloat16)
    gmix_ref[...] = dot(low, ow_ref[...]).astype(gmix_ref.dtype)
    mixed = jnp.where(step < steps // 2, low_ref[...], high_ref[...])
    og_acc[...] += dot(low, mixed, TN)

    @pl.when(step == steps - 1)
    def _():
        og_ref[...] = og_acc[...].astype(og_ref.dtype)
        p_width = pg_ref.shape[1]
        small_ref[:, :p_width] = pg_ref[...].astype(small_ref.dtype)
        small_ref[:, p_width:] = vec[...].T.astype(small_ref.dtype)


def first_back(mine, got, grad_h2, normed, inv, norms, output_w, mixed, proj_part, vec2):
    rows, width = grad_h2.shape
    cols = output_w.shape[1]
    block = 256
    per = rows // block // 2
    tile = rows_spec(block, width)
    low = jnp.bfloat16
    p_width = proj_part.shape[1]
    return pl.pallas_call(
        first_back_kernel,
        grid=(2 * per,),
        in_specs=[
            tile,
            tile,
            tile,
            tile,
            rows_spec(block, 128),
            full_spec(norms.shape),
            full_spec(output_w.shape),
            pl.BlockSpec((block, cols), lambda i: (jnp.minimum(i, per - 1), 0)),
            pl.BlockSpec((block, cols), lambda i: (jnp.maximum(i - per, 0), 0)),
            full_spec(proj_part.shape),
            full_spec(vec2.shape),
        ],
        out_specs=[
            tile,
            rows_spec(block, cols),
            full_spec((width, cols)),
            full_spec((width, p_width + 128)),
        ],
        out_shape=[
            jax.ShapeDtypeStruct((rows, width), jnp.float32),
            jax.ShapeDtypeStruct((rows, cols), low),
            jax.ShapeDtypeStruct((width, cols), low),
            jax.ShapeDtypeStruct((width, p_width + 128), low),
        ],
        scratch_shapes=[pltpu.VMEM((width, cols), jnp.float32), pltpu.VMEM((128, width), jnp.float32)],
        compiler_params=params(VMEM_MIB),
        cost_estimate=cost(6e-6),
        name="first_back",
    )(mine, got, grad_h2, normed, inv, norms, output_w, *mixed, proj_part, vec2)


def far_kernel(dk, dv, wk, wv, gx_ref):
    gx_ref[...] = (dot(dk[...], wk[...], NT) + dot(dv[...], wv[...], NT)).astype(gx_ref.dtype)


def far_grads(dk, dv, key_w, value_w):
    rows = dk.shape[0] // 2
    width, cols = key_w.shape
    block = 512
    tile = pl.BlockSpec((block, cols), lambda i: (i + rows // block, 0))
    return pl.pallas_call(
        far_kernel,
        grid=(rows // block,),
        in_specs=[tile] * 2 + [full_spec((width, cols))] * 2,
        out_specs=rows_spec(block, width),
        out_shape=jax.ShapeDtypeStruct((rows, width), jnp.bfloat16),
        compiler_params=params(VMEM_MIB),
        cost_estimate=cost(3e-6),
        name="far_grads",
    )(dk, dv, key_w, value_w)


def head_grads_kernel(x_ref, dq, dk, dv, wq, wk, wv, og_ref, gx_ref, a_ref, b_ref, acc):
    step = pl.program_id(0)
    steps = pl.num_programs(0)

    @pl.when(step == 0)
    def _():
        acc[...] = jnp.zeros_like(acc)

    x_t = x_ref[...].T
    acc[1] += dot(x_t, dk[...])
    acc[2] += dot(x_t, dv[...])

    @pl.when(step < steps // 2)
    def _():
        acc[0] += dot(x_t, dq[...])
        gx = dot(dk[...], wk[...], NT) + dot(dv[...], wv[...], NT) + dot(dq[...], wq[...], NT)
        gx_ref[...] = gx.astype(gx_ref.dtype)

    @pl.when(step == steps - 1)
    def _():
        for s, out in enumerate((a_ref, b_ref)):
            for i in range(4):
                part = og_ref if i == 3 else acc.at[i]
                lo = 128 * s
                out[:, 128 * i : 128 * i + 128] = part[:, lo : lo + 128].astype(out.dtype)
            for i in (0, 2):
                lo = 256 + DH * s
                both = [
                    (og_ref if j == 3 else acc.at[j])[:, lo : lo + DH].astype(out.dtype)
                    for j in (i, i + 1)
                ]
                out[:, 512 + DH * i : 512 + DH * i + 128] = jnp.concatenate(both, axis=1)


def head_grads(tok_all, dq, dk, dv, weights, output_part):
    span, width = tok_all.shape
    block = 512
    steps = span // block
    cols = dq.shape[1]
    low = jnp.bfloat16
    near = lambda i: (jnp.minimum(i, steps // 2 - 1), 0)
    packed = full_spec((width, 768))
    return pl.pallas_call(
        head_grads_kernel,
        grid=(steps,),
        in_specs=[
            rows_spec(block, width),
            pl.BlockSpec((block, cols), near),
            rows_spec(block, cols),
            rows_spec(block, cols),
        ]
        + [full_spec((width, cols))] * 4,
        out_specs=[pl.BlockSpec((block, width), near), packed, packed],
        out_shape=[
            jax.ShapeDtypeStruct((span // 2, width), low),
            jax.ShapeDtypeStruct((width, 768), low),
            jax.ShapeDtypeStruct((width, 768), low),
        ],
        scratch_shapes=[pltpu.VMEM((3, width, cols), jnp.float32)],
        compiler_params=params(VMEM_MIB),
        cost_estimate=cost(9e-6),
        name="head_grads",
    )(tok_all, dq, dk, dv, *weights, output_part)


def unpack_heads(packed):
    return [
        jnp.concatenate(
            [packed[:, 128 * i : 128 * i + 128], packed[:, 512 + DH * i : 512 + DH * i + DH]], axis=1
        )
        for i in range(4)
    ]


def per_device(
    tokens,
    segments,
    query_weight,
    key_weight,
    value_weight,
    output_weight,
    attn_gain,
    attn_shift,
    inner_weight,
    outer_weight,
    ffn_gain,
    ffn_shift,
    proj_weight,
    grad_embed,
):
    length, model_width = tokens.shape[2:]
    half = length // 2
    core = lax.axis_index("shard") % 2
    ctx = lax.axis_index("ctx")
    group = lax.axis_index("tp")
    micro, seat = group // 2, group % 2
    owner = core == seat
    edge = min(SEG_MOST, length)
    bf16, f32 = jnp.bfloat16, jnp.float32

    tok_m = lax.dynamic_index_in_dim(tokens, micro, 0, False)[0]
    sent = lax.dynamic_slice_in_dim(tok_m, (1 - ctx) * (length - edge), edge, 0)
    got = route(sent, lambda s, c, t: (s, 1 - c, t) if s % 2 == t % 2 else None)
    heads_own = pack_heads(query_weight, key_weight, value_weight)
    heads_parts = gather_tp_start(heads_own)
    tokens_in, segments_in, outer_in, output_in, cot_in = after_all(
        heads_own, tokens, segments, outer_weight, output_weight, grad_embed
    )
    vectors = jnp.stack([attn_gain, attn_shift, ffn_gain, ffn_shift])
    vectors = dot(vectors, jnp.eye(4, 64, dtype=bf16), TN).astype(bf16)
    ffn_own = jnp.concatenate([inner_weight, output_in.T, proj_weight, vectors, outer_in.T], axis=1)
    ffn_all = lax.all_gather(ffn_own, "tp", axis=0)
    tok_m = lax.dynamic_index_in_dim(tokens_in, micro, 0, False)[0]
    tok_got = swap(tok_m, "shard", 1)
    seg_m = lax.dynamic_index_in_dim(segments_in, micro, 0, False)
    seg_m = seg_m.reshape(1, -1, 128)
    upto = jnp.arange(8, dtype=jnp.int32).reshape(8, 1, 1)
    counts_own = jnp.sum((seg_m <= upto).astype(jnp.int32), axis=(1, 2))
    counts_got = swap(counts_own, "shard", 1)

    heads_a, heads_b = gather_tp_finish(tie(*heads_parts, ffn_own, counts_own)[:4])
    other_a, other_b = gather_start(heads_a, "y"), gather_start(heads_b, "x")
    cot_m = lax.dynamic_index_in_dim(after(cot_in, heads_a), micro, 0, False)[0]
    cot_got = swap(cot_m, "shard", 1)
    other_a, other_b, got, tok_got, counts_got = tie(other_a, other_b, got, tok_got, counts_got)
    heads_a, heads_b = gather_finish(heads_a, other_a, "y"), gather_finish(heads_b, other_b, "x")
    other_a, other_b = gather_start(heads_a, "x"), gather_start(heads_b, "y")
    got_core = swap(got, "shard", 1)
    counts = jnp.where(owner, counts_own, counts_got)
    counts = counts + swap(counts, "ctx", 1)
    place_of = jnp.arange(8)
    ends = jnp.where(place_of == SEG_COUNT, ctx * length, counts).astype(jnp.int32)
    tok_here = jnp.where(owner, tok_m, tok_got)
    tok_far = lax.dynamic_update_slice_in_dim(
        jnp.zeros_like(tok_here), jnp.where(owner, got, got_core), ctx * (length - edge), 0
    )
    tok_all = jnp.concatenate([tok_here, tok_far], axis=0)
    cot = jnp.where(owner, cot_m, cot_got)
    other_a, other_b, tok_all, cot, ends = tie(other_a, other_b, tok_all, cot, ends)
    heads_a, heads_b = gather_finish(heads_a, other_a, "x"), gather_finish(heads_b, other_b, "y")

    queries, keys, values, *head_w = project(tok_all, flat_rows(heads_a), flat_rows(heads_b))
    ffn_all = after(ffn_all, heads_a, heads_b)
    kept = lax.dynamic_slice_in_dim(ffn_all, 2 * core, 2, 0)
    other = swap(lax.dynamic_slice_in_dim(ffn_all, 2 - 2 * core, 2, 0), "shard", 1)
    other, queries, keys, values = tie(other, queries, keys, values)
    core_dim = shard_bits() - 1
    shape = (1,) * core_dim + (1, 1) + ffn_own.shape
    split = 1152
    inner, outer = [], []
    for s in range(2):
        both = join(kept[s].reshape(shape), other[s].reshape(shape), "shard", 1, core_dim)
        inner.append(both[..., :split])
        outer.append(both[..., split:])
    inner_got = [gather_start(inner[0], "x"), gather_start(inner[1], "y")]
    outer_got = [gather_start(outer[0], "x"), gather_start(outer[1], "y")]
    mixed_low, lse_low = attn_forward(after(ends, *inner, *outer), 0, queries, keys, values)
    inner_got = after_all(mixed_low, *inner_got)
    inner = [gather_finish(inner[0], inner_got[0], "x"), gather_finish(inner[1], inner_got[1], "y")]
    inner_got = [gather_start(inner[0], "y"), gather_start(inner[1], "x")]
    mixed_high, lse_high = attn_forward(
        after(ends, mixed_low, *inner), half // BQ, queries, keys, values
    )
    outer_got = after_all(mixed_high, *outer_got)
    outer = [gather_finish(outer[0], outer_got[0], "x"), gather_finish(outer[1], outer_got[1], "y")]
    outer_got = [gather_start(outer[0], "y"), gather_start(outer[1], "x")]
    inner_got = after_all(mixed_high, *inner_got)
    inner_got = after_all(outer[0], *inner_got)
    inner_a = flat_rows(gather_finish(inner[0], inner_got[0], "y"))
    inner_b = flat_rows(gather_finish(inner[1], inner_got[1], "x"))
    mixed = (mixed_low, mixed_high)
    part, output_w, proj, norms = attn_out(mixed, inner_a, inner_b)

    hidden_cols = outer_weight.shape[0]
    normed, inv, first_low, first_t = first_norm(tok_here, part, swap(part, "shard", 1), norms)
    act, slope = ffn_in(first_low, inner_a, inner_b, hidden_cols)
    outer_got = after_all(act, *outer_got)
    outer_a = flat_rows(gather_finish(outer[0], outer_got[0], "y"))
    outer_b = flat_rows(gather_finish(outer[1], outer_got[1], "x"))
    part = ffn_out(act, outer_a, outer_b)
    embedding, grad_h2, grad_ffn, grad_ffn_t, proj_part, vec2 = middle(
        normed, part, swap(part, "shard", 1), norms, proj, cot
    )

    outer_a, outer_b, grad_pre = back_outer(grad_ffn, grad_ffn_t, act, slope, outer_a, outer_b)
    outer = [split_rows(outer_a), split_rows(outer_b)]
    outer_got = [scatter_start(outer[0], "x"), scatter_start(outer[1], "y")]
    inner_a, inner_b, part = back_inner(
        first_t, after(grad_pre, *outer), inner_a, inner_b, hidden_cols
    )
    part_got = swap(part, "shard", 1)
    inner = [split_rows(inner_a), split_rows(inner_b)]
    inner_got = [scatter_start(inner[0], "x"), scatter_start(inner[1], "y")]
    outer_got = after_all(part, *outer_got)
    outer = [
        scatter_finish(outer[0], outer_got[0], "x"),
        scatter_finish(outer[1], outer_got[1], "y"),
    ]
    outer_got = [scatter_start(outer[0], "y"), scatter_start(outer[1], "x")]
    grad_h1, grad_mixed, output_part, small = first_back(
        part,
        after(part_got, *outer, *inner),
        grad_h2,
        normed,
        inv,
        norms,
        output_w,
        mixed,
        proj_part,
        vec2,
    )
    inner_got = after_all(grad_mixed, *inner_got)
    inner = [
        scatter_finish(inner[0], inner_got[0], "x"),
        scatter_finish(inner[1], inner_got[1], "y"),
    ]
    inner_got = [scatter_start(inner[0], "y"), scatter_start(inner[1], "x")]
    outer_got = after_all(grad_mixed, *outer_got)
    outer = [
        scatter_finish(outer[0], outer_got[0], "y"),
        scatter_finish(outer[1], outer_got[1], "x"),
    ]
    outer_parts = scatter_tp_start(*outer)

    small = lax.dynamic_slice_in_dim(split_rows(small), core, 1, core_dim)
    small_got = scatter_start(small, "y")
    quarter = half // 2
    emb_half = lax.dynamic_slice_in_dim(after(embedding, grad_mixed), core * half, half, 0)
    emb_got = [
        route(
            lax.select_n(micro ^ d, emb_half[:quarter], emb_half[quarter:]),
            lambda s, c, t, d=d: (s - s % 2 + t % 2, c, 2 * (s % 2) + ((t // 2) ^ d)),
        )
        for d in range(2)
    ]
    dq, dk, dv = attn_backward(
        after(ends, *inner, *outer, small, emb_half),
        queries,
        grad_mixed,
        mixed,
        (lse_low, lse_high),
        keys,
        values,
    )

    def start_half(full):
        return swap(lax.dynamic_slice_in_dim(full, (1 - core) * half, half, 0), "shard", 1)

    def sum_half(full, got_half):
        kept_half = lax.dynamic_slice_in_dim(full, core * half, half, 0)
        return kept_half.astype(f32) + got_half.astype(f32)

    gx_far = far_grads(dk, dv, *head_w[1:])
    far_got = start_half(gx_far)
    *inner_got, small_got = after_all(gx_far, *inner_got, small_got)
    inner = [
        scatter_finish(inner[0], inner_got[0], "y"),
        scatter_finish(inner[1], inner_got[1], "x"),
    ]
    small = scatter_finish(small, small_got, "y")
    small_got = scatter_start(small, "x")
    far_sum = sum_half(gx_far, after(far_got, *inner, small)).astype(bf16)
    from_far = swap(far_sum, "ctx", 1)
    inner_parts = scatter_tp_start(*inner)
    gx, grad_a, grad_b = head_grads(
        after(tok_all, far_sum, *inner), dq, dk, dv, head_w, output_part
    )
    gx_got = start_half(gx)
    grad_a, grad_b = split_rows(grad_a), split_rows(grad_b)
    got_a, got_b = scatter_start(grad_a, "y"), scatter_start(grad_b, "x")
    outer_parts = after_all(gx, *outer_parts)
    outer_grad = sum_all(outer_parts).reshape(-1, hidden_cols).T
    small = scatter_finish(small, after(small_got, gx), "x").reshape(-1, small.shape[-1])
    small_parts = [small] + [swap(small, "tp", d) for d in range(1, 4)]
    mine = lax.dynamic_slice_in_dim(grad_h1, core * half, half, 0)
    gx_sum = sum_half(gx, gx_got)
    grad_tok = (gx_sum + after(from_far, gx_got).astype(f32) + mine).astype(bf16)
    own_cols = model_width // lax.axis_size("tp")
    col_parts = [grad_tok[:, own_cols * j : own_cols * (j + 1)] for j in range(4)]
    place = 2 * micro + core
    arrived = [
        route(
            lax.select_n(place ^ d, *col_parts),
            lambda s, c, t, d=d: (s - s % 2 + t % 2, c, (2 * (t // 2) + s % 2) ^ d),
        )
        for d in range(4)
    ]
    got_a, got_b, *inner_parts = after_all(grad_tok, got_a, got_b, *inner_parts)
    grad_a, grad_b = scatter_finish(grad_a, got_a, "y"), scatter_finish(grad_b, got_b, "x")
    got_a, got_b = scatter_start(grad_a, "x"), scatter_start(grad_b, "y")
    *inner_parts, small_last = after_all((grad_a, grad_b), *inner_parts, small_parts[-1])
    inner_grad = sum_all(inner_parts).reshape(-1, hidden_cols)
    small = sum_all(small_parts[:3] + [small_last])
    emb_got = after_all(grad_tok, *emb_got)
    embeddings = jnp.stack([lax.select_n((group % 2) ^ m, *emb_got) for m in range(2)])
    embeddings = embeddings.reshape(2, 1, quarter, -1)
    got_a, got_b = after_all(inner_grad, got_a, got_b)
    grad_a, grad_b = scatter_finish(grad_a, got_a, "x"), scatter_finish(grad_b, got_b, "y")
    heads_grad = sum_all(scatter_tp_start(grad_a, grad_b))
    heads_grad = heads_grad.reshape(-1, heads_grad.shape[-1])
    arrived = after_all((grad_a, grad_b), *arrived)
    grad_tokens = jnp.stack([lax.select_n(group ^ j, *arrived) for j in range(4)])
    grad_tokens = grad_tokens.reshape(2, 1, length, own_cols).astype(f32)
    query_grad, key_grad, value_grad, output_grad = unpack_heads(heads_grad)
    p_width = proj_part.shape[1]
    return (
        embeddings,
        grad_tokens,
        query_grad,
        key_grad,
        value_grad,
        output_grad.T,
        small[:, p_width],
        small[:, p_width + 1],
        inner_grad,
        outer_grad,
        small[:, p_width + 2],
        small[:, p_width + 3],
        small[:, :p_width],
    )


def solution(mesh):
    rows = ("shard", "ctx")
    placed = (
        P(None, "shard", "ctx", None),
        P(None, "shard", "ctx"),
        P(rows, "tp"),
        P(rows, "tp"),
        P(rows, "tp"),
        P("tp", rows),
        P(rows),
        P(rows),
        P(rows, "tp"),
        P("tp", rows),
        P(rows),
        P(rows),
        P(rows, None),
        P(None, "shard", "ctx", None),
    )
    return jax.shard_map(
        per_device,
        mesh=mesh,
        in_specs=placed,
        out_specs=(
            P(None, "shard", ("ctx", "tp"), None),
            P(None, "shard", "ctx", "tp"),
            P(rows, "tp"),
            P(rows, "tp"),
            P(rows, "tp"),
            P("tp", rows),
            P(rows),
            P(rows),
            P(rows, "tp"),
            P("tp", rows),
            P(rows),
            P(rows),
            P(rows, None),
        ),
        check_vma=False,
    )
```

time: 474 us -> 378 us (0.80)
  Pallas kernels: 37.2 us -> 128 us
  matrix products: 63.5 us -> 0.88 us
  waiting for transfers between devices: 137 us -> 89.6 us
  other arithmetic: 63.1 us -> 23.1 us
  local copies, waits for them, and re-layouts: 65.7 us -> 28.7 us
  between operations: 2.89 us -> 15.8 us
  starting transfers between devices: 97.2 us -> 86.8 us
    pallas_call x1 -> x14, Pallas kernels: 17.3 us -> 104 us  [the longest x2 20.2 us: attn_forward(): pl.pallas_call(functools.partial(attn_fwd_kernel, first_block), grid_spec...]
    ppermute x58 -> x41, waiting for transfers between devices: 133 us -> 56.4 us  [swap(): return lax.ppermute(v, axis, [(i, i ^ bit) for i in range(count)])]
    dot_general x6 -> x0, matrix products: 41.4 us -> none  [the longest x1 18.3 us: per_device(): jnp.einsum('td,zdf->ztf', first_low, inner_full, preferred_element_type=f32)]
    ppermute x58 -> x41, starting transfers between devices: 74.7 us -> 44.7 us  [swap(): return lax.ppermute(v, axis, [(i, i ^ bit) for i in range(count)])]
    ppermute x7 -> x23, waiting for transfers between devices: 4.46 us -> 26.9 us  [route(): return lax.ppermute(v, ('shard', 'ctx', 'tp'), pairs)]
    dot_general x15 -> x1, matrix products: 22 us -> 0.88 us  [dot(): lax.dot_general(first_op, second_op, dims, preferred_element_type=jnp.flo...]
    ppermute x7 -> x23, starting transfers between devices: 22.5 us -> 42.1 us  [route(): return lax.ppermute(v, ('shard', 'ctx', 'tp'), pairs)]
    select_n x25 -> x24, other arithmetic: 23.6 us -> 7.55 us  [the longest x12 2.42 us: join(): jnp.where(first, cur, other)]
  transfers between devices with their start and end apart: 65 -> 65, of which waited for: 20 -> 28; matrix products, arithmetic and copies ran while one was open for 33% -> 7% of each run, Pallas kernels for 8% -> 23%
where the time goes in v2:
time: 378 us; the launch traced here: 373 us
  Pallas kernels  128 us (34%)
  waiting for transfers between devices  89.6 us (24%)
  starting transfers between devices  86.8 us (23%)
  local copies, waits for them, and re-layouts  28.7 us (8%)
  other arithmetic  23.1 us (6%)
  between operations  15.8 us (4%)
    ppermute x41, waiting for transfers between devices, swap(): return lax.ppermute(v, axis, [(i, i ^ bit) for i in range(count)])  56.4 us
    ppermute x41, starting transfers between devices, swap(): return lax.ppermute(v, axis, [(i, i ^ bit) for i in range(count)])  44.7 us
    ppermute x23, starting transfers between devices, route(): return lax.ppermute(v, ('shard', 'ctx', 'tp'), pairs)  42.1 us
    ppermute x23, waiting for transfers between devices, route(): return lax.ppermute(v, ('shard', 'ctx', 'tp'), pairs)  26.9 us
    pallas_call x1, Pallas kernels, attn_backward(): pl.pallas_call(attn_bwd_kernel, grid_spec=pltpu.PrefetchScalarGridSpec(nu...  23.6 us
    pallas_call x2, Pallas kernels, attn_forward(): pl.pallas_call(functools.partial(attn_fwd_kernel, first_block), grid_spec...  20.2 us
    unnamed x118, local copies, waits for them, and re-layouts  16.4 us
    pallas_call x1, Pallas kernels, back_outer(): pl.pallas_call(back_outer_kernel, grid=(2 * per,), in_specs=[full_spec((r...  11.3 us
  transfers between devices with their start and end apart: 65, of which 28 were waited for; matrix products, arithmetic and copies ran while one was open for 7% of the time, Pallas kernels for 23%

profile of v2, /device:TPU:1, one launch (start us, length us, event | category | flops | bytes accessed | tf_op | source)
XLA Modules:
  0.0 372.7 jit_solution(17729807433199184597)
XLA Ops:
  12.9 5.7 %collective-permute-start = (bf16[96,640]{1,0:T(8,128)(2,1)S(1)}, bf16[96,640]{1,0:T(8,128)(2,1)S(1)}, u32[]{:S(2)}, u32[]{:S(2)}) collective-permute-start(bf16[96,640]{1,0:T(8,128)(2,1)S(1)} %pack_heads.1), channel_id=1, source_target_pairs={{0,0},{1,1},{2,8},{3,9},{4,4},{5,5},{6,12},{7,13},{8,2},{9,3},{10,... | collective-permute-start | bytes 368648 | tf_op jit(solution)/shard_map/ppermute | solution.py:60
  23.0 2.9 collective-permute-start.3
  38.0 4.0 %collective-permute-done.5 = bf16[1,2,1,96,640]{4,3,2,1,0:T(8,128)(2,1)} collective-permute-done((bf16[1,2,1,96,640]{4,3,2,1,0:T(8,128)(2,1)S(1)}, bf16[1,2,1,96,640]{4,3,2,1,0:T(8,128)(2,1)}, u32[]{:S(2)}, u32[]{:S(2)}) %collective-permute-start.5) | collective-permute-done | bytes 245792 | tf_op jit(solution)/shard_map/ppermute | solution.py:44
  42.4 5.1 %collective-permute-start.11 = (bf16[800,768]{1,0:T(8,128)(2,1)S(1)}, bf16[800,768]{1,0:T(8,128)(2,1)S(1)}, u32[]{:S(2)}, u32[]{:S(2)}) collective-permute-start(bf16[800,768]{1,0:T(8,128)(2,1)S(1)} %collective-permute-done.6), channel_id=1, source_target_pairs={{0,8},{8,0},{16,24},{24,16},{1,9},{9,1},{17,25},{25,17},{2,10},{10... | collective-permute-start | bytes 3686408 | tf_op jit(solution)/shard_map/ppermute | solution.py:44
  56.9 5.7 %collective-permute-done.10 = bf16[1,2,2,96,640]{4,3,2,1,0:T(8,128)(2,1)S(1)} collective-permute-done((bf16[1,2,2,96,640]{4,3,2,1,0:T(8,128)(2,1)S(1)}, bf16[1,2,2,96,640]{4,3,2,1,0:T(8,128)(2,1)S(1)}, u32[]{:S(2)}, u32[]{:S(2)}) %collective-permute-start.10) | collective-permute-done | bytes 491552 | tf_op jit(solution)/shard_map/ppermute | solution.py:44
  64.2 6.4 %all-gather.3.cloned.1.call-done = bf16[384,1920]{1,0:T(8,128)(2,1)} async-done(((bf16[96,1920]{1,0:T(8,128)(2,1)}), bf16[384,1920]{1,0:T(8,128)(2,1)}) %all-gather.3.cloned.1.call-update) | async-done | bytes 1474576 | tf_op jit(solution)/shard_map/all_gather | solution.py:1018
  74.1 7.9 %qkv.1 = (bf16[1024,384]{1,0:T(8,128)(2,1)S(1)}, bf16[2048,384]{1,0:T(8,128)(2,1)S(1)}, bf16[2048,384]{1,0:T(8,128)(2,1)}, bf16[768,384]{1,0:T(8,128)(2,1)S(1)},...) custom-call(bf16[2048,768]{1,0:T(8,128)(2,1)} %pad_maximum_fusion.x_ref, bf16[768,640]{1,0:T(8,128)(2,1)S(1)} %bitcast.123, ...), custom_call_target="tpu_custom_call" | custom-call | flops 6899999744 | bytes 1048576 | tf_op jit(solution)/shard_map/qkv/pallas_call | solution.py:452
  87.8 8.3 %attn_fwd.2 = (bf16[512,384]{1,0:T(8,128)(2,1)S(1)}, f32[3,1,1024]{2,1,0:T(1,128)S(1)}) custom-call(s32[8]{0:T(128)S(1)} %compare_select_fusion.ends, bf16[1024,384]{1,0:T(8,128)(2,1)S(1)} %get-tuple-element.157.q_ref, bf16[2048,384]{1,0:T(8,128)(2,1)S(1)} %get-tuple-element.158.k_ref, bf16[2048,384]{1,0:T(8,128)(2,1)S(1)} %copy-done.32), custom_call_target="tpu_custom_call" | custom-call | flops 11500000256 | bytes 1048576 | tf_op jit(solution)/shard_map/attn_fwd/pallas_call | solution.py:332
  101.5 11.9 %attn_fwd.3 = (bf16[512,384]{1,0:T(8,128)(2,1)S(1)}, f32[3,1,1024]{2,1,0:T(1,128)S(1)}) custom-call(s32[8]{0:T(128)S(1)} %compare_select_fusion.ends, bf16[1024,384]{1,0:T(8,128)(2,1)S(1)} %get-tuple-element.157.q_ref, bf16[2048,384]{1,0:T(8,128)(2,1)S(1)} %get-tuple-element.158.k_ref, bf16[2048,384]{1,0:T(8,128)(2,1)S(1)} %copy-done.32), custom_call_target="tpu_custom_call" | custom-call | flops 11500000256 | bytes 1048576 | tf_op jit(solution)/shard_map/attn_fwd/pallas_call | solution.py:332
  113.6 9.2 %collective-permute-done.20 = bf16[2,2,1,96,1152]{4,3,2,1,0:T(8,128)(2,1)S(1)} collective-permute-done((bf16[2,2,1,96,1152]{4,3,2,1,0:T(8,128)(2,1)S(1)}, bf16[2,2,1,96,1152]{4,3,2,1,0:T(8,128)(2,1)S(1)}, u32[]{:S(2)}, u32[]{:S(2)}) %collective-permute-start.20) | collective-permute-done | bytes 884768 | tf_op jit(solution)/shard_map/ppermute | solution.py:44
  124.9 3.5 attn_out.1
  133.8 5.0 %first_norm.1 = (f32[1024,768]{1,0:T(8,128)}, f32[1024,128]{1,0:T(8,128)S(1)}, bf16[1024,768]{1,0:T(8,128)(2,1)S(1)}, bf16[768,1024]{1,0:T(8,128)(2,1)S(1)}) custom-call(bf16[1024,768]{1,0:T(8,128)(2,1)S(1)} %broadcast_select_fusion.x_ref, bf16[1024,768]{1,0:T(8,128)(2,1)} %copy-done.9, bf16[1024,768]{1,0:T(8,128)(2,1)} %copy-done.55, ...), custom_call_target="tpu_custom_call" | custom-call | flops 3449999872 | bytes 1048576 | tf_op jit(solution)/shard_map/first_norm/pallas_call | solution.py:558
  138.9 9.4 %ffn_in.1 = (bf16[1024,1536]{1,0:T(8,128)(2,1)}, bf16[1024,1536]{1,0:T(8,128)(2,1)}) custom-call(bf16[1024,768]{1,0:T(8,128)(2,1)S(1)} %get-tuple-element.174.x_ref, bf16[768,1152]{1,0:T(8,128)(2,1)S(1)} %bitcast.105, bf16[768,1152]{1,0:T(8,128)(2,1)S(1)} %bitcast.103), custom_call_target="tpu_custom_call" | custom-call | flops 11500000256 | bytes 1048576 | tf_op jit(solution)/shard_map/ffn_in/pallas_call | solution.py:610
  148.8 5.9 %ffn_out.1.mine_ref = bf16[1024,768]{1,0:T(8,128)(2,1)} custom-call(bf16[1024,1536]{1,0:T(8,128)(2,1)} %get-tuple-element.175.act_ref, bf16[768,768]{1,0:T(8,128)(2,1)S(1)} %bitcast.109, bf16[768,768]{1,0:T(8,128)(2,1)S(1)} %bitcast.107), custom_call_target="tpu_custom_call" | custom-call | flops 3449999872 | bytes 1048576 | tf_op jit(solution)/shard_map/ffn_out/pallas_call | solution.py:636
  155.1 3.4 collective-permute-done.24.got_ref
  158.5 8.6 %middle.1 = (f32[1024,128]{1,0:T(8,128)S(1)}, f32[1024,768]{1,0:T(8,128)}, bf16[1024,768]{1,0:T(8,128)(2,1)S(1)}, bf16[768,1024]{1,0:T(8,128)(2,1)S(1)}, f32[768,128]{1,0:T(8,128)S(1)}, /*index=5*/f32[8,768]{1,0:T(8,128)S(1)}) custom-call(f32[1024,768]{1,0:T(8,128)} %get-tuple-element.173.normed_ref, bf16[1024,768]{1,0:T(8,128)(2,1)} %ffn_out.1.mine_ref, ...), custom_call_target="tpu_custom_call" | custom-call | flops 5750000128 | bytes 1048576 | tf_op jit(solution)/shard_map/middle/pallas_call | solution.py:684
  170.8 11.3 %back_outer.1 = (bf16[768,768]{1,0:T(8,128)(2,1)S(1)}, bf16[768,768]{1,0:T(8,128)(2,1)S(1)}, bf16[1024,1536]{1,0:T(8,128)(2,1)}) custom-call(bf16[1024,768]{1,0:T(8,128)(2,1)} %copy-done.25, bf16[768,1024]{1,0:T(8,128)(2,1)} %copy-done.26, bf16[1024,1536]{1,0:T(8,128)(2,1)} %get-tuple-element.175.act_ref, bf16[1024,1536]{1,0:T(8,128)(2,1)} %get-tuple-element.183.slope_ref, ...), custom_call_target="tpu_custom_call" | custom-call | flops 10350000128 | bytes 1048576 | tf_op jit(solution)/shard_map/back_outer/pallas_call | solution.py:739
  182.1 11.0 %back_inner.1 = (bf16[768,768]{1,0:T(8,128)(2,1)S(1)}, bf16[768,768]{1,0:T(8,128)(2,1)S(1)}, bf16[1024,768]{1,0:T(8,128)(2,1)}) custom-call(bf16[768,1024]{1,0:T(8,128)(2,1)S(1)} %copy-done.16, bf16[1024,1536]{1,0:T(8,128)(2,1)} %get-tuple-element.187.gpre_ref, bf16[768,1152]{1,0:T(8,128)(2,1)} %bitcast.106, bf16[768,1152]{1,0:T(8,128)(2,1)} %bitcast.102), custom_call_target="tpu_custom_call" | custom-call | flops 10350000128 | bytes 1048576 | tf_op jit(solution)/shard_map/back_inner/pallas_call | solution.py:778
  198.4 11.1 %collective-permute-done.27 = bf16[1,2,2,96,768]{4,3,2,1,0:T(8,128)(2,1)} collective-permute-done((bf16[1,2,2,96,768]{4,3,2,1,0:T(8,128)(2,1)}, bf16[1,2,2,96,768]{4,3,2,1,0:T(8,128)(2,1)}, u32[]{:S(2)}, u32[]{:S(2)}) %collective-permute-start.27) | collective-permute-done | bytes 589856 | tf_op jit(solution)/shard_map/ppermute | solution.py:44
  215.4 8.0 %first_back.1 = (f32[1024,768]{1,0:T(8,128)}, bf16[1024,384]{1,0:T(8,128)(2,1)S(1)}, bf16[768,384]{1,0:T(8,128)(2,1)S(1)}, bf16[768,256]{1,0:T(8,128)(2,1)S(1)}) custom-call(bf16[1024,768]{1,0:T(8,128)(2,1)} %get-tuple-element.189.mine_ref, bf16[1024,768]{1,0:T(8,128)(2,1)} %collective-permute-done.25.got_ref, f32[1024,768]{1,0:T(8,128)} %get-tuple-element.194.gh2_ref, ...), custom_call_target="tpu_custom_call" | custom-call | flops 6899999744 | bytes 1048576 | tf_op jit(solution)/shard_map/first_back/pallas_call | solution.py:851
  223.4 4.9 %collective-permute-done.30 = bf16[1,2,1,96,768]{4,3,2,1,0:T(8,128)(2,1)S(1)} collective-permute-done((bf16[1,2,1,96,768]{4,3,2,1,0:T(8,128)(2,1)S(1)}, bf16[1,2,1,96,768]{4,3,2,1,0:T(8,128)(2,1)S(1)}, u32[]{:S(2)}, u32[]{:S(2)}) %collective-permute-start.30) | collective-permute-done | bytes 294944 | tf_op jit(solution)/shard_map/ppermute | solution.py:44
  231.6 3.0 collective-permute-start.63
  236.2 23.6 %attn_bwd.1 = (bf16[1024,384]{1,0:T(8,128)(2,1)S(1)}, bf16[2048,384]{1,0:T(8,128)(2,1)S(1)}, bf16[2048,384]{1,0:T(8,128)(2,1)}) custom-call(s32[8]{0:T(128)S(1)} %compare_select_fusion.ends, bf16[1024,384]{1,0:T(8,128)(2,1)S(1)} %copy-done.36, bf16[1024,384]{1,0:T(8,128)(2,1)S(1)} %get-tuple-element.199.do_ref, bf16[512,384]{1,0:T(8,128)(2,1)S(1)} %copy-done.28, ...), custom_call_target="tpu_custom_call" | custom-call | flops 28750000128 | bytes 1048576 | tf_op jit(solution)/shard_map/attn_bwd/pallas_call | solution.py:373
  270.1 4.7 %collective-permute-start.37 = (bf16[512,768]{1,0:T(8,128)(2,1)S(1)}, bf16[512,768]{1,0:T(8,128)(2,1)S(1)}, u32[]{:S(2)}, u32[]{:S(2)}) collective-permute-start(bf16[512,768]{1,0:T(8,128)(2,1)S(1)} %add_convert_fusion.1), channel_id=1, source_target_pairs={{0,4},{4,0},{1,5},{5,1},{2,6},{6,2},{3,7},{7,3},{8,12},{12,8},{9,1... | collective-permute-start | bytes 2359304 | tf_op jit(solution)/shard_map/ppermute | solution.py:44
  274.8 11.3 %head_grads.1 = (bf16[1024,768]{1,0:T(8,128)(2,1)}, bf16[768,768]{1,0:T(8,128)(2,1)S(1)}, bf16[768,768]{1,0:T(8,128)(2,1)S(1)}) custom-call(bf16[2048,768]{1,0:T(8,128)(2,1)} %pad_maximum_fusion.x_ref, bf16[1024,384]{1,0:T(8,128)(2,1)S(1)} %get-tuple-element.219.dq, bf16[2048,384]{1,0:T(8,128)(2,1)} %copy-done.13, bf16[2048,384]{1,0:T(8,128)(2,1)} %get-tuple-element.210.dv, ...), custom_call_target="tpu_custom_call" | custom-call | flops 10350000128 | bytes 1048576 | tf_op jit(solution)/shard_map/head_grads/pallas_call | solution.py:949
  290.4 3.2 collective-permute-done.46
  295.0 4.2 %collective-permute-start.42 = (bf16[1,1,96,768]{3,2,1,0:T(8,128)(2,1)S(1)}, bf16[1,1,96,768]{3,2,1,0:T(8,128)(2,1)S(1)}, u32[]{:S(2)}, u32[]{:S(2)}) collective-permute-start(bf16[1,1,96,768]{3,2,1,0:T(8,128)(2,1)S(1)} %get-tuple-element.333), channel_id=1, source_target_pairs={{0,0},{1,1},{2,8},{3,9},{4,4},{5,5},{6,12},{7,13},{8,2},{9,3},{10,... | collective-permute-start | bytes 442376 | tf_op jit(solution)/shard_map/ppermute | solution.py:60
  301.4 6.8 %collective-permute-start.38 = (f32[256,128]{1,0:T(8,128)S(1)}, f32[256,128]{1,0:T(8,128)S(1)}, u32[]{:S(2)}, u32[]{:S(2)}) collective-permute-start(f32[256,128]{1,0:T(8,128)S(1)} %get-tuple-element.339), channel_id=1, source_target_pairs={{0,0},{1,8},{2,1},{3,9},{4,4},{5,12},{6,5},{7,13},{8,2},{9,10},{10... | collective-permute-start | bytes 393224 | tf_op jit(solution)/shard_map/ppermute | solution.py:60
  317.5 3.7 collective-permute-done.59
  331.3 3.4 collective-permute-start.54
  344.7 13.8 %collective-permute-done.54 = bf16[1,1,96,768]{3,2,1,0:T(8,128)(2,1)S(1)} collective-permute-done((bf16[1,1,96,768]{3,2,1,0:T(8,128)(2,1)S(1)}, bf16[1,1,96,768]{3,2,1,0:T(8,128)(2,1)S(1)}, u32[]{:S(2)}, u32[]{:S(2)}) %collective-permute-start.54) | collective-permute-done | bytes 147488 | tf_op jit(solution)/shard_map/ppermute | solution.py:60
  358.6 4.0 %collective-permute-done.57 = bf16[1,1,96,768]{3,2,1,0:T(8,128)(2,1)S(1)} collective-permute-done((bf16[1,1,96,768]{3,2,1,0:T(8,128)(2,1)S(1)}, bf16[1,1,96,768]{3,2,1,0:T(8,128)(2,1)S(1)}, u32[]{:S(2)}, u32[]{:S(2)}) %collective-permute-start.57) | collective-permute-done | bytes 147488 | tf_op jit(solution)/shard_map/ppermute | solution.py:60
  (337 shorter events, 126.1 us)
Async XLA Ops:
  7.2 63.4 %all-gather.3.cloned.1.call-start = ((), (), s32[]{:S(2)}) async-start(), calls=%async_computation | async-start | bytes 1843200 | tf_op jit(solution)/shard_map/all_gather | solution.py:1018
  12.8 29.6 %collective-permute-start.7 = (bf16[1024,768]{1,0:T(8,128)(2,1)}, bf16[1024,768]{1,0:T(8,128)(2,1)}, u32[]{:S(2)}, u32[]{:S(2)}) collective-permute-start(bf16[1024,768]{1,0:T(8,128)(2,1)} %dynamic-slice_bitcast_fusion), channel_id=1, source_target_pairs={{0,8},{8,0},{16,24},{24,16},{1,9},{9,1},{17,25},{25,17},{2,10},{10... | collective-permute-start | bytes 4718600 | tf_op jit(solution)/shard_map/ppermute | solution.py:44
  21.3 21.1 %collective-permute-start.6 = (bf16[800,768]{1,0:T(8,128)(2,1)}, bf16[800,768]{1,0:T(8,128)(2,1)S(1)}, u32[]{:S(2)}, u32[]{:S(2)}) collective-permute-start(bf16[800,768]{1,0:T(8,128)(2,1)} %dynamic-slice_bitcast_fusion.1), channel_id=1, source_target_pairs={{0,4},{2,6},{4,0},{6,2},{9,13},{11,15},{13,9},{15,11},{16,20},{18,... | collective-permute-start | bytes 3686408 | tf_op jit(solution)/shard_map/ppermute | solution.py:60
  87.3 26.1 %collective-permute-start.18 = (bf16[1,2,1,96,768]{4,3,2,1,0:T(8,128)(2,1)S(1)}, bf16[1,2,1,96,768]{4,3,2,1,0:T(8,128)(2,1)S(1)}, u32[]{:S(2)}, u32[]{:S(2)}) collective-permute-start(bf16[1,2,1,96,768]{4,3,2,1,0:T(8,128)(2,1)S(1)} %pad_maximum_fusion.14), channel_id=1, source_target_pairs={{0,16},{8,24},{16,0},{24,8},{1,17},{9,25},{17,1},{25,9},{2,18},{10... | collective-permute-start | bytes 884744 | tf_op jit(solution)/shard_map/ppermute | solution.py:44
  87.6 25.9 %collective-permute-start.17 = (bf16[1,2,1,96,768]{4,3,2,1,0:T(8,128)(2,1)S(1)}, bf16[1,2,1,96,768]{4,3,2,1,0:T(8,128)(2,1)S(1)}, u32[]{:S(2)}, u32[]{:S(2)}) collective-permute-start(bf16[1,2,1,96,768]{4,3,2,1,0:T(8,128)(2,1)S(1)} %pad_maximum_fusion.15), channel_id=1, source_target_pairs={{0,4},{4,0},{1,5},{5,1},{2,6},{6,2},{3,7},{7,3},{8,12},{12,8},{9,1... | collective-permute-start | bytes 884744 | tf_op jit(solution)/shard_map/ppermute | solution.py:44
  97.9 25.0 %collective-permute-start.20 = (bf16[2,2,1,96,1152]{4,3,2,1,0:T(8,128)(2,1)S(1)}, bf16[2,2,1,96,1152]{4,3,2,1,0:T(8,128)(2,1)S(1)}, u32[]{:S(2)}, u32[]{:S(2)}) collective-permute-start(bf16[2,2,1,96,1152]{4,3,2,1,0:T(8,128)(2,1)S(1)} %pad_maximum_fusion.9), channel_id=1, source_target_pairs={{0,4},{4,0},{1,5},{5,1},{2,6},{6,2},{3,7},{7,3},{8,12},{12,8},{9,1... | collective-permute-start | bytes 2654216 | tf_op jit(solution)/shard_map/ppermute | solution.py:44
  100.2 22.6 %collective-permute-start.19 = (bf16[1,2,2,96,1152]{4,3,2,1,0:T(8,128)(2,1)S(1)}, bf16[1,2,2,96,1152]{4,3,2,1,0:T(8,128)(2,1)S(1)}, u32[]{:S(2)}, u32[]{:S(2)}) collective-permute-start(bf16[1,2,2,96,1152]{4,3,2,1,0:T(8,128)(2,1)S(1)} %pad_maximum_fusion.8), channel_id=1, source_target_pairs={{0,16},{8,24},{16,0},{24,8},{1,17},{9,25},{17,1},{25,9},{2,18},{10... | collective-permute-start | bytes 2654216 | tf_op jit(solution)/shard_map/ppermute | solution.py:44
  129.6 18.7 %collective-permute-start.22 = (bf16[1,2,2,96,768]{4,3,2,1,0:T(8,128)(2,1)S(1)}, bf16[1,2,2,96,768]{4,3,2,1,0:T(8,128)(2,1)S(1)}, u32[]{:S(2)}, u32[]{:S(2)}) collective-permute-start(bf16[1,2,2,96,768]{4,3,2,1,0:T(8,128)(2,1)S(1)} %pad_maximum_fusion.10), channel_id=1, source_target_pairs={{0,16},{8,24},{16,0},{24,8},{1,17},{9,25},{17,1},{25,9},{2,18},{10... | collective-permute-start | bytes 1769480 | tf_op jit(solution)/shard_map/ppermute | solution.py:44
  130.1 18.2 %collective-permute-start.23 = (bf16[2,2,1,96,768]{4,3,2,1,0:T(8,128)(2,1)S(1)}, bf16[2,2,1,96,768]{4,3,2,1,0:T(8,128)(2,1)S(1)}, u32[]{:S(2)}, u32[]{:S(2)}) collective-permute-start(bf16[2,2,1,96,768]{4,3,2,1,0:T(8,128)(2,1)S(1)} %pad_maximum_fusion.11), channel_id=1, source_target_pairs={{0,4},{4,0},{1,5},{5,1},{2,6},{6,2},{3,7},{7,3},{8,12},{12,8},{9,1... | collective-permute-start | bytes 1769480 | tf_op jit(solution)/shard_map/ppermute | solution.py:44
  193.2 22.2 %collective-permute-start.25 = (bf16[1024,768]{1,0:T(8,128)(2,1)}, bf16[1024,768]{1,0:T(8,128)(2,1)}, u32[]{:S(2)}, u32[]{:S(2)}) collective-permute-start(bf16[1024,768]{1,0:T(8,128)(2,1)} %get-tuple-element.189.mine_ref), channel_id=1, source_target_pairs={{0,8},{8,0},{16,24},{24,16},{1,9},{9,1},{17,25},{25,17},{2,10},{10... | collective-permute-start | bytes 4718600 | tf_op jit(solution)/shard_map/ppermute | solution.py:44
  194.4 15.1 %collective-permute-start.27 = (bf16[1,2,2,96,768]{4,3,2,1,0:T(8,128)(2,1)}, bf16[1,2,2,96,768]{4,3,2,1,0:T(8,128)(2,1)}, u32[]{:S(2)}, u32[]{:S(2)}) collective-permute-start(bf16[1,2,2,96,768]{4,3,2,1,0:T(8,128)(2,1)} %constant_dynamic-slice_fusion.15), channel_id=1, source_target_pairs={{0,16},{8,24},{16,0},{24,8},{1,17},{9,25},{17,1},{25,9},{2,18},{10... | collective-permute-start | bytes 1769480 | tf_op jit(solution)/shard_map/ppermute | solution.py:44
  196.8 33.4 %collective-permute-start.29 = (bf16[1,2,2,96,768]{4,3,2,1,0:T(8,128)(2,1)S(1)}, bf16[1,2,2,96,768]{4,3,2,1,0:T(8,128)(2,1)S(1)}, u32[]{:S(2)}, u32[]{:S(2)}) collective-permute-start(bf16[1,2,2,96,768]{4,3,2,1,0:T(8,128)(2,1)S(1)} %constant_dynamic-slice_fusion.13), channel_id=1, source_target_pairs={{0,16},{8,24},{16,0},{24,8},{1,17},{9,25},{17,1},{25,9},{2,18},{10... | collective-permute-start | bytes 1769480 | tf_op jit(solution)/shard_map/ppermute | solution.py:44
  198.1 32.1 %collective-permute-start.28 = (bf16[2,2,1,96,768]{4,3,2,1,0:T(8,128)(2,1)S(1)}, bf16[2,2,1,96,768]{4,3,2,1,0:T(8,128)(2,1)S(1)}, u32[]{:S(2)}, u32[]{:S(2)}) collective-permute-start(bf16[2,2,1,96,768]{4,3,2,1,0:T(8,128)(2,1)S(1)} %constant_dynamic-slice_fusion.14), channel_id=1, source_target_pairs={{0,4},{4,0},{1,5},{5,1},{2,6},{6,2},{3,7},{7,3},{8,12},{12,8},{9,1... | collective-permute-start | bytes 1769480 | tf_op jit(solution)/shard_map/ppermute | solution.py:44
  211.6 16.7 %collective-permute-start.30 = (bf16[1,2,1,96,768]{4,3,2,1,0:T(8,128)(2,1)S(1)}, bf16[1,2,1,96,768]{4,3,2,1,0:T(8,128)(2,1)S(1)}, u32[]{:S(2)}, u32[]{:S(2)}) collective-permute-start(bf16[1,2,1,96,768]{4,3,2,1,0:T(8,128)(2,1)S(1)} %constant_dynamic-slice_fusion.12), channel_id=1, source_target_pairs={{0,16},{8,24},{16,0},{24,8},{1,17},{9,25},{17,1},{25,9},{2,18},{10... | collective-permute-start | bytes 884744 | tf_op jit(solution)/shard_map/ppermute | solution.py:44
  214.1 15.0 %collective-permute-start.31 = (bf16[1,2,1,96,768]{4,3,2,1,0:T(8,128)(2,1)S(1)}, bf16[1,2,1,96,768]{4,3,2,1,0:T(8,128)(2,1)S(1)}, u32[]{:S(2)}, u32[]{:S(2)}) collective-permute-start(bf16[1,2,1,96,768]{4,3,2,1,0:T(8,128)(2,1)S(1)} %constant_dynamic-slice_fusion.11), channel_id=1, source_target_pairs={{0,4},{4,0},{1,5},{5,1},{2,6},{6,2},{3,7},{7,3},{8,12},{12,8},{9,1... | collective-permute-start | bytes 884744 | tf_op jit(solution)/shard_map/ppermute | solution.py:44
  230.6 56.7 %collective-permute-start.62 = (bf16[1,1,96,768]{3,2,1,0:T(8,128)(2,1)}, bf16[1,1,96,768]{3,2,1,0:T(8,128)(2,1)S(1)}, u32[]{:S(2)}, u32[]{:S(2)}) collective-permute-start(bf16[1,1,96,768]{3,2,1,0:T(8,128)(2,1)} %get-tuple-element.323), channel_id=1, source_target_pairs={{0,8},{1,9},{2,0},{3,1},{4,12},{5,13},{6,4},{7,5},{8,10},{9,11},{1... | collective-permute-start | bytes 442376 | tf_op jit(solution)/shard_map/ppermute | solution.py:60
  231.6 56.1 %collective-permute-start.63 = (bf16[1,1,96,768]{3,2,1,0:T(8,128)(2,1)}, bf16[1,1,96,768]{3,2,1,0:T(8,128)(2,1)S(1)}, u32[]{:S(2)}, u32[]{:S(2)}) collective-permute-start(bf16[1,1,96,768]{3,2,1,0:T(8,128)(2,1)} %get-tuple-element.322), channel_id=1, source_target_pairs={{0,9},{1,8},{2,1},{3,0},{4,13},{5,12},{6,5},{7,4},{8,11},{9,10},{1... | collective-permute-start | bytes 442376 | tf_op jit(solution)/shard_map/ppermute | solution.py:60
  234.6 32.9 %collective-permute-start.33 = (bf16[1,2,1,96,768]{4,3,2,1,0:T(8,128)(2,1)S(1)}, bf16[1,2,1,96,768]{4,3,2,1,0:T(8,128)(2,1)S(1)}, u32[]{:S(2)}, u32[]{:S(2)}) collective-permute-start(bf16[1,2,1,96,768]{4,3,2,1,0:T(8,128)(2,1)S(1)} %constant_dynamic-slice_fusion.8), channel_id=1, source_target_pairs={{0,16},{8,24},{16,0},{24,8},{1,17},{9,25},{17,1},{25,9},{2,18},{10... | collective-permute-start | bytes 884744 | tf_op jit(solution)/shard_map/ppermute | solution.py:44
  234.6 30.2 %collective-permute-start.35 = (bf16[1,1,2,96,256]{4,3,2,1,0:T(8,128)(2,1)S(1)}, bf16[1,1,2,96,256]{4,3,2,1,0:T(8,128)(2,1)S(1)}, u32[]{:S(2)}, u32[]{:S(2)}) collective-permute-start(bf16[1,1,2,96,256]{4,3,2,1,0:T(8,128)(2,1)S(1)} %constant_dynamic-slice_fusion.6), channel_id=1, source_target_pairs={{0,16},{8,24},{16,0},{24,8},{1,17},{9,25},{17,1},{25,9},{2,18},{10... | collective-permute-start | bytes 294920 | tf_op jit(solution)/shard_map/ppermute | solution.py:44
  236.1 31.4 %collective-permute-start.34 = (bf16[1,2,1,96,768]{4,3,2,1,0:T(8,128)(2,1)S(1)}, bf16[1,2,1,96,768]{4,3,2,1,0:T(8,128)(2,1)S(1)}, u32[]{:S(2)}, u32[]{:S(2)}) collective-permute-start(bf16[1,2,1,96,768]{4,3,2,1,0:T(8,128)(2,1)S(1)} %constant_dynamic-slice_fusion.7), channel_id=1, source_target_pairs={{0,4},{4,0},{1,5},{5,1},{2,6},{6,2},{3,7},{7,3},{8,12},{12,8},{9,1... | collective-permute-start | bytes 884744 | tf_op jit(solution)/shard_map/ppermute | solution.py:44
  264.8 23.0 %collective-permute-start.60 = (bf16[1,1,96,768]{3,2,1,0:T(8,128)(2,1)S(1)}, bf16[1,1,96,768]{3,2,1,0:T(8,128)(2,1)S(1)}, u32[]{:S(2)}, u32[]{:S(2)}) collective-permute-start(bf16[1,1,96,768]{3,2,1,0:T(8,128)(2,1)S(1)} %get-tuple-element.325), channel_id=1, source_target_pairs={{0,0},{1,1},{2,8},{3,9},{4,4},{5,5},{6,12},{7,13},{8,2},{9,3},{10,... | collective-permute-start | bytes 442376 | tf_op jit(solution)/shard_map/ppermute | solution.py:60
  267.5 20.4 %collective-permute-start.61 = (bf16[1,1,96,768]{3,2,1,0:T(8,128)(2,1)S(1)}, bf16[1,1,96,768]{3,2,1,0:T(8,128)(2,1)S(1)}, u32[]{:S(2)}, u32[]{:S(2)}) collective-permute-start(bf16[1,1,96,768]{3,2,1,0:T(8,128)(2,1)S(1)} %get-tuple-element.324), channel_id=1, source_target_pairs={{0,1},{1,0},{2,9},{3,8},{4,5},{5,4},{6,13},{7,12},{8,3},{9,2},{10,... | collective-permute-start | bytes 442376 | tf_op jit(solution)/shard_map/ppermute | solution.py:60
  270.1 24.9 %collective-permute-start.37 = (bf16[512,768]{1,0:T(8,128)(2,1)S(1)}, bf16[512,768]{1,0:T(8,128)(2,1)S(1)}, u32[]{:S(2)}, u32[]{:S(2)}) collective-permute-start(bf16[512,768]{1,0:T(8,128)(2,1)S(1)} %add_convert_fusion.1), channel_id=1, source_target_pairs={{0,4},{4,0},{1,5},{5,1},{2,6},{6,2},{3,7},{7,3},{8,12},{12,8},{9,1... | collective-permute-start | bytes 2359304 | tf_op jit(solution)/shard_map/ppermute | solution.py:44
  287.9 23.1 %collective-permute-start.40 = (bf16[1,2,2,96,768]{4,3,2,1,0:T(8,128)(2,1)S(1)}, bf16[1,2,2,96,768]{4,3,2,1,0:T(8,128)(2,1)S(1)}, u32[]{:S(2)}, u32[]{:S(2)}) collective-permute-start(bf16[1,2,2,96,768]{4,3,2,1,0:T(8,128)(2,1)S(1)} %constant_dynamic-slice_fusion.4), channel_id=1, source_target_pairs={{0,16},{8,24},{16,0},{24,8},{1,17},{9,25},{17,1},{25,9},{2,18},{10... | collective-permute-start | bytes 1769480 | tf_op jit(solution)/shard_map/ppermute | solution.py:44
  289.5 23.6 %collective-permute-start.41 = (bf16[2,2,1,96,768]{4,3,2,1,0:T(8,128)(2,1)S(1)}, bf16[2,2,1,96,768]{4,3,2,1,0:T(8,128)(2,1)S(1)}, u32[]{:S(2)}, u32[]{:S(2)}) collective-permute-start(bf16[2,2,1,96,768]{4,3,2,1,0:T(8,128)(2,1)S(1)} %constant_dynamic-slice_fusion.3), channel_id=1, source_target_pairs={{0,4},{4,0},{1,5},{5,1},{2,6},{6,2},{3,7},{7,3},{8,12},{12,8},{9,1... | collective-permute-start | bytes 1769480 | tf_op jit(solution)/shard_map/ppermute | solution.py:44
  295.0 15.9 %collective-permute-start.42 = (bf16[1,1,96,768]{3,2,1,0:T(8,128)(2,1)S(1)}, bf16[1,1,96,768]{3,2,1,0:T(8,128)(2,1)S(1)}, u32[]{:S(2)}, u32[]{:S(2)}) collective-permute-start(bf16[1,1,96,768]{3,2,1,0:T(8,128)(2,1)S(1)} %get-tuple-element.333), channel_id=1, source_target_pairs={{0,0},{1,1},{2,8},{3,9},{4,4},{5,5},{6,12},{7,13},{8,2},{9,3},{10,... | collective-permute-start | bytes 442376 | tf_op jit(solution)/shard_map/ppermute | solution.py:60
  301.4 24.5 %collective-permute-start.38 = (f32[256,128]{1,0:T(8,128)S(1)}, f32[256,128]{1,0:T(8,128)S(1)}, u32[]{:S(2)}, u32[]{:S(2)}) collective-permute-start(f32[256,128]{1,0:T(8,128)S(1)} %get-tuple-element.339), channel_id=1, source_target_pairs={{0,0},{1,8},{2,1},{3,9},{4,4},{5,12},{6,5},{7,13},{8,2},{9,10},{10... | collective-permute-start | bytes 393224 | tf_op jit(solution)/shard_map/ppermute | solution.py:60
  311.0 15.0 %collective-permute-start.39 = (f32[256,128]{1,0:T(8,128)S(1)}, f32[256,128]{1,0:T(8,128)S(1)}, u32[]{:S(2)}, u32[]{:S(2)}) collective-permute-start(f32[256,128]{1,0:T(8,128)S(1)} %get-tuple-element.338), channel_id=1, source_target_pairs={{0,1},{1,9},{2,0},{3,8},{4,5},{5,13},{6,4},{7,12},{8,3},{9,11},{10... | collective-permute-start | bytes 393224 | tf_op jit(solution)/shard_map/ppermute | solution.py:60
  331.3 27.3 %collective-permute-start.54 = (bf16[1,1,96,768]{3,2,1,0:T(8,128)(2,1)S(1)}, bf16[1,1,96,768]{3,2,1,0:T(8,128)(2,1)S(1)}, u32[]{:S(2)}, u32[]{:S(2)}) collective-permute-start(bf16[1,1,96,768]{3,2,1,0:T(8,128)(2,1)S(1)} %get-tuple-element.326), channel_id=1, source_target_pairs={{0,0},{1,1},{2,8},{3,9},{4,4},{5,5},{6,12},{7,13},{8,2},{9,3},{10,... | collective-permute-start | bytes 442376 | tf_op jit(solution)/shard_map/ppermute | solution.py:60
  334.8 23.8 %collective-permute-start.56 = (bf16[1,1,96,768]{3,2,1,0:T(8,128)(2,1)S(1)}, bf16[1,1,96,768]{3,2,1,0:T(8,128)(2,1)S(1)}, u32[]{:S(2)}, u32[]{:S(2)}) collective-permute-start(bf16[1,1,96,768]{3,2,1,0:T(8,128)(2,1)S(1)} %get-tuple-element.327), channel_id=1, source_target_pairs={{0,8},{1,9},{2,0},{3,1},{4,12},{5,13},{6,4},{7,5},{8,10},{9,11},{1... | collective-permute-start | bytes 442376 | tf_op jit(solution)/shard_map/ppermute | solution.py:60
  335.8 22.7 %collective-permute-start.55 = (bf16[1,1,96,768]{3,2,1,0:T(8,128)(2,1)S(1)}, bf16[1,1,96,768]{3,2,1,0:T(8,128)(2,1)S(1)}, u32[]{:S(2)}, u32[]{:S(2)}) collective-permute-start(bf16[1,1,96,768]{3,2,1,0:T(8,128)(2,1)S(1)} %get-tuple-element.328), channel_id=1, source_target_pairs={{0,1},{1,0},{2,9},{3,8},{4,5},{5,4},{6,13},{7,12},{8,3},{9,2},{10,... | collective-permute-start | bytes 442376 | tf_op jit(solution)/shard_map/ppermute | solution.py:60
  340.8 21.7 %collective-permute-start.57 = (bf16[1,1,96,768]{3,2,1,0:T(8,128)(2,1)S(1)}, bf16[1,1,96,768]{3,2,1,0:T(8,128)(2,1)S(1)}, u32[]{:S(2)}, u32[]{:S(2)}) collective-permute-start(bf16[1,1,96,768]{3,2,1,0:T(8,128)(2,1)S(1)} %get-tuple-element.329), channel_id=1, source_target_pairs={{0,9},{1,8},{2,1},{3,0},{4,13},{5,12},{6,5},{7,4},{8,11},{9,10},{1... | collective-permute-start | bytes 442376 | tf_op jit(solution)/shard_map/ppermute | solution.py:60
  (91 other events, 755.8 us)
Sparse Core Ops, SparseCore 0:
  36.5 33.9 all-gather.2

commit v3 on v2

--- a/solution.py
+++ b/solution.py
@@ -12,7 +12,7 @@
 SEG_MOST = 800
 BQ = 256
 BK = 256
-VMEM_MIB = 48
+VMEM_MIB = 34
 
 eps_norm = 1e-12
 eps_unit = 1e-06
@@ -68,7 +68,7 @@
     bits = shard_bits()
     if name == "x":
         return [("ctx", 1, bits)]
-    return [("shard", 1 << i, bits - 1 - i) for i in range(1, bits)]
+    return [("shard", 1 << i, bits - 1 - i) for i in range(bits - 1, 0, -1)]
 
 
 def my_bit(axis, bit):
@@ -124,19 +124,28 @@
     return full.reshape(full.shape[:-2] + (2,) * (shard_bits() + 1) + (rows, full.shape[-1]))
 
 
-def scatter_start(cur, name):
+def scatter_start(cur, name, lead=0):
     axis, bit, dim = steps_of(name)[0]
-    return swap(lax.dynamic_slice_in_dim(cur, 1 - my_bit(axis, bit), 1, dim), axis, bit)
-
-
-def scatter_finish(cur, other, name):
+    return swap(lax.dynamic_slice_in_dim(cur, 1 - my_bit(axis, bit), 1, dim + lead), axis, bit)
+
+
+def scatter_finish(cur, other, name, lead=0):
     first, *rest = steps_of(name)
-    kept = lax.dynamic_slice_in_dim(cur, my_bit(*first[:2]), 1, first[2])
+    kept = lax.dynamic_slice_in_dim(cur, my_bit(*first[:2]), 1, first[2] + lead)
     cur = (kept.astype(jnp.float32) + other.astype(jnp.float32)).astype(jnp.bfloat16)
     for axis, bit, dim in rest:
         mine = my_bit(axis, bit)
-        other = swap(lax.dynamic_slice_in_dim(cur, 1 - mine, 1, dim), axis, bit)
-        kept = lax.dynamic_slice_in_dim(cur, mine, 1, dim)
+        other = swap(lax.dynamic_slice_in_dim(cur, 1 - mine, 1, dim + lead), axis, bit)
+        kept = lax.dynamic_slice_in_dim(cur, mine, 1, dim + lead)
+        cur = (kept.astype(jnp.float32) + other.astype(jnp.float32)).astype(jnp.bfloat16)
+    return cur
+
+
+def scatter_rest(cur, name, lead=0):
+    for axis, bit, dim in steps_of(name)[1:]:
+        mine = my_bit(axis, bit)
+        other = swap(lax.dynamic_slice_in_dim(cur, 1 - mine, 1, dim + lead), axis, bit)
+        kept = lax.dynamic_slice_in_dim(cur, mine, 1, dim + lead)
         cur = (kept.astype(jnp.float32) + other.astype(jnp.float32)).astype(jnp.bfloat16)
     return cur
 
@@ -359,37 +368,36 @@
     )(ends, queries, keys, values)
 
 
-def attn_backward(ends, queries, grads, mixed, lse, keys, values):
-    rows, width = queries.shape
+def attn_backward(ends, start, pairs, queries, grads, mixed, lse, keys, values):
+    rows = queries.shape[0]
     span = keys.shape[0]
-    pairs = width // 128
     half = rows // BQ // 2
-    tile = pl.BlockSpec((BQ, width), lambda i, e: (i, 0))
-    low = pl.BlockSpec((BQ, width), lambda i, e: (jnp.minimum(i, half - 1), 0))
-    high = pl.BlockSpec((BQ, width), lambda i, e: (jnp.maximum(i - half, 0), 0))
-    low_line = pl.BlockSpec((pairs, 1, 2 * BQ), lambda i, e: (0, 0, jnp.minimum(i, half - 1)))
-    high_line = pl.BlockSpec((pairs, 1, 2 * BQ), lambda i, e: (0, 0, jnp.maximum(i - half, 0)))
-    every = pl.BlockSpec((span, width), lambda i, e: (0, 0))
+    width = 128 * pairs
+    col = start // pairs
+    tile = pl.BlockSpec((BQ, width), lambda i, e: (i, col))
+    low = pl.BlockSpec((BQ, width), lambda i, e: (jnp.minimum(i, half - 1), col))
+    high = pl.BlockSpec((BQ, width), lambda i, e: (jnp.maximum(i - half, 0), col))
+    low_line = pl.BlockSpec((pairs, 1, 2 * BQ), lambda i, e: (col, 0, jnp.minimum(i, half - 1)))
+    high_line = pl.BlockSpec((pairs, 1, 2 * BQ), lambda i, e: (col, 0, jnp.maximum(i - half, 0)))
+    every = pl.BlockSpec((span, width), lambda i, e: (0, col))
+    out = pl.BlockSpec((span, width), lambda i, e: (0, 0))
+    shape = jax.ShapeDtypeStruct((span, width), jnp.bfloat16)
     return pl.pallas_call(
         attn_bwd_kernel,
         grid_spec=pltpu.PrefetchScalarGridSpec(
             num_scalar_prefetch=1,
             grid=(rows // BQ,),
             in_specs=[tile, tile, low, high, low_line, high_line, every, every],
-            out_specs=[tile, every, every],
+            out_specs=[pl.BlockSpec((BQ, width), lambda i, e: (i, 0)), out, out],
             scratch_shapes=[
                 pltpu.VMEM((span, width), jnp.float32),
                 pltpu.VMEM((span, width), jnp.float32),
                 pltpu.VMEM((pairs, 128, 2 * BQ), jnp.float32),
             ],
         ),
-        out_shape=[
-            jax.ShapeDtypeStruct((rows, width), jnp.bfloat16),
-            jax.ShapeDtypeStruct((span, width), jnp.bfloat16),
-            jax.ShapeDtypeStruct((span, width), jnp.bfloat16),
-        ],
+        out_shape=[jax.ShapeDtypeStruct((rows, width), jnp.bfloat16), shape, shape],
         compiler_params=params(VMEM_MIB),
-        cost_estimate=cost(25e-6),
+        cost_estimate=cost(1e-6 * pairs),
         name="attn_bwd",
     )(ends, queries, grads, *mixed, *lse, keys, values)
 
@@ -422,24 +430,28 @@
     )(*parts)
 
 
-def qkv_kernel(x_ref, a_ref, b_ref, q_ref, k_ref, v_ref, wq_ref, wk_ref, wv_ref):
+def build_heads(outs, a_ref, b_ref):
+    for i, out in enumerate(outs):
+        lo = 384 + DH * i
+        out[:, :128] = a_ref[:, 128 * i : 128 * i + 128]
+        out[:, 128:256] = b_ref[:, 128 * i : 128 * i + 128]
+        out[:, 256:] = jnp.concatenate([a_ref[:, lo : lo + DH], b_ref[:, lo : lo + DH]], axis=1)
+
+
+def qkv_kernel(x_ref, a_ref, b_ref, q_ref, k_ref, v_ref, wq, wk, wv):
     step = pl.program_id(0)
 
     @pl.when(step == 0)
     def _():
-        for i, out in enumerate((wq_ref, wk_ref, wv_ref)):
-            lo = 384 + DH * i
-            out[:, :128] = a_ref[:, 128 * i : 128 * i + 128]
-            out[:, 128:256] = b_ref[:, 128 * i : 128 * i + 128]
-            out[:, 256:] = jnp.concatenate([a_ref[:, lo : lo + DH], b_ref[:, lo : lo + DH]], axis=1)
+        build_heads((wq, wk, wv), a_ref, b_ref)
 
     x = x_ref[...]
-    k_ref[...] = dot(x, wk_ref[...]).astype(k_ref.dtype)
-    v_ref[...] = dot(x, wv_ref[...]).astype(v_ref.dtype)
+    k_ref[...] = dot(x, wk[...]).astype(k_ref.dtype)
+    v_ref[...] = dot(x, wv[...]).astype(v_ref.dtype)
 
     @pl.when(step < pl.num_programs(0) // 2)
     def _():
-        q = dot(x, wq_ref[...]).astype(jnp.bfloat16).astype(jnp.float32)
+        q = dot(x, wq[...]).astype(jnp.bfloat16).astype(jnp.float32)
         q_ref[...] = (q * DH**-0.5).astype(q_ref.dtype)
 
 
@@ -457,14 +469,13 @@
             pl.BlockSpec((block, cols), lambda i: (jnp.minimum(i, steps // 2 - 1), 0)),
             rows_spec(block, cols),
             rows_spec(block, cols),
-        ]
-        + [full_spec((width, cols))] * 3,
+        ],
         out_shape=[
             jax.ShapeDtypeStruct((span // 2, cols), low),
             jax.ShapeDtypeStruct((span, cols), low),
             jax.ShapeDtypeStruct((span, cols), low),
-        ]
-        + [jax.ShapeDtypeStruct((width, cols), low)] * 3,
+        ],
+        scratch_shapes=[pltpu.VMEM((width, cols), low)] * 3,
         compiler_params=params(VMEM_MIB),
         cost_estimate=cost(6e-6),
         name="qkv",
@@ -493,7 +504,7 @@
     block = 256
     per = half // block
     low = jnp.bfloat16
-    third = pl.BlockSpec((width, 384), lambda i: (0, 2))
+    third = pl.BlockSpec((width, 384), lambda i: (0, w_a.shape[1] // 384 - 1))
     return pl.pallas_call(
         attn_out_kernel,
         grid=(2 * per,),
@@ -542,41 +553,6 @@
     return ref[...].astype(jnp.float32)
 
 
-def first_norm_kernel(x_ref, mine_ref, got_ref, norms, normed_ref, inv_ref, low_ref, turned_ref):
-    normed, inv = normalize(wide(x_ref) + (wide(mine_ref) + wide(got_ref)))
-    normed_ref[...] = normed
-    inv_ref[...] = jnp.broadcast_to(inv, inv_ref.shape)
-    low = (normed * norms[0:1, :] + norms[1:2, :]).astype(jnp.bfloat16)
-    low_ref[...] = low
-    turned_ref[...] = low.T
-
-
-def first_norm(tok, mine, got, norms):
-    rows, width = tok.shape
-    block = 256
-    tile = rows_spec(block, width)
-    return pl.pallas_call(
-        first_norm_kernel,
-        grid=(rows // block,),
-        in_specs=[tile, tile, tile, full_spec(norms.shape)],
-        out_specs=[
-            tile,
-            rows_spec(block, 128),
-            tile,
-            pl.BlockSpec((width, block), lambda i: (0, i)),
-        ],
-        out_shape=[
-            jax.ShapeDtypeStruct((rows, width), jnp.float32),
-            jax.ShapeDtypeStruct((rows, 128), jnp.float32),
-            jax.ShapeDtypeStruct((rows, width), jnp.bfloat16),
-            jax.ShapeDtypeStruct((width, rows), jnp.bfloat16),
-        ],
-        compiler_params=params(VMEM_MIB),
-        cost_estimate=cost(3e-6),
-        name="first_norm",
-    )(tok, mine, got, norms)
-
-
 def gelu_parts(v):
     e = jnp.exp(v * v * -0.5)
     t = 1.0 / (1.0 + (0.3275911 * 0.5**0.5) * jnp.abs(v))
@@ -588,39 +564,65 @@
     return v * cdf, cdf + v * e * 0.3989422804014327
 
 
-def ffn_in_kernel(x_ref, a_ref, b_ref, act_ref, slope_ref):
-    def work(w_ref):
-        for r in range(0, x_ref.shape[0], 256):
-            rows = slice(r, r + 256)
-            act, slope = gelu_parts(dot(x_ref[rows, :], w_ref[...]))
+def ffn_kernel(
+    x_ref, mine_ref, got_ref, norms, ia, ib, normed_ref, inv_ref, low_ref, act_ref, slope_ref
+):
+    step = pl.program_id(0)
+    steps = pl.num_programs(0)
+    parts = [slice(r, r + 256) for r in range(0, x_ref.shape[0], 256)]
+
+    @pl.when(step == 0)
+    def _():
+        for rows in parts:
+            hidden = x_ref[rows, :].astype(jnp.float32) + (
+                mine_ref[rows, :].astype(jnp.float32) + got_ref[rows, :].astype(jnp.float32)
+            )
+            normed, inv = normalize(hidden)
+            normed_ref[rows, :] = normed.astype(normed_ref.dtype)
+            inv_ref[rows, :] = jnp.broadcast_to(inv, (256, 128))
+            low_ref[rows, :] = (normed * norms[0:1, :] + norms[1:2, :]).astype(low_ref.dtype)
+
+    def work(i_ref):
+        for rows in parts:
+            act, slope = gelu_parts(dot(low_ref[rows, :], i_ref[...]))
             act_ref[rows, :] = act.astype(act_ref.dtype)
             slope_ref[rows, :] = slope.astype(slope_ref.dtype)
 
-    first = pl.program_id(0) < pl.num_programs(0) // 2
-    pl.when(first)(lambda: work(a_ref))
-    pl.when(jnp.logical_not(first))(lambda: work(b_ref))
-
-
-def ffn_in(x, w_a, w_b, hidden):
-    rows, width = x.shape
-    cols = 384
+    first = step < steps // 2
+    pl.when(first)(lambda: work(ia))
+    pl.when(jnp.logical_not(first))(lambda: work(ib))
+
+
+def slice_specs(width, cols, per):
+    return [
+        pl.BlockSpec((width, cols), lambda i: (0, jnp.minimum(i, per - 1))),
+        pl.BlockSpec((width, cols), lambda i: (0, jnp.maximum(i - per, 0))),
+    ]
+
+
+FFN_COLS = 256
+GROUPS = 1
+
+
+def feed_forward(tok, mine, got, norms, inner, hidden):
+    rows, width = tok.shape
+    cols = FFN_COLS
     per = hidden // cols
-    out = pl.BlockSpec((rows, cols), lambda i: (0, i))
-    shape = jax.ShapeDtypeStruct((rows, 2 * hidden), jnp.bfloat16)
+    tile = full_spec((rows, width))
+    chunk = pl.BlockSpec((rows, cols), lambda i: (0, i))
+    low = jax.ShapeDtypeStruct((rows, width), jnp.bfloat16)
+    units = jax.ShapeDtypeStruct((rows, 2 * hidden), jnp.bfloat16)
     return pl.pallas_call(
-        ffn_in_kernel,
+        ffn_kernel,
         grid=(2 * per,),
-        in_specs=[
-            full_spec((rows, width)),
-            pl.BlockSpec((width, cols), lambda i: (0, jnp.minimum(i, per - 1))),
-            pl.BlockSpec((width, cols), lambda i: (0, jnp.maximum(i - per, 0))),
-        ],
-        out_specs=[out, out],
-        out_shape=[shape, shape],
+        in_specs=[tile, tile, tile, full_spec(norms.shape)]
+        + slice_specs(width, cols, per),
+        out_specs=[tile, full_spec((rows, 128)), tile, chunk, chunk],
+        out_shape=[low, jax.ShapeDtypeStruct((rows, 128), jnp.float32), low, units, units],
         compiler_params=params(VMEM_MIB),
-        cost_estimate=cost(10e-6),
-        name="ffn_in",
-    )(x, w_a, w_b)
+        cost_estimate=cost(14e-6),
+        name="feed_forward",
+    )(tok, mine, got, norms, *inner)
 
 
 def ffn_out_kernel(act_ref, a_ref, b_ref, out_ref):
@@ -646,10 +648,10 @@
 
 
 def middle_kernel(
-    normed_ref, mine_ref, got_ref, norms, proj_ref, cot_ref, emb_ref, gh2_ref, low_ref, turned_ref, pg_ref, vec_ref
+    normed_ref, mine_ref, got_ref, norms, proj_ref, cot_ref, emb_ref, gh2_ref, low_ref, pg_ref, vec_ref
 ):
     step = pl.program_id(0)
-    first = normed_ref[...] * norms[0:1, :] + norms[1:2, :]
+    first = wide(normed_ref) * norms[0:1, :] + norms[1:2, :]
     normed, inv = normalize(first + (wide(mine_ref) + wide(got_ref)))
     second = (normed * norms[2:3, :] + norms[3:4, :]).astype(jnp.bfloat16)
     projected = dot(second, proj_ref[...])
@@ -662,9 +664,7 @@
     grad_second = dot(grad_projected, proj_ref[...], NT)
     grad = norm_backward(grad_second, normed, inv, norms[2:3, :])
     gh2_ref[...] = grad
-    low = grad.astype(jnp.bfloat16)
-    low_ref[...] = low
-    turned_ref[...] = low.T
+    low_ref[...] = grad.astype(low_ref.dtype)
 
     @pl.when(step == 0)
     def _():
@@ -696,7 +696,6 @@
             rows_spec(block, p_width),
             tile,
             tile,
-            pl.BlockSpec((width, block), lambda i: (0, i)),
             full_spec((width, p_width)),
             full_spec((8, width)),
         ],
@@ -704,7 +703,6 @@
             jax.ShapeDtypeStruct((rows, p_width), jnp.float32),
             jax.ShapeDtypeStruct((rows, width), jnp.float32),
             jax.ShapeDtypeStruct((rows, width), jnp.bfloat16),
-            jax.ShapeDtypeStruct((width, rows), jnp.bfloat16),
             jax.ShapeDtypeStruct((width, p_width), jnp.float32),
             jax.ShapeDtypeStruct((8, width), jnp.float32),
         ],
@@ -714,83 +712,84 @@
     )(normed, mine, got, norms, proj, cot)
 
 
-def back_outer_kernel(g_ref, gt_ref, act_ref, slope_ref, a_ref, b_ref, wga_ref, wgb_ref, gpre_ref):
-    def work(w_ref, wg_ref):
-        wg_ref[...] = dot(gt_ref[...], act_ref[...]).astype(wg_ref.dtype)
-        for r in range(0, g_ref.shape[0], 256):
-            rows = slice(r, r + 256)
-            grad = dot(g_ref[rows, :], w_ref[...]) * slope_ref[rows, :].astype(jnp.float32)
-            gpre_ref[rows, :] = grad.astype(gpre_ref.dtype)
-
-    first = pl.program_id(0) < pl.num_programs(0) // 2
-    pl.when(first)(lambda: work(a_ref, wga_ref))
-    pl.when(jnp.logical_not(first))(lambda: work(b_ref, wgb_ref))
-
-
-def back_outer(grad, grad_t, act, slope, w_a, w_b):
+def ffn_back_kernel(
+    turns, bits, g_ref, x_ref, act_ref, slope_ref, ia, ib, oa, ob, keep_a, send_a, keep_b, send_b, out_ref, acc, g_t, x_t, wgrad
+):
+    step = pl.program_id(0)
+    steps = pl.num_programs(0)
+
+    @pl.when(step == 0)
+    def _():
+        g_t[...] = g_ref[...].T
+        x_t[...] = x_ref[...].T
+        acc[...] = jnp.zeros_like(acc)
+
+    def put(which, run, keep, send, bit):
+        for j in range(keep.shape[1] // run):
+            for out, side in ((keep, bit), (send, 1 - bit)):
+                rows = pl.ds(pl.multiple_of((2 * j + side) * run, run), run)
+                out[which, j * run : (j + 1) * run, :] = wgrad[rows, :].astype(out.dtype)
+
+    def work(i_ref, o_ref, run, keep, send, bit):
+        wgrad[...] = dot(g_t[...], act_ref[...])
+        put(0, run, keep, send, bit)
+        grad = dot(g_ref[...], o_ref[...]) * slope_ref[...].astype(jnp.float32)
+        grad = grad.astype(jnp.bfloat16)
+        wgrad[...] = dot(x_t[...], grad)
+        put(1, run, keep, send, bit)
+        acc[...] += dot(grad, i_ref[...], NT)
+
+    first = step < steps // 2
+    pl.when(first)(lambda: work(ia, oa, turns[0], keep_a, send_a, bits[0]))
+    pl.when(jnp.logical_not(first))(lambda: work(ib, ob, turns[1], keep_b, send_b, bits[1]))
+
+    @pl.when(step == steps - 1)
+    def _():
+        out_ref[...] = acc[...].astype(out_ref.dtype)
+
+
+def ffn_back(bits, turns, grad, x, act, slope, inner, outer, hidden):
     rows, width = grad.shape
-    hidden = w_a.shape[1]
-    cols = 384
+    cols = FFN_COLS
     per = hidden // cols
-    tile = pl.BlockSpec((rows, cols), lambda i: (0, i))
-    mat_a = pl.BlockSpec((width, cols), lambda i: (0, jnp.minimum(i, per - 1)))
-    mat_b = pl.BlockSpec((width, cols), lambda i: (0, jnp.maximum(i - per, 0)))
-    shape = jax.ShapeDtypeStruct((width, hidden), jnp.bfloat16)
+
+    def left(i):
+        return jnp.minimum(i, per - 1)
+
+    def right(i):
+        return jnp.maximum(i - per, 0)
+
+    tile = pl.BlockSpec((rows, width), lambda i, e: (0, 0))
+    chunk = pl.BlockSpec((rows, cols), lambda i, e: (0, i))
+    mats = [
+        pl.BlockSpec((width, cols), lambda i, e: (0, left(i))),
+        pl.BlockSpec((width, cols), lambda i, e: (0, right(i))),
+    ]
+    outs = [
+        pl.BlockSpec((2, width // 2, cols), lambda i, e: (0, 0, left(i))),
+        pl.BlockSpec((2, width // 2, cols), lambda i, e: (0, 0, right(i))),
+    ]
+    low = jnp.bfloat16
+    shape = jax.ShapeDtypeStruct((2, width // 2, hidden), low)
     return pl.pallas_call(
-        back_outer_kernel,
-        grid=(2 * per,),
-        in_specs=[full_spec((rows, width)), full_spec((width, rows)), tile, tile, mat_a, mat_b],
-        out_specs=[mat_a, mat_b, tile],
-        out_shape=[shape, shape, jax.ShapeDtypeStruct(act.shape, jnp.bfloat16)],
+        functools.partial(ffn_back_kernel, turns),
+        grid_spec=pltpu.PrefetchScalarGridSpec(
+            num_scalar_prefetch=1,
+            grid=(2 * per,),
+            in_specs=[tile, tile, chunk, chunk] + mats * 2,
+            out_specs=[outs[0], outs[0], outs[1], outs[1], tile],
+            scratch_shapes=[
+                pltpu.VMEM((rows, width), jnp.float32),
+                pltpu.VMEM((width, rows), low),
+                pltpu.VMEM((width, rows), low),
+                pltpu.VMEM((width, cols), jnp.float32),
+            ],
+        ),
+        out_shape=[shape] * 4 + [jax.ShapeDtypeStruct((rows, width), low)],
         compiler_params=params(VMEM_MIB),
-        cost_estimate=cost(9e-6),
-        name="back_outer",
-    )(grad, grad_t, act, slope, w_a, w_b)
-
-
-def back_inner_kernel(xt_ref, gpre_ref, a_ref, b_ref, wga_ref, wgb_ref, out_ref, acc):
-    step = pl.program_id(0)
-
-    @pl.when(step == 0)
-    def _():
-        acc[...] = jnp.zeros_like(acc)
-
-    def work(w_ref, wg_ref):
-        wg_ref[...] = dot(xt_ref[...], gpre_ref[...]).astype(wg_ref.dtype)
-        acc[...] += dot(gpre_ref[...], w_ref[...], NT)
-
-    first = step < pl.num_programs(0) // 2
-    pl.when(first)(lambda: work(a_ref, wga_ref))
-    pl.when(jnp.logical_not(first))(lambda: work(b_ref, wgb_ref))
-
-    @pl.when(step == pl.num_programs(0) - 1)
-    def _():
-        out_ref[...] = acc[...].astype(out_ref.dtype)
-
-
-def back_inner(x_t, grad_pre, w_a, w_b, hidden):
-    width, rows = x_t.shape
-    cols = 384
-    per = hidden // cols
-    mat_a = pl.BlockSpec((width, cols), lambda i: (0, jnp.minimum(i, per - 1)))
-    mat_b = pl.BlockSpec((width, cols), lambda i: (0, jnp.maximum(i - per, 0)))
-    shape = jax.ShapeDtypeStruct((width, hidden), jnp.bfloat16)
-    return pl.pallas_call(
-        back_inner_kernel,
-        grid=(2 * per,),
-        in_specs=[
-            full_spec((width, rows)),
-            pl.BlockSpec((rows, cols), lambda i: (0, i)),
-            mat_a,
-            mat_b,
-        ],
-        out_specs=[mat_a, mat_b, full_spec((rows, width))],
-        out_shape=[shape, shape, jax.ShapeDtypeStruct((rows, width), jnp.bfloat16)],
-        scratch_shapes=[pltpu.VMEM((rows, width), jnp.float32)],
-        compiler_params=params(VMEM_MIB),
-        cost_estimate=cost(9e-6),
-        name="back_inner",
-    )(x_t, grad_pre, w_a, w_b)
+        cost_estimate=cost(17e-6),
+        name="ffn_back",
+    )(bits, grad, x, act, slope, *inner, *outer)
 
 
 def first_back_kernel(
@@ -822,7 +821,7 @@
         vec[2:4, :] = vec2_ref[0:2, :]
 
     grad = gh2_ref[...] + (wide(mine_ref) + wide(got_ref))
-    normed = normed_ref[...]
+    normed = wide(normed_ref)
     vec[0:1, :] += jnp.sum(grad * normed, axis=0, keepdims=True)
     vec[1:2, :] += jnp.sum(grad, axis=0, keepdims=True)
     grad_h1 = norm_backward(grad, normed, inv_ref[:, 0:1], norms[0:1, :])
@@ -878,33 +877,62 @@
         ],
         scratch_shapes=[pltpu.VMEM((width, cols), jnp.float32), pltpu.VMEM((128, width), jnp.float32)],
         compiler_params=params(VMEM_MIB),
-        cost_estimate=cost(6e-6),
+        cost_estimate=cost(1e-6),
         name="first_back",
     )(mine, got, grad_h2, normed, inv, norms, output_w, *mixed, proj_part, vec2)
 
 
-def far_kernel(dk, dv, wk, wv, gx_ref):
-    gx_ref[...] = (dot(dk[...], wk[...], NT) + dot(dv[...], wv[...], NT)).astype(gx_ref.dtype)
-
-
-def far_grads(dk, dv, key_w, value_w):
-    rows = dk.shape[0] // 2
-    width, cols = key_w.shape
-    block = 512
-    tile = pl.BlockSpec((block, cols), lambda i: (i + rows // block, 0))
+def token_grads_kernel(core, *refs):
+    *parts, a_ref, b_ref, theirs, mine, wq, wk, wv = refs
+    step = pl.program_id(0)
+    weights = (wq, wk, wv)[-(len(parts) // GROUPS) :]
+
+    @pl.when(step == 0)
+    def _():
+        build_heads((wq, wk, wv), a_ref, b_ref)
+
+    total = 0.0
+    for i, w in enumerate(weights):
+        grads = [parts[p * len(weights) + i][...] for p in range(GROUPS)]
+        total = total + dot(jnp.concatenate(grads, axis=1), w[...], NT)
+
+    @pl.when(step == 0)
+    def _():
+        theirs[...] = total.astype(theirs.dtype)
+
+    @pl.when(step == 1)
+    def _():
+        mine[...] = total.astype(mine.dtype)
+
+
+def token_grads(core, far, grads, w_a, w_b):
+    half = grads[0][0].shape[0] // 2
+    width = w_a.shape[0]
+    skip = 2 if far else 0
+    used = [arrays[1:] if far else arrays for arrays in grads]
+    rows = lambda i, core: (skip + jnp.where(i < 1, 1 - core[0], core[0]), 0)
+    specs = [pl.BlockSpec((half, x.shape[1]), rows) for arrays in used for x in arrays]
+    mat = pl.BlockSpec(w_a.shape, lambda i, core: (0, 0))
+    shape = jax.ShapeDtypeStruct((half, width), jnp.bfloat16)
+    whole = pl.BlockSpec((half, width), lambda i, core: (0, 0))
     return pl.pallas_call(
-        far_kernel,
-        grid=(rows // block,),
-        in_specs=[tile] * 2 + [full_spec((width, cols))] * 2,
-        out_specs=rows_spec(block, width),
-        out_shape=jax.ShapeDtypeStruct((rows, width), jnp.bfloat16),
+        token_grads_kernel,
+        grid_spec=pltpu.PrefetchScalarGridSpec(
+            num_scalar_prefetch=1,
+            grid=(2,),
+            in_specs=specs + [mat, mat],
+            out_specs=[whole, whole],
+            scratch_shapes=[pltpu.VMEM((width, 384), jnp.bfloat16)] * 3,
+        ),
+        out_shape=[shape, shape],
         compiler_params=params(VMEM_MIB),
-        cost_estimate=cost(3e-6),
-        name="far_grads",
-    )(dk, dv, key_w, value_w)
-
-
-def head_grads_kernel(x_ref, dq, dk, dv, wq, wk, wv, og_ref, gx_ref, a_ref, b_ref, acc):
+        cost_estimate=cost(0.5e-6),
+        name="token_grads",
+    )(core.reshape(1), *[x for arrays in used for x in arrays], w_a, w_b)
+
+
+def head_grads_kernel(x_ref, *refs):
+    *parts, og_ref, a_ref, b_ref, acc = refs
     step = pl.program_id(0)
     steps = pl.num_programs(0)
 
@@ -913,14 +941,14 @@
         acc[...] = jnp.zeros_like(acc)
 
     x_t = x_ref[...].T
-    acc[1] += dot(x_t, dk[...])
-    acc[2] += dot(x_t, dv[...])
-
-    @pl.when(step < steps // 2)
-    def _():
-        acc[0] += dot(x_t, dq[...])
-        gx = dot(dk[...], wk[...], NT) + dot(dv[...], wv[...], NT) + dot(dq[...], wq[...], NT)
-        gx_ref[...] = gx.astype(gx_ref.dtype)
+
+    def add(i):
+        grads = [parts[3 * p + i][...] for p in range(GROUPS)]
+        acc[i] += dot(x_t, jnp.concatenate(grads, axis=1))
+
+    add(1)
+    add(2)
+    pl.when(step < steps // 2)(lambda: add(0))
 
     @pl.when(step == steps - 1)
     def _():
@@ -938,35 +966,28 @@
                 out[:, 512 + DH * i : 512 + DH * i + 128] = jnp.concatenate(both, axis=1)
 
 
-def head_grads(tok_all, dq, dk, dv, weights, output_part):
+def head_grads(tok_all, grads, output_part):
     span, width = tok_all.shape
     block = 512
     steps = span // block
-    cols = dq.shape[1]
-    low = jnp.bfloat16
     near = lambda i: (jnp.minimum(i, steps // 2 - 1), 0)
+    specs = []
+    for dq, _, _ in grads:
+        cols = dq.shape[1]
+        specs += [pl.BlockSpec((block, cols), near), rows_spec(block, cols), rows_spec(block, cols)]
     packed = full_spec((width, 768))
+    shape = jax.ShapeDtypeStruct((width, 768), jnp.bfloat16)
     return pl.pallas_call(
         head_grads_kernel,
         grid=(steps,),
-        in_specs=[
-            rows_spec(block, width),
-            pl.BlockSpec((block, cols), near),
-            rows_spec(block, cols),
-            rows_spec(block, cols),
-        ]
-        + [full_spec((width, cols))] * 4,
-        out_specs=[pl.BlockSpec((block, width), near), packed, packed],
-        out_shape=[
-            jax.ShapeDtypeStruct((span // 2, width), low),
-            jax.ShapeDtypeStruct((width, 768), low),
-            jax.ShapeDtypeStruct((width, 768), low),
-        ],
-        scratch_shapes=[pltpu.VMEM((3, width, cols), jnp.float32)],
+        in_specs=[rows_spec(block, width)] + specs + [full_spec(output_part.shape)],
+        out_specs=[packed, packed],
+        out_shape=[shape, shape],
+        scratch_shapes=[pltpu.VMEM((3, width, 384), jnp.float32)],
         compiler_params=params(VMEM_MIB),
-        cost_estimate=cost(9e-6),
+        cost_estimate=cost(0.5e-6),
         name="head_grads",
-    )(tok_all, dq, dk, dv, *weights, output_part)
+    )(tok_all, *[x for arrays in grads for x in arrays], output_part)
 
 
 def unpack_heads(packed):
@@ -1004,6 +1025,11 @@
     edge = min(SEG_MOST, length)
     bf16, f32 = jnp.bfloat16, jnp.float32
 
+    def by_core(mine, theirs, axis):
+        return jnp.concatenate(
+            [jnp.where(core == 0, mine, theirs), jnp.where(core == 0, theirs, mine)], axis=axis
+        )
+
     tok_m = lax.dynamic_index_in_dim(tokens, micro, 0, False)[0]
     sent = lax.dynamic_slice_in_dim(tok_m, (1 - ctx) * (length - edge), edge, 0)
     got = route(sent, lambda s, c, t: (s, 1 - c, t) if s % 2 == t % 2 else None)
@@ -1017,21 +1043,24 @@
     ffn_own = jnp.concatenate([inner_weight, output_in.T, proj_weight, vectors, outer_in.T], axis=1)
     ffn_all = lax.all_gather(ffn_own, "tp", axis=0)
     tok_m = lax.dynamic_index_in_dim(tokens_in, micro, 0, False)[0]
+
+    *heads_parts, got, ffn_own, tok_m, segments_in, cot_in = tie(
+        *heads_parts, got, ffn_own, tok_m, segments_in, cot_in
+    )
+    heads_a, heads_b = gather_tp_finish(heads_parts)
+    other_a, other_b = gather_start(heads_a, "y"), gather_start(heads_b, "x")
     tok_got = swap(tok_m, "shard", 1)
     seg_m = lax.dynamic_index_in_dim(segments_in, micro, 0, False)
     seg_m = seg_m.reshape(1, -1, 128)
     upto = jnp.arange(8, dtype=jnp.int32).reshape(8, 1, 1)
     counts_own = jnp.sum((seg_m <= upto).astype(jnp.int32), axis=(1, 2))
     counts_got = swap(counts_own, "shard", 1)
-
-    heads_a, heads_b = gather_tp_finish(tie(*heads_parts, ffn_own, counts_own)[:4])
-    other_a, other_b = gather_start(heads_a, "y"), gather_start(heads_b, "x")
-    cot_m = lax.dynamic_index_in_dim(after(cot_in, heads_a), micro, 0, False)[0]
-    cot_got = swap(cot_m, "shard", 1)
-    other_a, other_b, got, tok_got, counts_got = tie(other_a, other_b, got, tok_got, counts_got)
+    cot_m = lax.dynamic_index_in_dim(cot_in, micro, 0, False)[0]
+    other_a, other_b, tok_got, counts_got, cot_m = tie(other_a, other_b, tok_got, counts_got, cot_m)
     heads_a, heads_b = gather_finish(heads_a, other_a, "y"), gather_finish(heads_b, other_b, "x")
     other_a, other_b = gather_start(heads_a, "x"), gather_start(heads_b, "y")
     got_core = swap(got, "shard", 1)
+    cot_got = swap(cot_m, "shard", 1)
     counts = jnp.where(owner, counts_own, counts_got)
     counts = counts + swap(counts, "ctx", 1)
     place_of = jnp.arange(8)
@@ -1044,15 +1073,15 @@
     cot = jnp.where(owner, cot_m, cot_got)
     other_a, other_b, tok_all, cot, ends = tie(other_a, other_b, tok_all, cot, ends)
     heads_a, heads_b = gather_finish(heads_a, other_a, "x"), gather_finish(heads_b, other_b, "y")
-
-    queries, keys, values, *head_w = project(tok_all, flat_rows(heads_a), flat_rows(heads_b))
-    ffn_all = after(ffn_all, heads_a, heads_b)
+    heads_a, heads_b = flat_rows(heads_a), flat_rows(heads_b)
+
+    core_dim = shard_bits() - 1
+    queries, keys, values = project(tok_all, heads_a, heads_b)
+    ffn_all = after(ffn_all, keys)
     kept = lax.dynamic_slice_in_dim(ffn_all, 2 * core, 2, 0)
     other = swap(lax.dynamic_slice_in_dim(ffn_all, 2 - 2 * core, 2, 0), "shard", 1)
-    other, queries, keys, values = tie(other, queries, keys, values)
-    core_dim = shard_bits() - 1
     shape = (1,) * core_dim + (1, 1) + ffn_own.shape
-    split = 1152
+    split = inner_weight.shape[1] + 384
     inner, outer = [], []
     for s in range(2):
         both = join(kept[s].reshape(shape), other[s].reshape(shape), "shard", 1, core_dim)
@@ -1061,72 +1090,53 @@
     inner_got = [gather_start(inner[0], "x"), gather_start(inner[1], "y")]
     outer_got = [gather_start(outer[0], "x"), gather_start(outer[1], "y")]
     mixed_low, lse_low = attn_forward(after(ends, *inner, *outer), 0, queries, keys, values)
-    inner_got = after_all(mixed_low, *inner_got)
+    mixed_low, *inner_got = tie(mixed_low, *inner_got)
     inner = [gather_finish(inner[0], inner_got[0], "x"), gather_finish(inner[1], inner_got[1], "y")]
     inner_got = [gather_start(inner[0], "y"), gather_start(inner[1], "x")]
     mixed_high, lse_high = attn_forward(
         after(ends, mixed_low, *inner), half // BQ, queries, keys, values
     )
-    outer_got = after_all(mixed_high, *outer_got)
-    outer = [gather_finish(outer[0], outer_got[0], "x"), gather_finish(outer[1], outer_got[1], "y")]
+    mixed_high, *got_all = tie(mixed_high, *inner_got, *outer_got)
+    outer = [gather_finish(outer[0], got_all[2], "x"), gather_finish(outer[1], got_all[3], "y")]
     outer_got = [gather_start(outer[0], "y"), gather_start(outer[1], "x")]
-    inner_got = after_all(mixed_high, *inner_got)
-    inner_got = after_all(outer[0], *inner_got)
-    inner_a = flat_rows(gather_finish(inner[0], inner_got[0], "y"))
-    inner_b = flat_rows(gather_finish(inner[1], inner_got[1], "x"))
+    inner = [
+        flat_rows(gather_finish(inner[0], got_all[0], "y")),
+        flat_rows(gather_finish(inner[1], got_all[1], "x")),
+    ]
     mixed = (mixed_low, mixed_high)
-    part, output_w, proj, norms = attn_out(mixed, inner_a, inner_b)
+    part, output_w, proj, norms = attn_out(mixed, *inner)
 
     hidden_cols = outer_weight.shape[0]
-    normed, inv, first_low, first_t = first_norm(tok_here, part, swap(part, "shard", 1), norms)
-    act, slope = ffn_in(first_low, inner_a, inner_b, hidden_cols)
-    outer_got = after_all(act, *outer_got)
-    outer_a = flat_rows(gather_finish(outer[0], outer_got[0], "y"))
-    outer_b = flat_rows(gather_finish(outer[1], outer_got[1], "x"))
-    part = ffn_out(act, outer_a, outer_b)
-    embedding, grad_h2, grad_ffn, grad_ffn_t, proj_part, vec2 = middle(
+    normed, inv, first_low, act, slope = feed_forward(
+        tok_here, part, swap(part, "shard", 1), norms, inner, hidden_cols
+    )
+    act, *outer_got = tie(act, *outer_got)
+    outer = [
+        flat_rows(gather_finish(outer[0], outer_got[0], "y")),
+        flat_rows(gather_finish(outer[1], outer_got[1], "x")),
+    ]
+    part = ffn_out(act, *outer)
+    embedding, grad_h2, grad_ffn, proj_part, vec2 = middle(
         normed, part, swap(part, "shard", 1), norms, proj, cot
     )
 
-    outer_a, outer_b, grad_pre = back_outer(grad_ffn, grad_ffn_t, act, slope, outer_a, outer_b)
-    outer = [split_rows(outer_a), split_rows(outer_b)]
-    outer_got = [scatter_start(outer[0], "x"), scatter_start(outer[1], "y")]
-    inner_a, inner_b, part = back_inner(
-        first_t, after(grad_pre, *outer), inner_a, inner_b, hidden_cols
-    )
+    rows = model_width // (lax.axis_size("shard") * lax.axis_size("ctx"))
+    y_axis, y_bit, _ = steps_of("y")[0]
+    y_mine = my_bit(y_axis, y_bit)
+    x_first = rows % 16 == 0
+    bits = jnp.stack([ctx if x_first else y_mine, y_mine]).astype(jnp.int32)
+    turns = (rows if x_first else model_width // 2, model_width // 2)
+    keep_a, send_a, keep_b, send_b, part = ffn_back(
+        bits, turns, grad_ffn, first_low, act, slope, inner, outer, hidden_cols
+    )
+    wgrad_got = [
+        swap(send_a, "ctx", 1) if x_first else swap(send_a, y_axis, y_bit),
+        swap(send_b, y_axis, y_bit),
+    ]
     part_got = swap(part, "shard", 1)
-    inner = [split_rows(inner_a), split_rows(inner_b)]
-    inner_got = [scatter_start(inner[0], "x"), scatter_start(inner[1], "y")]
-    outer_got = after_all(part, *outer_got)
-    outer = [
-        scatter_finish(outer[0], outer_got[0], "x"),
-        scatter_finish(outer[1], outer_got[1], "y"),
-    ]
-    outer_got = [scatter_start(outer[0], "y"), scatter_start(outer[1], "x")]
     grad_h1, grad_mixed, output_part, small = first_back(
-        part,
-        after(part_got, *outer, *inner),
-        grad_h2,
-        normed,
-        inv,
-        norms,
-        output_w,
-        mixed,
-        proj_part,
-        vec2,
-    )
-    inner_got = after_all(grad_mixed, *inner_got)
-    inner = [
-        scatter_finish(inner[0], inner_got[0], "x"),
-        scatter_finish(inner[1], inner_got[1], "y"),
-    ]
-    inner_got = [scatter_start(inner[0], "y"), scatter_start(inner[1], "x")]
-    outer_got = after_all(grad_mixed, *outer_got)
-    outer = [
-        scatter_finish(outer[0], outer_got[0], "y"),
-        scatter_finish(outer[1], outer_got[1], "x"),
-    ]
-    outer_parts = scatter_tp_start(*outer)
+        part, part_got, grad_h2, normed, inv, norms, output_w, mixed, proj_part, vec2
+    )
 
     small = lax.dynamic_slice_in_dim(split_rows(small), core, 1, core_dim)
     small_got = scatter_start(small, "y")
@@ -1139,48 +1149,47 @@
         )
         for d in range(2)
     ]
-    dq, dk, dv = attn_backward(
-        after(ends, *inner, *outer, small, emb_half),
-        queries,
-        grad_mixed,
-        mixed,
-        (lse_low, lse_high),
-        keys,
-        values,
-    )
-
-    def start_half(full):
-        return swap(lax.dynamic_slice_in_dim(full, (1 - core) * half, half, 0), "shard", 1)
-
-    def sum_half(full, got_half):
-        kept_half = lax.dynamic_slice_in_dim(full, core * half, half, 0)
-        return kept_half.astype(f32) + got_half.astype(f32)
-
-    gx_far = far_grads(dk, dv, *head_w[1:])
-    far_got = start_half(gx_far)
-    *inner_got, small_got = after_all(gx_far, *inner_got, small_got)
-    inner = [
-        scatter_finish(inner[0], inner_got[0], "y"),
-        scatter_finish(inner[1], inner_got[1], "x"),
+    flow = (queries, grad_mixed, mixed, (lse_low, lse_high), keys, values)
+    grads = attn_backward(after(ends, small, emb_half), 0, 3, *flow)
+    *grads, wgrad_got[0], wgrad_got[1], small_got, emb_got[0], emb_got[1] = tie(
+        *grads, *wgrad_got, small_got, *emb_got
+    )
+    grads = [grads]
+
+    def added(kept, got):
+        return (kept.astype(f32) + got.astype(f32)).astype(bf16)
+
+    theirs, far_mine = token_grads(core, True, grads, heads_a, heads_b)
+    far_got = swap(theirs, "shard", 1)
+    wgrad_got = after_all(theirs, *wgrad_got)
+    lead = (2,) * (shard_bits() - 1)
+    last = (rows, hidden_cols)
+    shapes = [(2, *lead, 2, 1, *last), (2, 1, *lead[1:], 2, 2, *last)]
+    second_steps = ("y" if x_first else "x", "x")
+    wgrad = [
+        added(keep_a, wgrad_got[0]).reshape(shapes[0 if x_first else 1]),
+        added(keep_b, wgrad_got[1]).reshape(shapes[1]),
     ]
-    small = scatter_finish(small, small_got, "y")
+    wgrad = [scatter_rest(w, "y", 1) if n == "x" else w for w, n in zip(wgrad, second_steps)]
+    far_got, *wgrad = tie(far_got, *wgrad)
+    far_sum = added(far_mine, far_got)
+    from_far = swap(far_sum, "ctx", 1)
+    wgrad_got = [scatter_start(w, n, 1) for w, n in zip(after_all(far_sum, *wgrad), second_steps)]
+    small = scatter_finish(small, after(small_got, far_sum), "y")
     small_got = scatter_start(small, "x")
-    far_sum = sum_half(gx_far, after(far_got, *inner, small)).astype(bf16)
-    from_far = swap(far_sum, "ctx", 1)
-    inner_parts = scatter_tp_start(*inner)
-    gx, grad_a, grad_b = head_grads(
-        after(tok_all, far_sum, *inner), dq, dk, dv, head_w, output_part
-    )
-    gx_got = start_half(gx)
+    theirs, near_mine = token_grads(core, False, grads, after(heads_a, far_sum, *wgrad), heads_b)
+    near_got = swap(theirs, "shard", 1)
+    grad_a, grad_b = head_grads(after(tok_all, theirs), grads, output_part)
+    grad_a, grad_b, near_got, *wgrad_got = tie(grad_a, grad_b, near_got, *wgrad_got)
     grad_a, grad_b = split_rows(grad_a), split_rows(grad_b)
     got_a, got_b = scatter_start(grad_a, "y"), scatter_start(grad_b, "x")
-    outer_parts = after_all(gx, *outer_parts)
-    outer_grad = sum_all(outer_parts).reshape(-1, hidden_cols).T
-    small = scatter_finish(small, after(small_got, gx), "x").reshape(-1, small.shape[-1])
-    small_parts = [small] + [swap(small, "tp", d) for d in range(1, 4)]
+    wgrad = [scatter_finish(w, g, n, 1) for w, g, n in zip(wgrad, wgrad_got, second_steps)]
     mine = lax.dynamic_slice_in_dim(grad_h1, core * half, half, 0)
-    gx_sum = sum_half(gx, gx_got)
-    grad_tok = (gx_sum + after(from_far, gx_got).astype(f32) + mine).astype(bf16)
+    near_sum = near_mine.astype(f32) + near_got.astype(f32) + mine
+    small = scatter_finish(small, after(small_got, near_sum), "x").reshape(-1, small.shape[-1])
+    near_sum, from_far, small, *wgrad = tie(near_sum, from_far, small, *wgrad)
+    grad_tok = (near_sum + from_far.astype(f32)).astype(bf16)
+    wgrad_parts = scatter_tp_start(*wgrad)
     own_cols = model_width // lax.axis_size("tp")
     col_parts = [grad_tok[:, own_cols * j : own_cols * (j + 1)] for j in range(4)]
     place = 2 * micro + core
@@ -1191,20 +1200,21 @@
         )
         for d in range(4)
     ]
-    got_a, got_b, *inner_parts = after_all(grad_tok, got_a, got_b, *inner_parts)
+    small_parts = [small] + [swap(small, "tp", d) for d in range(1, 4)]
+    got_a, got_b = after_all(grad_tok, got_a, got_b)
     grad_a, grad_b = scatter_finish(grad_a, got_a, "y"), scatter_finish(grad_b, got_b, "x")
     got_a, got_b = scatter_start(grad_a, "x"), scatter_start(grad_b, "y")
-    *inner_parts, small_last = after_all((grad_a, grad_b), *inner_parts, small_parts[-1])
-    inner_grad = sum_all(inner_parts).reshape(-1, hidden_cols)
-    small = sum_all(small_parts[:3] + [small_last])
-    emb_got = after_all(grad_tok, *emb_got)
+    wgrad_parts = after_all((grad_a, grad_b), *wgrad_parts)
+    wgrad_sum = sum_all(wgrad_parts).reshape(2, -1, hidden_cols)
+    outer_grad, inner_grad = wgrad_sum[0].T, wgrad_sum[1]
+    small = sum_all(small_parts)
     embeddings = jnp.stack([lax.select_n((group % 2) ^ m, *emb_got) for m in range(2)])
     embeddings = embeddings.reshape(2, 1, quarter, -1)
     got_a, got_b = after_all(inner_grad, got_a, got_b)
     grad_a, grad_b = scatter_finish(grad_a, got_a, "x"), scatter_finish(grad_b, got_b, "y")
+    arrived = after_all((grad_a, grad_b), *arrived)
     heads_grad = sum_all(scatter_tp_start(grad_a, grad_b))
     heads_grad = heads_grad.reshape(-1, heads_grad.shape[-1])
-    arrived = after_all((grad_a, grad_b), *arrived)
     grad_tokens = jnp.stack([lax.select_n(group ^ j, *arrived) for j in range(4)])
     grad_tokens = grad_tokens.reshape(2, 1, length, own_cols).astype(f32)
     query_grad, key_grad, value_grad, output_grad = unpack_heads(heads_grad)

time: 378 us -> 349 us (0.923)
  Pallas kernels: 128 us -> 98.7 us
  waiting for transfers between devices: 89.6 us -> 78.2 us
  local copies, waits for them, and re-layouts: 28.7 us -> 35.9 us
  starting transfers between devices: 86.8 us -> 92.2 us
    unnamed x118 -> x138, local copies, waits for them, and re-layouts: 16.4 us -> 26.5 us
    all_gather x1, waiting for transfers between devices: 6.4 us -> 0.01 us  [per_device(): ffn_all = lax.all_gather(ffn_own, 'tp', axis=0)]
    ppermute x23 -> x19, waiting for transfers between devices: 26.9 us -> 21.3 us  [route(): return lax.ppermute(v, ('shard', 'ctx', 'tp'), pairs)]
    pallas_call x5 -> x4, Pallas kernels: 38.8 us -> 33.4 us  [the longest x1 16.5 us: ffn_back(): pl.pallas_call(functools.partial(ffn_back_kernel, turns), grid_spec=pltpu...]
    pallas_call x1, Pallas kernels: 23.6 us -> 18.3 us  [attn_backward(): pl.pallas_call(attn_bwd_kernel, grid_spec=pltpu.PrefetchScalarGridSpec(nu...]
    pallas_call x1, Pallas kernels: 11.3 us -> 5.95 us  [head_grads(): pl.pallas_call(head_grads_kernel, grid=(steps,), in_specs=[rows_spec(bloc...]
    ppermute x23 -> x19, starting transfers between devices: 42.1 us -> 47.4 us  [route(): return lax.ppermute(v, ('shard', 'ctx', 'tp'), pairs)]
    convert_element_type x2 -> x3, other arithmetic: 0.59 us -> 4.58 us  [the longest x2 4.43 us: added(): return (kept.astype(f32) + got.astype(f32)).astype(bf16)]
  transfers between devices with their start and end apart: 65 -> 57, of which waited for: 28 -> 21; matrix products, arithmetic and copies ran while one was open for 7% -> 7% of each run, Pallas kernels for 23% -> 20%
where the time goes in v3:
time: 349 us; the launch traced here: 343 us
  Pallas kernels  98.7 us (28%)
  starting transfers between devices  92.2 us (26%)
  waiting for transfers between devices  78.2 us (22%)
  local copies, waits for them, and re-layouts  35.9 us (10%)
  other arithmetic  22.3 us (6%)
  between operations  15.8 us (5%)
    ppermute x37, waiting for transfers between devices, swap(): return lax.ppermute(v, axis, [(i, i ^ bit) for i in range(count)])  56.9 us
    ppermute x19, starting transfers between devices, route(): return lax.ppermute(v, ('shard', 'ctx', 'tp'), pairs)  47.4 us
    ppermute x37, starting transfers between devices, swap(): return lax.ppermute(v, axis, [(i, i ^ bit) for i in range(count)])  44.8 us
    unnamed x138, local copies, waits for them, and re-layouts  26.5 us
    ppermute x19, waiting for transfers between devices, route(): return lax.ppermute(v, ('shard', 'ctx', 'tp'), pairs)  21.3 us
    pallas_call x1, Pallas kernels, attn_backward(): pl.pallas_call(attn_bwd_kernel, grid_spec=pltpu.PrefetchScalarGridSpec(nu...  18.3 us
    pallas_call x2, Pallas kernels, attn_forward(): pl.pallas_call(functools.partial(attn_fwd_kernel, first_block), grid_spec...  17.8 us
    pallas_call x1, Pallas kernels, ffn_back(): pl.pallas_call(functools.partial(ffn_back_kernel, turns), grid_spec=pltpu...  16.5 us
  transfers between devices with their start and end apart: 57, of which 21 were waited for; matrix products, arithmetic and copies ran while one was open for 7% of the time, Pallas kernels for 20%

profile of v3, /device:TPU:1, one launch (start us, length us, event | category | flops | bytes accessed | tf_op | source)
XLA Modules:
  0.0 343.3 jit_solution(9709223383205715649)
XLA Ops:
  12.4 7.3 %collective-permute-start = (bf16[96,640]{1,0:T(8,128)(2,1)S(1)}, bf16[96,640]{1,0:T(8,128)(2,1)S(1)}, u32[]{:S(2)}, u32[]{:S(2)}) collective-permute-start(bf16[96,640]{1,0:T(8,128)(2,1)S(1)} %pack_heads.1), channel_id=1, source_target_pairs={{0,0},{1,1},{2,8},{3,9},{4,4},{5,5},{6,12},{7,13},{8,2},{9,3},{10,... | collective-permute-start | bytes 368648 | tf_op jit(solution)/shard_map/ppermute | solution.py:60
  20.3 3.6 %collective-permute-start.3 = (bf16[96,640]{1,0:T(8,128)(2,1)S(1)}, bf16[96,640]{1,0:T(8,128)(2,1)}, u32[]{:S(2)}, u32[]{:S(2)}) collective-permute-start(bf16[96,640]{1,0:T(8,128)(2,1)S(1)} %pack_heads.1), channel_id=1, source_target_pairs={{0,3},{1,2},{2,11},{3,10},{4,7},{5,6},{6,15},{7,14},{8,1},{9,0},{1... | collective-permute-start | bytes 368648 | tf_op jit(solution)/shard_map/ppermute | solution.py:60
  48.1 9.0 %collective-permute-done.10 = bf16[1,2,2,96,640]{4,3,2,1,0:T(8,128)(2,1)S(1)} collective-permute-done((bf16[1,2,2,96,640]{4,3,2,1,0:T(8,128)(2,1)S(1)}, bf16[1,2,2,96,640]{4,3,2,1,0:T(8,128)(2,1)S(1)}, u32[]{:S(2)}, u32[]{:S(2)}) %collective-permute-start.10) | collective-permute-done | bytes 491552 | tf_op jit(solution)/shard_map/ppermute | solution.py:44
  59.7 5.7 %qkv.1 = (bf16[1024,384]{1,0:T(8,128)(2,1)S(1)}, bf16[2048,384]{1,0:T(8,128)(2,1)S(1)}, bf16[2048,384]{1,0:T(8,128)(2,1)S(1)}) custom-call(bf16[2048,768]{1,0:T(8,128)(2,1)S(1)} %pad_maximum_fusion.x_ref, bf16[768,640]{1,0:T(8,128)(2,1)S(1)} %bitcast.95, bf16[768,640]{1,0:T(8,128)(2,1)S(1)} %bitcast.92), custom_call_target="tpu_custom_call" | custom-call | flops 6899999744 | bytes 1048576 | tf_op jit(solution)/shard_map/qkv/pallas_call | solution.py:464
  79.4 8.3 %attn_fwd.2 = (bf16[512,384]{1,0:T(8,128)(2,1)S(1)}, f32[3,1,1024]{2,1,0:T(1,128)S(1)}) custom-call(s32[8]{0:T(128)S(1)} %compare_select_fusion.ends, bf16[1024,384]{1,0:T(8,128)(2,1)S(1)} %copy-done.48, bf16[2048,384]{1,0:T(8,128)(2,1)S(1)} %copy-done.42, bf16[2048,384]{1,0:T(8,128)(2,1)S(1)} %copy-done.45), custom_call_target="tpu_custom_call" | custom-call | flops 11500000256 | bytes 1048576 | tf_op jit(solution)/shard_map/attn_fwd/pallas_call | solution.py:341
  88.1 4.7 %collective-permute-start.18 = (bf16[2,2,1,96,1152]{4,3,2,1,0:T(8,128)(2,1)S(1)}, bf16[2,2,1,96,1152]{4,3,2,1,0:T(8,128)(2,1)S(1)}, u32[]{:S(2)}, u32[]{:S(2)}) collective-permute-start(bf16[2,2,1,96,1152]{4,3,2,1,0:T(8,128)(2,1)S(1)} %pad_maximum_fusion.9), channel_id=1, source_target_pairs={{0,4},{4,0},{1,5},{5,1},{2,6},{6,2},{3,7},{7,3},{8,12},{12,8},{9,1... | collective-permute-start | bytes 2654216 | tf_op jit(solution)/shard_map/ppermute | solution.py:44
  93.3 9.5 %attn_fwd.3 = (bf16[512,384]{1,0:T(8,128)(2,1)S(1)}, f32[3,1,1024]{2,1,0:T(1,128)S(1)}) custom-call(s32[8]{0:T(128)S(1)} %compare_select_fusion.ends, bf16[1024,384]{1,0:T(8,128)(2,1)S(1)} %copy-done.48, bf16[2048,384]{1,0:T(8,128)(2,1)S(1)} %copy-done.42, bf16[2048,384]{1,0:T(8,128)(2,1)S(1)} %copy-done.45), custom_call_target="tpu_custom_call" | custom-call | flops 11500000256 | bytes 1048576 | tf_op jit(solution)/shard_map/attn_fwd/pallas_call | solution.py:341
  102.9 10.2 %collective-permute-done.18 = bf16[2,2,1,96,1152]{4,3,2,1,0:T(8,128)(2,1)S(1)} collective-permute-done((bf16[2,2,1,96,1152]{4,3,2,1,0:T(8,128)(2,1)S(1)}, bf16[2,2,1,96,1152]{4,3,2,1,0:T(8,128)(2,1)S(1)}, u32[]{:S(2)}, u32[]{:S(2)}) %collective-permute-start.18) | collective-permute-done | bytes 884768 | tf_op jit(solution)/shard_map/ppermute | solution.py:44
  121.1 10.1 %feed_forward.1 = (bf16[1024,768]{1,0:T(8,128)(2,1)S(1)}, f32[1024,128]{1,0:T(8,128)S(1)}, bf16[1024,768]{1,0:T(8,128)(2,1)S(1)}, bf16[1024,1536]{1,0:T(8,128)(2,1)S(1)}, bf16[1024,1536]{1,0:T(8,128)(2,1)S(1)}) custom-call(bf16[1024,768]{1,0:T(8,128)(2,1)S(1)} %broadcast_select_fusion.x_ref, bf16[1024,768]{1,0:T(8,128)(2,1)S(1)} %get-tuple-element.168.mine_ref, ...), custom_call_target="tpu_custom_call" | custom-call | flops 16099999744 | bytes 1048576 | tf_op jit(solution)/shard_map/feed_forward/pallas_call | solution.py:615
  134.3 3.5 %ffn_out.1.mine_ref = bf16[1024,768]{1,0:T(8,128)(2,1)S(1)} custom-call(bf16[1024,1536]{1,0:T(8,128)(2,1)S(1)} %get-tuple-element.174.act_ref, bf16[768,768]{1,0:T(8,128)(2,1)S(1)} %bitcast.106, bf16[768,768]{1,0:T(8,128)(2,1)S(1)} %bitcast.104), custom_call_target="tpu_custom_call" | custom-call | flops 3449999872 | bytes 1048576 | tf_op jit(solution)/shard_map/ffn_out/pallas_call | solution.py:638
  139.0 3.0 collective-permute-done.24.got_ref
  142.0 6.1 %middle.1 = (f32[1024,128]{1,0:T(8,128)S(1)}, f32[1024,768]{1,0:T(8,128)S(1)}, bf16[1024,768]{1,0:T(8,128)(2,1)S(1)}, f32[768,128]{1,0:T(8,128)S(1)}, f32[8,768]{1,0:T(8,128)S(1)}) custom-call(bf16[1024,768]{1,0:T(8,128)(2,1)S(1)} %get-tuple-element.170.normed_ref, bf16[1024,768]{1,0:T(8,128)(2,1)S(1)} %ffn_out.1.mine_ref, ...), custom_call_target="tpu_custom_call" | custom-call | flops 5750000128 | bytes 1048576 | tf_op jit(solution)/shard_map/middle/pallas_call | solution.py:684
  150.3 16.5 %ffn_back.1 = (bf16[2,384,768]{2,1,0:T(8,128)(2,1)S(1)}, bf16[2,384,768]{2,1,0:T(8,128)(2,1)}, bf16[2,384,768]{2,1,0:T(8,128)(2,1)S(1)}, bf16[2,384,768]{2,1,0:T(8,128)(2,1)}, bf16[1024,768]{1,0:T(8,128)(2,1)}) custom-call(s32[2]{0:T(128)S(1)} %pad_add_fusion.bits, bf16[1024,768]{1,0:T(8,128)(2,1)S(1)} %get-tuple-element.180.g_ref, ...), custom_call_target="tpu_custom_call" | custom-call | flops 19549999104 | bytes 1048576 | tf_op jit(solution)/shard_map/ffn_back/pallas_call | solution.py:774
  179.6 5.9 %first_back.1 = (f32[1024,768]{1,0:T(8,128)S(1)}, bf16[1024,384]{1,0:T(8,128)(2,1)S(1)}, bf16[768,384]{1,0:T(8,128)(2,1)S(1)}, bf16[768,256]{1,0:T(8,128)(2,1)S(1)}) custom-call(bf16[1024,768]{1,0:T(8,128)(2,1)} %get-tuple-element.183.mine_ref, bf16[1024,768]{1,0:T(8,128)(2,1)} %collective-permute-done.25.got_ref, ...), custom_call_target="tpu_custom_call" | custom-call | flops 1150000000 | bytes 1048576 | tf_op jit(solution)/shard_map/first_back/pallas_call | solution.py:850
  187.3 4.5 %collective-permute-start.29 = (f32[256,128]{1,0:T(8,128)S(1)}, f32[256,128]{1,0:T(8,128)S(1)}, u32[]{:S(2)}, u32[]{:S(2)}) collective-permute-start(f32[256,128]{1,0:T(8,128)S(1)} %get-tuple-element.350), channel_id=1, source_target_pairs={{0,0},{1,8},{2,1},{3,9},{4,4},{5,12},{6,5},{7,13},{8,2},{9,10},{10... | collective-permute-start | bytes 393224 | tf_op jit(solution)/shard_map/ppermute | solution.py:60
  193.4 18.3 %attn_bwd.1 = (bf16[1024,384]{1,0:T(8,128)(2,1)S(1)}, bf16[2048,384]{1,0:T(8,128)(2,1)S(1)}, bf16[2048,384]{1,0:T(8,128)(2,1)S(1)}) custom-call(s32[8]{0:T(128)S(1)} %compare_select_fusion.ends, bf16[1024,384]{1,0:T(8,128)(2,1)S(1)} %copy-done.49, bf16[1024,384]{1,0:T(8,128)(2,1)S(1)} %get-tuple-element.189.do_ref, ...), custom_call_target="tpu_custom_call" | custom-call | flops 3449999872 | bytes 1048576 | tf_op jit(solution)/shard_map/attn_bwd/pallas_call | solution.py:385
  212.6 3.4 token_grads.2
  216.9 3.0 add_convert_fusion
  221.5 5.9 %collective-permute-start.34 = (bf16[2,1,2,1,96,768]{5,4,0,3,2,1:T(8,128)(2,1)S(1)}, bf16[2,1,2,1,96,768]{5,4,0,3,2,1:T(8,128)(2,1)S(1)}, u32[]{:S(2)}, u32[]{:S(2)}) collective-permute-start(bf16[2,1,2,1,96,768]{5,4,0,3,2,1:T(8,128)(2,1)S(1)} %constant_dynamic-slice_fusion.5), channel_id=1, source_target_pairs={{0,4},{4,0},{1,5},{5,1},{2,6},{6,2},{3,7},{7,3},{8,12},{12,8},{9,1... | collective-permute-start | bytes 1769480 | tf_op jit(solution)/shard_map/ppermute | solution.py:44
  227.4 3.4 token_grads.3
  235.0 5.9 %head_grads.1 = (bf16[768,768]{1,0:T(8,128)(2,1)S(1)}, bf16[768,768]{1,0:T(8,128)(2,1)S(1)}) custom-call(bf16[2048,768]{1,0:T(8,128)(2,1)S(1)} %copy-done.3, bf16[1024,384]{1,0:T(8,128)(2,1)S(1)} %copy-done.11, bf16[2048,384]{1,0:T(8,128)(2,1)S(1)} %get-tuple-element.203.refs_0_.refs_1_, bf16[2048,384]{1,0:T(8,128)(2,1)S(1)} %get-tuple-element.204.refs_1_.refs_2_, ...), custom_call_target="tpu_custom_call" | custom-call | flops 575000000 | bytes 1048576 | tf_op jit(solution)/shard_map/head_grads/pallas_call | solution.py:980
  241.0 5.7 %collective-permute-done.33 = bf16[2,1,2,1,96,768]{5,4,0,3,2,1:T(8,128)(2,1)S(1)} collective-permute-done((bf16[2,1,2,1,96,768]{5,4,0,3,2,1:T(8,128)(2,1)S(1)}, bf16[2,1,2,1,96,768]{5,4,0,3,2,1:T(8,128)(2,1)S(1)}, u32[]{:S(2)}, u32[]{:S(2)}) %collective-permute-start.33) | collective-permute-done | bytes 589856 | tf_op jit(solution)/shard_map/ppermute | solution.py:44
  246.9 11.6 %collective-permute-done.36 = bf16[1,1,1,96,256]{4,3,2,1,0:T(8,128)(2,1)S(1)} collective-permute-done((bf16[1,1,1,96,256]{4,3,2,1,0:T(8,128)(2,1)S(1)}, bf16[1,1,1,96,256]{4,3,2,1,0:T(8,128)(2,1)S(1)}, u32[]{:S(2)}, u32[]{:S(2)}) %collective-permute-start.36) | collective-permute-done | bytes 49184 | tf_op jit(solution)/shard_map/ppermute | solution.py:44
  259.5 3.0 collective-permute-start.55
  262.7 4.3 %collective-permute-start.37 = (bf16[1,2,2,96,768]{4,3,2,1,0:T(8,128)(2,1)S(1)}, bf16[1,2,2,96,768]{4,3,2,1,0:T(8,128)(2,1)S(1)}, u32[]{:S(2)}, u32[]{:S(2)}) collective-permute-start(bf16[1,2,2,96,768]{4,3,2,1,0:T(8,128)(2,1)S(1)} %constant_dynamic-slice_fusion.3), channel_id=1, source_target_pairs={{0,16},{8,24},{16,0},{24,8},{1,17},{9,25},{17,1},{25,9},{2,18},{10... | collective-permute-start | bytes 1769480 | tf_op jit(solution)/shard_map/ppermute | solution.py:44
  270.3 4.2 %collective-permute-start.42 = (bf16[2,1,1,96,768]{4,3,2,1,0:T(8,128)(2,1)S(1)}, bf16[2,1,1,96,768]{4,3,2,1,0:T(8,128)(2,1)S(1)}, u32[]{:S(2)}, u32[]{:S(2)}) collective-permute-start(bf16[2,1,1,96,768]{4,3,2,1,0:T(8,128)(2,1)S(1)} %get-tuple-element.315), channel_id=1, source_target_pairs={{0,9},{1,8},{2,1},{3,0},{4,13},{5,12},{6,5},{7,4},{8,11},{9,10},{1... | collective-permute-start | bytes 884744 | tf_op jit(solution)/shard_map/ppermute | solution.py:60
  279.5 4.9 %collective-permute-start.40 = (bf16[2,1,1,96,768]{4,3,0,2,1:T(8,128)(2,1)S(1)}, bf16[2,1,1,96,768]{4,3,0,2,1:T(8,128)(2,1)S(1)}, u32[]{:S(2)}, u32[]{:S(2)}) collective-permute-start(bf16[2,1,1,96,768]{4,3,0,2,1:T(8,128)(2,1)S(1)} %get-tuple-element.317), channel_id=1, source_target_pairs={{0,1},{1,0},{2,9},{3,8},{4,5},{5,4},{6,13},{7,12},{8,3},{9,2},{10,... | collective-permute-start | bytes 884744 | tf_op jit(solution)/shard_map/ppermute | solution.py:60
  286.5 6.4 %collective-permute-start.45 = (bf16[512,192]{1,0:T(8,128)(2,1)S(1)}, bf16[512,192]{1,0:T(8,128)(2,1)S(1)}, u32[]{:S(2)}, u32[]{:S(2)}) collective-permute-start(bf16[512,192]{1,0:T(8,128)(2,1)S(1)} %get-tuple-element.336), channel_id=1, source_target_pairs={{0,0},{1,8},{2,2},{3,10},{4,4},{5,12},{6,6},{7,14},{8,1},{9,9},{10... | collective-permute-start | bytes 589832 | tf_op jit(solution)/shard_map/ppermute | solution.py:60
  292.8 14.2 %collective-permute-done.39 = bf16[2,1,1,96,768]{4,3,0,2,1:T(8,128)(2,1)S(1)} collective-permute-done((bf16[2,1,1,96,768]{4,3,0,2,1:T(8,128)(2,1)S(1)}, bf16[2,1,1,96,768]{4,3,0,2,1:T(8,128)(2,1)S(1)}, u32[]{:S(2)}, u32[]{:S(2)}) %collective-permute-start.39) | collective-permute-done | bytes 294944 | tf_op jit(solution)/shard_map/ppermute | solution.py:60
  308.0 4.9 %collective-permute-done.44 = bf16[1,2,1,96,768]{4,3,2,1,0:T(8,128)(2,1)S(1)} collective-permute-done((bf16[1,2,1,96,768]{4,3,2,1,0:T(8,128)(2,1)S(1)}, bf16[1,2,1,96,768]{4,3,2,1,0:T(8,128)(2,1)S(1)}, u32[]{:S(2)}, u32[]{:S(2)}) %collective-permute-start.44) | collective-permute-done | bytes 294944 | tf_op jit(solution)/shard_map/ppermute | solution.py:44
  314.2 6.5 %collective-permute-start.49 = (bf16[1,1,96,768]{3,2,1,0:T(8,128)(2,1)}, bf16[1,1,96,768]{3,2,1,0:T(8,128)(2,1)S(1)}, u32[]{:S(2)}, u32[]{:S(2)}) collective-permute-start(bf16[1,1,96,768]{3,2,1,0:T(8,128)(2,1)} %get-tuple-element.341), channel_id=1, source_target_pairs={{0,0},{1,1},{2,8},{3,9},{4,4},{5,5},{6,12},{7,13},{8,2},{9,3},{10,... | collective-permute-start | bytes 442376 | tf_op jit(solution)/shard_map/ppermute | solution.py:60
  327.4 4.7 %collective-permute-done.50 = bf16[1,1,96,768]{3,2,1,0:T(8,128)(2,1)} collective-permute-done((bf16[1,1,96,768]{3,2,1,0:T(8,128)(2,1)}, bf16[1,1,96,768]{3,2,1,0:T(8,128)(2,1)}, u32[]{:S(2)}, u32[]{:S(2)}) %collective-permute-start.50) | collective-permute-done | bytes 147488 | tf_op jit(solution)/shard_map/ppermute | solution.py:60
  (328 shorter events, 109.5 us)
Async XLA Ops:
  7.2 62.4 %all-gather.3.cloned.1.call-start = ((), (), s32[]{:S(2)}) async-start(), calls=%async_computation | async-start | bytes 1843200 | tf_op jit(solution)/shard_map/all_gather | solution.py:1044
  10.4 19.5 %collective-permute-start.4 = (bf16[800,768]{1,0:T(8,128)(2,1)}, bf16[800,768]{1,0:T(8,128)(2,1)}, u32[]{:S(2)}, u32[]{:S(2)}) collective-permute-start(bf16[800,768]{1,0:T(8,128)(2,1)} %dynamic-slice_bitcast_fusion.1), channel_id=1, source_target_pairs={{0,4},{2,6},{4,0},{6,2},{9,13},{11,15},{13,9},{15,11},{16,20},{18,... | collective-permute-start | bytes 3686408 | tf_op jit(solution)/shard_map/ppermute | solution.py:60
  12.4 15.6 %collective-permute-start = (bf16[96,640]{1,0:T(8,128)(2,1)S(1)}, bf16[96,640]{1,0:T(8,128)(2,1)S(1)}, u32[]{:S(2)}, u32[]{:S(2)}) collective-permute-start(bf16[96,640]{1,0:T(8,128)(2,1)S(1)} %pack_heads.1), channel_id=1, source_target_pairs={{0,0},{1,1},{2,8},{3,9},{4,4},{5,5},{6,12},{7,13},{8,2},{9,3},{10,... | collective-permute-start | bytes 368648 | tf_op jit(solution)/shard_map/ppermute | solution.py:60
  44.2 13.0 %collective-permute-start.10 = (bf16[1,2,2,96,640]{4,3,2,1,0:T(8,128)(2,1)S(1)}, bf16[1,2,2,96,640]{4,3,2,1,0:T(8,128)(2,1)S(1)}, u32[]{:S(2)}, u32[]{:S(2)}) collective-permute-start(bf16[1,2,2,96,640]{4,3,2,1,0:T(8,128)(2,1)S(1)} %pad_maximum_fusion.13), channel_id=1, source_target_pairs={{0,16},{8,24},{16,0},{24,8},{1,17},{9,25},{17,1},{25,9},{2,18},{10... | collective-permute-start | bytes 1474568 | tf_op jit(solution)/shard_map/ppermute | solution.py:44
  45.8 12.7 %collective-permute-start.9 = (bf16[2,2,1,96,640]{4,3,2,1,0:T(8,128)(2,1)S(1)}, bf16[2,2,1,96,640]{4,3,2,1,0:T(8,128)(2,1)S(1)}, u32[]{:S(2)}, u32[]{:S(2)}) collective-permute-start(bf16[2,2,1,96,640]{4,3,2,1,0:T(8,128)(2,1)S(1)} %pad_maximum_fusion.12), channel_id=1, source_target_pairs={{0,4},{4,0},{1,5},{5,1},{2,6},{6,2},{3,7},{7,3},{8,12},{12,8},{9,1... | collective-permute-start | bytes 1474568 | tf_op jit(solution)/shard_map/ppermute | solution.py:44
  77.9 24.9 %collective-permute-start.20 = (bf16[1,2,1,96,768]{4,3,2,1,0:T(8,128)(2,1)S(1)}, bf16[1,2,1,96,768]{4,3,2,1,0:T(8,128)(2,1)S(1)}, u32[]{:S(2)}, u32[]{:S(2)}) collective-permute-start(bf16[1,2,1,96,768]{4,3,2,1,0:T(8,128)(2,1)S(1)} %pad_maximum_fusion.14), channel_id=1, source_target_pairs={{0,16},{8,24},{16,0},{24,8},{1,17},{9,25},{17,1},{25,9},{2,18},{10... | collective-permute-start | bytes 884744 | tf_op jit(solution)/shard_map/ppermute | solution.py:44
  79.2 23.7 %collective-permute-start.19 = (bf16[1,2,1,96,768]{4,3,2,1,0:T(8,128)(2,1)S(1)}, bf16[1,2,1,96,768]{4,3,2,1,0:T(8,128)(2,1)S(1)}, u32[]{:S(2)}, u32[]{:S(2)}) collective-permute-start(bf16[1,2,1,96,768]{4,3,2,1,0:T(8,128)(2,1)S(1)} %pad_maximum_fusion.15), channel_id=1, source_target_pairs={{0,4},{4,0},{1,5},{5,1},{2,6},{6,2},{3,7},{7,3},{8,12},{12,8},{9,1... | collective-permute-start | bytes 884744 | tf_op jit(solution)/shard_map/ppermute | solution.py:44
  88.1 25.0 %collective-permute-start.18 = (bf16[2,2,1,96,1152]{4,3,2,1,0:T(8,128)(2,1)S(1)}, bf16[2,2,1,96,1152]{4,3,2,1,0:T(8,128)(2,1)S(1)}, u32[]{:S(2)}, u32[]{:S(2)}) collective-permute-start(bf16[2,2,1,96,1152]{4,3,2,1,0:T(8,128)(2,1)S(1)} %pad_maximum_fusion.9), channel_id=1, source_target_pairs={{0,4},{4,0},{1,5},{5,1},{2,6},{6,2},{3,7},{7,3},{8,12},{12,8},{9,1... | collective-permute-start | bytes 2654216 | tf_op jit(solution)/shard_map/ppermute | solution.py:44
  93.0 20.1 %collective-permute-start.17 = (bf16[1,2,2,96,1152]{4,3,2,1,0:T(8,128)(2,1)S(1)}, bf16[1,2,2,96,1152]{4,3,2,1,0:T(8,128)(2,1)S(1)}, u32[]{:S(2)}, u32[]{:S(2)}) collective-permute-start(bf16[1,2,2,96,1152]{4,3,2,1,0:T(8,128)(2,1)S(1)} %pad_maximum_fusion.8), channel_id=1, source_target_pairs={{0,16},{8,24},{16,0},{24,8},{1,17},{9,25},{17,1},{25,9},{2,18},{10... | collective-permute-start | bytes 2654216 | tf_op jit(solution)/shard_map/ppermute | solution.py:44
  118.3 15.0 %collective-permute-start.23 = (bf16[2,2,1,96,768]{4,3,2,1,0:T(8,128)(2,1)S(1)}, bf16[2,2,1,96,768]{4,3,2,1,0:T(8,128)(2,1)S(1)}, u32[]{:S(2)}, u32[]{:S(2)}) collective-permute-start(bf16[2,2,1,96,768]{4,3,2,1,0:T(8,128)(2,1)S(1)} %pad_maximum_fusion.11), channel_id=1, source_target_pairs={{0,4},{4,0},{1,5},{5,1},{2,6},{6,2},{3,7},{7,3},{8,12},{12,8},{9,1... | collective-permute-start | bytes 1769480 | tf_op jit(solution)/shard_map/ppermute | solution.py:44
  119.2 14.7 %collective-permute-start.22 = (bf16[1,2,2,96,768]{4,3,2,1,0:T(8,128)(2,1)S(1)}, bf16[1,2,2,96,768]{4,3,2,1,0:T(8,128)(2,1)S(1)}, u32[]{:S(2)}, u32[]{:S(2)}) collective-permute-start(bf16[1,2,2,96,768]{4,3,2,1,0:T(8,128)(2,1)S(1)} %pad_maximum_fusion.10), channel_id=1, source_target_pairs={{0,16},{8,24},{16,0},{24,8},{1,17},{9,25},{17,1},{25,9},{2,18},{10... | collective-permute-start | bytes 1769480 | tf_op jit(solution)/shard_map/ppermute | solution.py:44
  169.2 43.3 %collective-permute-start.26 = (bf16[2,384,768]{2,1,0:T(8,128)(2,1)}, bf16[2,384,768]{2,1,0:T(8,128)(2,1)}, u32[]{:S(2)}, u32[]{:S(2)}) collective-permute-start(bf16[2,384,768]{2,1,0:T(8,128)(2,1)} %get-tuple-element.197), channel_id=1, source_target_pairs={{0,4},{4,0},{1,5},{5,1},{2,6},{6,2},{3,7},{7,3},{8,12},{12,8},{9,1... | collective-permute-start | bytes 3538952 | tf_op jit(solution)/shard_map/ppermute | solution.py:44
  170.1 42.5 %collective-permute-start.27 = (bf16[2,384,768]{2,1,0:T(8,128)(2,1)}, bf16[2,384,768]{2,1,0:T(8,128)(2,1)}, u32[]{:S(2)}, u32[]{:S(2)}) collective-permute-start(bf16[2,384,768]{2,1,0:T(8,128)(2,1)} %get-tuple-element.198), channel_id=1, source_target_pairs={{0,16},{8,24},{16,0},{24,8},{1,17},{9,25},{17,1},{25,9},{2,18},{10... | collective-permute-start | bytes 3538952 | tf_op jit(solution)/shard_map/ppermute | solution.py:44
  187.3 25.3 %collective-permute-start.29 = (f32[256,128]{1,0:T(8,128)S(1)}, f32[256,128]{1,0:T(8,128)S(1)}, u32[]{:S(2)}, u32[]{:S(2)}) collective-permute-start(f32[256,128]{1,0:T(8,128)S(1)} %get-tuple-element.350), channel_id=1, source_target_pairs={{0,0},{1,8},{2,1},{3,9},{4,4},{5,12},{6,5},{7,13},{8,2},{9,10},{10... | collective-permute-start | bytes 393224 | tf_op jit(solution)/shard_map/ppermute | solution.py:60
  191.8 20.9 %collective-permute-start.30 = (f32[256,128]{1,0:T(8,128)S(1)}, f32[256,128]{1,0:T(8,128)S(1)}, u32[]{:S(2)}, u32[]{:S(2)}) collective-permute-start(f32[256,128]{1,0:T(8,128)S(1)} %get-tuple-element.349), channel_id=1, source_target_pairs={{0,1},{1,9},{2,0},{3,8},{4,5},{5,13},{6,4},{7,12},{8,3},{9,11},{10... | collective-permute-start | bytes 393224 | tf_op jit(solution)/shard_map/ppermute | solution.py:60
  192.0 20.5 %collective-permute-start.28 = (bf16[1,1,2,96,256]{4,3,2,1,0:T(8,128)(2,1)S(1)}, bf16[1,1,2,96,256]{4,3,2,1,0:T(8,128)(2,1)S(1)}, u32[]{:S(2)}, u32[]{:S(2)}) collective-permute-start(bf16[1,1,2,96,256]{4,3,2,1,0:T(8,128)(2,1)S(1)} %constant_dynamic-slice_fusion.7), channel_id=1, source_target_pairs={{0,16},{8,24},{16,0},{24,8},{1,17},{9,25},{17,1},{25,9},{2,18},{10... | collective-permute-start | bytes 294920 | tf_op jit(solution)/shard_map/ppermute | solution.py:44
  221.5 19.5 %collective-permute-start.34 = (bf16[2,1,2,1,96,768]{5,4,0,3,2,1:T(8,128)(2,1)S(1)}, bf16[2,1,2,1,96,768]{5,4,0,3,2,1:T(8,128)(2,1)S(1)}, u32[]{:S(2)}, u32[]{:S(2)}) collective-permute-start(bf16[2,1,2,1,96,768]{5,4,0,3,2,1:T(8,128)(2,1)S(1)} %constant_dynamic-slice_fusion.5), channel_id=1, source_target_pairs={{0,4},{4,0},{1,5},{5,1},{2,6},{6,2},{3,7},{7,3},{8,12},{12,8},{9,1... | collective-permute-start | bytes 1769480 | tf_op jit(solution)/shard_map/ppermute | solution.py:44
  230.8 15.9 %collective-permute-start.32 = (bf16[512,768]{1,0:T(8,128)(2,1)S(1)}, bf16[512,768]{1,0:T(8,128)(2,1)S(1)}, u32[]{:S(2)}, u32[]{:S(2)}) collective-permute-start(bf16[512,768]{1,0:T(8,128)(2,1)S(1)} %get-tuple-element.217), channel_id=1, source_target_pairs={{0,8},{8,0},{16,24},{24,16},{1,9},{9,1},{17,25},{25,17},{2,10},{10... | collective-permute-start | bytes 2359304 | tf_op jit(solution)/shard_map/ppermute | solution.py:44
  231.7 15.0 %collective-permute-start.33 = (bf16[2,1,2,1,96,768]{5,4,0,3,2,1:T(8,128)(2,1)S(1)}, bf16[2,1,2,1,96,768]{5,4,0,3,2,1:T(8,128)(2,1)S(1)}, u32[]{:S(2)}, u32[]{:S(2)}) collective-permute-start(bf16[2,1,2,1,96,768]{5,4,0,3,2,1:T(8,128)(2,1)S(1)} %constant_dynamic-slice_fusion.6), channel_id=1, source_target_pairs={{0,16},{8,24},{16,0},{24,8},{1,17},{9,25},{17,1},{25,9},{2,18},{10... | collective-permute-start | bytes 1769480 | tf_op jit(solution)/shard_map/ppermute | solution.py:44
  232.6 26.3 %collective-permute-start.35 = (bf16[512,768]{1,0:T(8,128)(2,1)S(1)}, bf16[512,768]{1,0:T(8,128)(2,1)S(1)}, u32[]{:S(2)}, u32[]{:S(2)}) collective-permute-start(bf16[512,768]{1,0:T(8,128)(2,1)S(1)} %add_convert_fusion.3), channel_id=1, source_target_pairs={{0,4},{4,0},{1,5},{5,1},{2,6},{6,2},{3,7},{7,3},{8,12},{12,8},{9,1... | collective-permute-start | bytes 2359304 | tf_op jit(solution)/shard_map/ppermute | solution.py:44
  233.5 25.0 %collective-permute-start.36 = (bf16[1,1,1,96,256]{4,3,2,1,0:T(8,128)(2,1)S(1)}, bf16[1,1,1,96,256]{4,3,2,1,0:T(8,128)(2,1)S(1)}, u32[]{:S(2)}, u32[]{:S(2)}) collective-permute-start(bf16[1,1,1,96,256]{4,3,2,1,0:T(8,128)(2,1)S(1)} %constant_dynamic-slice_fusion.4), channel_id=1, source_target_pairs={{0,4},{4,0},{1,5},{5,1},{2,6},{6,2},{3,7},{7,3},{8,12},{12,8},{9,1... | collective-permute-start | bytes 147464 | tf_op jit(solution)/shard_map/ppermute | solution.py:44
  259.5 15.0 %collective-permute-start.55 = (bf16[96,256]{1,0:T(8,128)(2,1)S(1)}, bf16[96,256]{1,0:T(8,128)(2,1)S(1)}, u32[]{:S(2)}, u32[]{:S(2)}) collective-permute-start(bf16[96,256]{1,0:T(8,128)(2,1)S(1)} %fusion.2), channel_id=1, source_target_pairs={{0,3},{1,2},{2,1},{3,0},{4,7},{5,6},{6,5},{7,4},{8,11},{9,10},{10,... | collective-permute-start | bytes 147464 | tf_op jit(solution)/shard_map/ppermute | solution.py:44
  262.7 16.8 %collective-permute-start.37 = (bf16[1,2,2,96,768]{4,3,2,1,0:T(8,128)(2,1)S(1)}, bf16[1,2,2,96,768]{4,3,2,1,0:T(8,128)(2,1)S(1)}, u32[]{:S(2)}, u32[]{:S(2)}) collective-permute-start(bf16[1,2,2,96,768]{4,3,2,1,0:T(8,128)(2,1)S(1)} %constant_dynamic-slice_fusion.3), channel_id=1, source_target_pairs={{0,16},{8,24},{16,0},{24,8},{1,17},{9,25},{17,1},{25,9},{2,18},{10... | collective-permute-start | bytes 1769480 | tf_op jit(solution)/shard_map/ppermute | solution.py:44
  267.1 17.4 %collective-permute-start.38 = (bf16[2,2,1,96,768]{4,3,2,1,0:T(8,128)(2,1)S(1)}, bf16[2,2,1,96,768]{4,3,2,1,0:T(8,128)(2,1)S(1)}, u32[]{:S(2)}, u32[]{:S(2)}) collective-permute-start(bf16[2,2,1,96,768]{4,3,2,1,0:T(8,128)(2,1)S(1)} %constant_dynamic-slice_fusion.2), channel_id=1, source_target_pairs={{0,4},{4,0},{1,5},{5,1},{2,6},{6,2},{3,7},{7,3},{8,12},{12,8},{9,1... | collective-permute-start | bytes 1769480 | tf_op jit(solution)/shard_map/ppermute | solution.py:44
  269.0 15.8 %collective-permute-start.41 = (bf16[2,1,1,96,768]{4,3,0,2,1:T(8,128)(2,1)S(1)}, bf16[2,1,1,96,768]{4,3,0,2,1:T(8,128)(2,1)S(1)}, u32[]{:S(2)}, u32[]{:S(2)}) collective-permute-start(bf16[2,1,1,96,768]{4,3,0,2,1:T(8,128)(2,1)S(1)} %get-tuple-element.316), channel_id=1, source_target_pairs={{0,8},{1,9},{2,0},{3,1},{4,12},{5,13},{6,4},{7,5},{8,10},{9,11},{1... | collective-permute-start | bytes 884744 | tf_op jit(solution)/shard_map/ppermute | solution.py:60
  270.3 16.1 %collective-permute-start.42 = (bf16[2,1,1,96,768]{4,3,2,1,0:T(8,128)(2,1)S(1)}, bf16[2,1,1,96,768]{4,3,2,1,0:T(8,128)(2,1)S(1)}, u32[]{:S(2)}, u32[]{:S(2)}) collective-permute-start(bf16[2,1,1,96,768]{4,3,2,1,0:T(8,128)(2,1)S(1)} %get-tuple-element.315), channel_id=1, source_target_pairs={{0,9},{1,8},{2,1},{3,0},{4,13},{5,12},{6,5},{7,4},{8,11},{9,10},{1... | collective-permute-start | bytes 884744 | tf_op jit(solution)/shard_map/ppermute | solution.py:60
  274.5 32.5 %collective-permute-start.39 = (bf16[2,1,1,96,768]{4,3,0,2,1:T(8,128)(2,1)S(1)}, bf16[2,1,1,96,768]{4,3,0,2,1:T(8,128)(2,1)S(1)}, u32[]{:S(2)}, u32[]{:S(2)}) collective-permute-start(bf16[2,1,1,96,768]{4,3,0,2,1:T(8,128)(2,1)S(1)} %get-tuple-element.318), channel_id=1, source_target_pairs={{0,0},{1,1},{2,8},{3,9},{4,4},{5,5},{6,12},{7,13},{8,2},{9,3},{10,... | collective-permute-start | bytes 884744 | tf_op jit(solution)/shard_map/ppermute | solution.py:60
  279.5 27.5 %collective-permute-start.40 = (bf16[2,1,1,96,768]{4,3,0,2,1:T(8,128)(2,1)S(1)}, bf16[2,1,1,96,768]{4,3,0,2,1:T(8,128)(2,1)S(1)}, u32[]{:S(2)}, u32[]{:S(2)}) collective-permute-start(bf16[2,1,1,96,768]{4,3,0,2,1:T(8,128)(2,1)S(1)} %get-tuple-element.317), channel_id=1, source_target_pairs={{0,1},{1,0},{2,9},{3,8},{4,5},{5,4},{6,13},{7,12},{8,3},{9,2},{10,... | collective-permute-start | bytes 884744 | tf_op jit(solution)/shard_map/ppermute | solution.py:60
  284.4 37.0 %collective-permute-start.46 = (bf16[512,192]{1,0:T(8,128)(2,1)S(1)}, bf16[512,192]{1,0:T(8,128)(2,1)S(1)}, u32[]{:S(2)}, u32[]{:S(2)}) collective-permute-start(bf16[512,192]{1,0:T(8,128)(2,1)S(1)} %get-tuple-element.338), channel_id=1, source_target_pairs={{0,1},{1,9},{2,3},{3,11},{4,5},{5,13},{6,7},{7,15},{8,0},{9,8},{10... | collective-permute-start | bytes 589832 | tf_op jit(solution)/shard_map/ppermute | solution.py:60
  284.8 36.6 %collective-permute-start.47 = (bf16[512,192]{1,0:T(8,128)(2,1)S(1)}, bf16[512,192]{1,0:T(8,128)(2,1)S(1)}, u32[]{:S(2)}, u32[]{:S(2)}) collective-permute-start(bf16[512,192]{1,0:T(8,128)(2,1)S(1)} %get-tuple-element.337), channel_id=1, source_target_pairs={{0,2},{1,10},{2,0},{3,8},{4,6},{5,14},{6,4},{7,12},{8,3},{9,11},{1... | collective-permute-start | bytes 589832 | tf_op jit(solution)/shard_map/ppermute | solution.py:60
  286.5 37.0 %collective-permute-start.45 = (bf16[512,192]{1,0:T(8,128)(2,1)S(1)}, bf16[512,192]{1,0:T(8,128)(2,1)S(1)}, u32[]{:S(2)}, u32[]{:S(2)}) collective-permute-start(bf16[512,192]{1,0:T(8,128)(2,1)S(1)} %get-tuple-element.336), channel_id=1, source_target_pairs={{0,0},{1,8},{2,2},{3,10},{4,4},{5,12},{6,6},{7,14},{8,1},{9,9},{10... | collective-permute-start | bytes 589832 | tf_op jit(solution)/shard_map/ppermute | solution.py:60
  314.2 13.2 %collective-permute-start.49 = (bf16[1,1,96,768]{3,2,1,0:T(8,128)(2,1)}, bf16[1,1,96,768]{3,2,1,0:T(8,128)(2,1)S(1)}, u32[]{:S(2)}, u32[]{:S(2)}) collective-permute-start(bf16[1,1,96,768]{3,2,1,0:T(8,128)(2,1)} %get-tuple-element.341), channel_id=1, source_target_pairs={{0,0},{1,1},{2,8},{3,9},{4,4},{5,5},{6,12},{7,13},{8,2},{9,3},{10,... | collective-permute-start | bytes 442376 | tf_op jit(solution)/shard_map/ppermute | solution.py:60
  (93 other events, 658.5 us)
Sparse Core Ops, SparseCore 0:
  30.6 35.3 all-gather.2

commit v4 on v3

--- a/solution.py
+++ b/solution.py
@@ -323,6 +323,10 @@
     def _():
         dk_ref[...] = dk_acc[...].astype(dk_ref.dtype)
         dv_ref[...] = dv_acc[...].astype(dv_ref.dtype)
+
+
+def in_hbm(*arrays):
+    return [pltpu.with_memory_space_constraint(a, pltpu.HBM) for a in arrays]
 
 
 def params(mib):
@@ -785,11 +789,11 @@
                 pltpu.VMEM((width, cols), jnp.float32),
             ],
         ),
-        out_shape=[shape] * 4 + [jax.ShapeDtypeStruct((rows, width), low)],
+        out_shape=[pltpu.HBM(shape.shape, low)] * 4 + [jax.ShapeDtypeStruct((rows, width), low)],
         compiler_params=params(VMEM_MIB),
         cost_estimate=cost(17e-6),
         name="ffn_back",
-    )(bits, grad, x, act, slope, *inner, *outer)
+    )(bits, grad, *in_hbm(x, act, slope, *inner, *outer))
 
 
 def first_back_kernel(
@@ -870,7 +874,7 @@
             full_spec((width, p_width + 128)),
         ],
         out_shape=[
-            jax.ShapeDtypeStruct((rows, width), jnp.float32),
+            pltpu.HBM((rows, width), jnp.float32),
             jax.ShapeDtypeStruct((rows, cols), low),
             jax.ShapeDtypeStruct((width, cols), low),
             jax.ShapeDtypeStruct((width, p_width + 128), low),
@@ -879,7 +883,7 @@
         compiler_params=params(VMEM_MIB),
         cost_estimate=cost(1e-6),
         name="first_back",
-    )(mine, got, grad_h2, normed, inv, norms, output_w, *mixed, proj_part, vec2)
+    )(mine, got, *in_hbm(grad_h2, normed, inv), norms, *in_hbm(output_w, *mixed, proj_part), vec2)
 
 
 def token_grads_kernel(core, *refs):
@@ -932,7 +936,7 @@
 
 
 def head_grads_kernel(x_ref, *refs):
-    *parts, og_ref, a_ref, b_ref, acc = refs
+    *parts, og_ref, twos, thirds, acc = refs
     step = pl.program_id(0)
     steps = pl.num_programs(0)
 
@@ -952,18 +956,18 @@
 
     @pl.when(step == steps - 1)
     def _():
-        for s, out in enumerate((a_ref, b_ref)):
+        for s in range(2):
             for i in range(4):
                 part = og_ref if i == 3 else acc.at[i]
                 lo = 128 * s
-                out[:, 128 * i : 128 * i + 128] = part[:, lo : lo + 128].astype(out.dtype)
+                twos[s, :, 128 * i : 128 * i + 128] = part[:, lo : lo + 128].astype(twos.dtype)
             for i in (0, 2):
                 lo = 256 + DH * s
                 both = [
-                    (og_ref if j == 3 else acc.at[j])[:, lo : lo + DH].astype(out.dtype)
+                    (og_ref if j == 3 else acc.at[j])[:, lo : lo + DH].astype(thirds.dtype)
                     for j in (i, i + 1)
                 ]
-                out[:, 512 + DH * i : 512 + DH * i + 128] = jnp.concatenate(both, axis=1)
+                thirds[s, :, DH * i : DH * i + 128] = jnp.concatenate(both, axis=1)
 
 
 def head_grads(tok_all, grads, output_part):
@@ -975,28 +979,53 @@
     for dq, _, _ in grads:
         cols = dq.shape[1]
         specs += [pl.BlockSpec((block, cols), near), rows_spec(block, cols), rows_spec(block, cols)]
-    packed = full_spec((width, 768))
-    shape = jax.ShapeDtypeStruct((width, 768), jnp.bfloat16)
     return pl.pallas_call(
         head_grads_kernel,
         grid=(steps,),
         in_specs=[rows_spec(block, width)] + specs + [full_spec(output_part.shape)],
-        out_specs=[packed, packed],
-        out_shape=[shape, shape],
+        out_specs=[full_spec((2, width, 512)), full_spec((2, width, 256))],
+        out_shape=[
+            jax.ShapeDtypeStruct((2, width, 512), jnp.bfloat16),
+            jax.ShapeDtypeStruct((2, width, 256), jnp.bfloat16),
+        ],
         scratch_shapes=[pltpu.VMEM((3, width, 384), jnp.float32)],
         compiler_params=params(VMEM_MIB),
         cost_estimate=cost(0.5e-6),
         name="head_grads",
-    )(tok_all, *[x for arrays in grads for x in arrays], output_part)
-
-
-def unpack_heads(packed):
-    return [
-        jnp.concatenate(
-            [packed[:, 128 * i : 128 * i + 128], packed[:, 512 + DH * i : 512 + DH * i + DH]], axis=1
-        )
-        for i in range(4)
-    ]
+    )(*in_hbm(tok_all), *[x for arrays in grads for x in arrays], output_part)
+
+
+def finish_kernel(p0, p1, p2, p3, small, q_ref, k_ref, v_ref, o_ref, proj_ref, vec_ref):
+    total = (wide(p0) + wide(p1)) + (wide(p2) + wide(p3))
+    rows = total.shape[0]
+
+    def part(i):
+        third = total[:, 512 + DH * i : 512 + DH * i + DH]
+        return jnp.concatenate([total[:, 128 * i : 128 * i + 128], third], axis=1)
+
+    def turned(block):
+        pad = jnp.zeros((128 - rows, block.shape[1]), block.dtype)
+        return jnp.concatenate([block, pad], axis=0).T[:, :rows]
+
+    for i, out in enumerate((q_ref, k_ref, v_ref)):
+        out[...] = part(i)
+    o_ref[:128, :] = turned(total[:, 384:512])
+    o_ref[128:, :] = turned(total[:, 640:768])[DH:, :]
+    sums = wide(small)
+    proj_ref[...] = sums[:, :128]
+    vec_ref[...] = turned(sums[:, 128:])[:8, :]
+
+
+def finish(parts, small):
+    rows = parts[0].shape[0]
+    shapes = [(rows, 192)] * 3 + [(192, rows), (rows, 128), (8, rows)]
+    return pl.pallas_call(
+        finish_kernel,
+        out_shape=[jax.ShapeDtypeStruct(s, jnp.float32) for s in shapes],
+        compiler_params=params(16),
+        cost_estimate=cost(2e-6),
+        name="finish",
+    )(*parts, small)
 
 
 def per_device(
@@ -1138,7 +1167,7 @@
         part, part_got, grad_h2, normed, inv, norms, output_w, mixed, proj_part, vec2
     )
 
-    small = lax.dynamic_slice_in_dim(split_rows(small), core, 1, core_dim)
+    small = split_rows(small)
     small_got = scatter_start(small, "y")
     quarter = half // 2
     emb_half = lax.dynamic_slice_in_dim(after(embedding, grad_mixed), core * half, half, 0)
@@ -1159,9 +1188,6 @@
     def added(kept, got):
         return (kept.astype(f32) + got.astype(f32)).astype(bf16)
 
-    theirs, far_mine = token_grads(core, True, grads, heads_a, heads_b)
-    far_got = swap(theirs, "shard", 1)
-    wgrad_got = after_all(theirs, *wgrad_got)
     lead = (2,) * (shard_bits() - 1)
     last = (rows, hidden_cols)
     shapes = [(2, *lead, 2, 1, *last), (2, 1, *lead[1:], 2, 2, *last)]
@@ -1171,68 +1197,90 @@
         added(keep_b, wgrad_got[1]).reshape(shapes[1]),
     ]
     wgrad = [scatter_rest(w, "y", 1) if n == "x" else w for w, n in zip(wgrad, second_steps)]
-    far_got, *wgrad = tie(far_got, *wgrad)
+    small = scatter_finish(small, small_got, "y")
+    *wgrad, small, dq, dk, dv = tie(*wgrad, small, *grads[0])
+    grads = [[dq, dk, dv]]
+    wgrad_got = [scatter_start(w, n, 1) for w, n in zip(wgrad, second_steps)]
+    small_got = scatter_start(small, "x")
+
+    far_theirs, far_mine = token_grads(core, True, grads, heads_a, heads_b)
+    near_theirs, near_mine = token_grads(core, False, grads, heads_a, heads_b)
+    far_theirs, near_theirs, tok_in = tie(far_theirs, near_theirs, tok_all)
+    far_got = swap(far_theirs, "shard", 1)
+    near_got = swap(near_theirs, "shard", 1)
+    twos, thirds = head_grads(tok_in, grads, output_part)
+    twos, thirds, far_got, near_got, small_got, *wgrad_got = tie(
+        twos, thirds, far_got, near_got, small_got, *wgrad_got
+    )
     far_sum = added(far_mine, far_got)
     from_far = swap(far_sum, "ctx", 1)
-    wgrad_got = [scatter_start(w, n, 1) for w, n in zip(after_all(far_sum, *wgrad), second_steps)]
-    small = scatter_finish(small, after(small_got, far_sum), "y")
-    small_got = scatter_start(small, "x")
-    theirs, near_mine = token_grads(core, False, grads, after(heads_a, far_sum, *wgrad), heads_b)
-    near_got = swap(theirs, "shard", 1)
-    grad_a, grad_b = head_grads(after(tok_all, theirs), grads, output_part)
-    grad_a, grad_b, near_got, *wgrad_got = tie(grad_a, grad_b, near_got, *wgrad_got)
-    grad_a, grad_b = split_rows(grad_a), split_rows(grad_b)
-    got_a, got_b = scatter_start(grad_a, "y"), scatter_start(grad_b, "x")
     wgrad = [scatter_finish(w, g, n, 1) for w, g, n in zip(wgrad, wgrad_got, second_steps)]
+    blocks = jnp.stack([w.reshape(2, 2, rows, hidden_cols) for w in wgrad], axis=0)
+    wgrad_theirs = swap(lax.dynamic_index_in_dim(blocks, 1 - core, 2, False), "shard", 1)
+    twos, thirds = split_rows(twos), split_rows(thirds)
+    twos_got, thirds_got = scatter_start(twos, "y", 1), scatter_start(thirds, "x", 1)
     mine = lax.dynamic_slice_in_dim(grad_h1, core * half, half, 0)
     near_sum = near_mine.astype(f32) + near_got.astype(f32) + mine
-    small = scatter_finish(small, after(small_got, near_sum), "x").reshape(-1, small.shape[-1])
-    near_sum, from_far, small, *wgrad = tie(near_sum, from_far, small, *wgrad)
+    small = scatter_finish(small, small_got, "x")
+    near_sum, wgrad_theirs, small = tie(near_sum, wgrad_theirs, small)
+    ours = lax.dynamic_index_in_dim(blocks, core, 2, False)
+    blocks = by_core(ours, wgrad_theirs, 0).reshape(4, 2 * rows, hidden_cols)
+    small = lax.dynamic_index_in_dim(small.reshape(2, rows, -1), core, 0, False)
+    extra = small.reshape(1, -1, hidden_cols)
+    blocks = jnp.concatenate([blocks, jnp.concatenate([extra] * 4, axis=0)], axis=1)
+    wgrad_sum = lax.psum_scatter(blocks, "tp", scatter_dimension=0)
+    near_sum, from_far, twos_got, thirds_got = tie(near_sum, from_far, twos_got, thirds_got)
     grad_tok = (near_sum + from_far.astype(f32)).astype(bf16)
-    wgrad_parts = scatter_tp_start(*wgrad)
+
     own_cols = model_width // lax.axis_size("tp")
-    col_parts = [grad_tok[:, own_cols * j : own_cols * (j + 1)] for j in range(4)]
-    place = 2 * micro + core
+    cols = [grad_tok[:, own_cols * j : own_cols * (j + 1)] for j in range(4)]
+    even, odd = jnp.stack(cols[0::2]), jnp.stack(cols[1::2])
+    kept = jnp.where(core == 0, even, odd)
+    other = swap(jnp.where(core == 0, odd, even), "shard", 1)
+    twos = scatter_finish(twos, twos_got, "y", 1)
+    thirds = scatter_finish(thirds, thirds_got, "x", 1)
+    twos_got, thirds_got = scatter_start(twos, "x", 1), scatter_start(thirds, "y", 1)
+    both = [jnp.where(core == 0, kept, other), jnp.where(core == 0, other, kept)]
+    both = [jnp.concatenate([both[0][j], both[1][j]], axis=0) for j in range(2)]
     arrived = [
         route(
-            lax.select_n(place ^ d, *col_parts),
-            lambda s, c, t, d=d: (s - s % 2 + t % 2, c, (2 * (t // 2) + s % 2) ^ d),
+            lax.select_n(micro ^ d, *both),
+            lambda s, c, t, d=d: (s - s % 2 + t % 2, c, 2 * ((t // 2) ^ d) + s % 2),
         )
-        for d in range(4)
+        for d in range(2)
     ]
-    small_parts = [small] + [swap(small, "tp", d) for d in range(1, 4)]
-    got_a, got_b = after_all(grad_tok, got_a, got_b)
-    grad_a, grad_b = scatter_finish(grad_a, got_a, "y"), scatter_finish(grad_b, got_b, "x")
-    got_a, got_b = scatter_start(grad_a, "x"), scatter_start(grad_b, "y")
-    wgrad_parts = after_all((grad_a, grad_b), *wgrad_parts)
-    wgrad_sum = sum_all(wgrad_parts).reshape(2, -1, hidden_cols)
-    outer_grad, inner_grad = wgrad_sum[0].T, wgrad_sum[1]
-    small = sum_all(small_parts)
+    twos = scatter_finish(twos, twos_got, "x", 1)
+    thirds = scatter_finish(thirds, thirds_got, "y", 1)
+    pieces = jnp.concatenate([twos, thirds], axis=-1).reshape(2, 2, rows, -1)
+    theirs = swap(lax.dynamic_index_in_dim(pieces, 1 - core, 1, False), "shard", 1)
+    ours = lax.dynamic_index_in_dim(pieces, core, 1, False)
+    pieces = by_core(ours, theirs, 0)
+    wgrad_sum, pieces = tie(wgrad_sum, pieces)
+    parts = [lax.dynamic_index_in_dim(pieces, group ^ d, 0, False) for d in range(4)]
+    parts = parts[:1] + [swap(parts[d], "tp", d) for d in range(1, 4)]
+    *parts, arrived[0], arrived[1] = tie(*parts, *arrived)
+    outer_grad = wgrad_sum[:rows].astype(f32).T
+    inner_grad = wgrad_sum[rows : 2 * rows].astype(f32)
+    small = wgrad_sum[2 * rows :].reshape(rows, -1)
     embeddings = jnp.stack([lax.select_n((group % 2) ^ m, *emb_got) for m in range(2)])
     embeddings = embeddings.reshape(2, 1, quarter, -1)
-    got_a, got_b = after_all(inner_grad, got_a, got_b)
-    grad_a, grad_b = scatter_finish(grad_a, got_a, "x"), scatter_finish(grad_b, got_b, "y")
-    arrived = after_all((grad_a, grad_b), *arrived)
-    heads_grad = sum_all(scatter_tp_start(grad_a, grad_b))
-    heads_grad = heads_grad.reshape(-1, heads_grad.shape[-1])
-    grad_tokens = jnp.stack([lax.select_n(group ^ j, *arrived) for j in range(4)])
+    grad_tokens = jnp.stack([lax.select_n(m ^ micro, *arrived) for m in range(2)])
     grad_tokens = grad_tokens.reshape(2, 1, length, own_cols).astype(f32)
-    query_grad, key_grad, value_grad, output_grad = unpack_heads(heads_grad)
-    p_width = proj_part.shape[1]
+    query_grad, key_grad, value_grad, output_grad, proj_grad, norm_grads = finish(parts, small)
     return (
         embeddings,
         grad_tokens,
         query_grad,
         key_grad,
         value_grad,
-        output_grad.T,
-        small[:, p_width],
-        small[:, p_width + 1],
+        output_grad,
+        norm_grads[0],
+        norm_grads[1],
         inner_grad,
         outer_grad,
-        small[:, p_width + 2],
-        small[:, p_width + 3],
-        small[:, :p_width],
+        norm_grads[2],
+        norm_grads[3],
+        proj_grad,
     )
 
 

time: 349 us -> 340 us (0.974)
  starting transfers between devices: 92.2 us -> 74.2 us
  Pallas kernels: 98.7 us -> 106 us
  local copies, waits for them, and re-layouts: 35.9 us -> 31.9 us
    ppermute x19 -> x9, starting transfers between devices: 47.4 us -> 22.7 us  [route(): return lax.ppermute(v, ('shard', 'ctx', 'tp'), pairs)]
    unnamed x138 -> x145, local copies, waits for them, and re-layouts: 26.5 us -> 17.7 us
    ppermute x37 -> x40, starting transfers between devices: 44.8 us -> 51.5 us  [swap(): return lax.ppermute(v, axis, [(i, i ^ bit) for i in range(count)])]
    ppermute x37 -> x40, waiting for transfers between devices: 56.9 us -> 62.4 us  [swap(): return lax.ppermute(v, axis, [(i, i ^ bit) for i in range(count)])]
    ppermute x19 -> x9, waiting for transfers between devices: 21.3 us -> 17.8 us  [route(): return lax.ppermute(v, ('shard', 'ctx', 'tp'), pairs)]
  transfers between devices with their start and end apart: 57 -> 51, of which waited for: 21 -> 18; matrix products, arithmetic and copies ran while one was open for 7% -> 8% of each run, Pallas kernels for 20% -> 20%
where the time goes in v4:
time: 340 us; the launch traced here: 334 us
  Pallas kernels  106 us (31%)
  waiting for transfers between devices  80.3 us (24%)
  starting transfers between devices  74.2 us (22%)
  local copies, waits for them, and re-layouts  31.9 us (9%)
  other arithmetic  25.6 us (8%)
  between operations  15.8 us (5%)
    ppermute x40, waiting for transfers between devices, swap(): return lax.ppermute(v, axis, [(i, i ^ bit) for i in range(count)])  62.4 us
    ppermute x40, starting transfers between devices, swap(): return lax.ppermute(v, axis, [(i, i ^ bit) for i in range(count)])  51.5 us
    ppermute x9, starting transfers between devices, route(): return lax.ppermute(v, ('shard', 'ctx', 'tp'), pairs)  22.7 us
    pallas_call x1, Pallas kernels, attn_backward(): pl.pallas_call(attn_bwd_kernel, grid_spec=pltpu.PrefetchScalarGridSpec(nu...  18.3 us
    pallas_call x1, Pallas kernels, ffn_back(): pl.pallas_call(functools.partial(ffn_back_kernel, turns), grid_spec=pltpu...  18.1 us
    ppermute x9, waiting for transfers between devices, route(): return lax.ppermute(v, ('shard', 'ctx', 'tp'), pairs)  17.8 us
    pallas_call x2, Pallas kernels, attn_forward(): pl.pallas_call(functools.partial(attn_fwd_kernel, first_block), grid_spec...  17.8 us
    unnamed x145, local copies, waits for them, and re-layouts  17.7 us
  transfers between devices with their start and end apart: 51, of which 18 were waited for; matrix products, arithmetic and copies ran while one was open for 8% of the time, Pallas kernels for 20%

profile of v4, /device:TPU:1, one launch (start us, length us, event | category | flops | bytes accessed | tf_op | source)
XLA Modules:
  0.0 334.2 jit_solution(7758511959684497071)
XLA Ops:
  12.4 7.3 %collective-permute-start = (bf16[96,640]{1,0:T(8,128)(2,1)S(1)}, bf16[96,640]{1,0:T(8,128)(2,1)S(1)}, u32[]{:S(2)}, u32[]{:S(2)}) collective-permute-start(bf16[96,640]{1,0:T(8,128)(2,1)S(1)} %pack_heads.1), channel_id=1, source_target_pairs={{0,0},{1,1},{2,8},{3,9},{4,4},{5,5},{6,12},{7,13},{8,2},{9,3},{10,... | collective-permute-start | bytes 368648 | tf_op jit(solution)/shard_map/ppermute | solution.py:60
  20.3 3.6 %collective-permute-start.3 = (bf16[96,640]{1,0:T(8,128)(2,1)S(1)}, bf16[96,640]{1,0:T(8,128)(2,1)}, u32[]{:S(2)}, u32[]{:S(2)}) collective-permute-start(bf16[96,640]{1,0:T(8,128)(2,1)S(1)} %pack_heads.1), channel_id=1, source_target_pairs={{0,3},{1,2},{2,11},{3,10},{4,7},{5,6},{6,15},{7,14},{8,1},{9,0},{1... | collective-permute-start | bytes 368648 | tf_op jit(solution)/shard_map/ppermute | solution.py:60
  41.0 3.1 collective-permute-start.12
  48.2 9.0 %collective-permute-done.10 = bf16[1,2,2,96,640]{4,3,2,1,0:T(8,128)(2,1)S(1)} collective-permute-done((bf16[1,2,2,96,640]{4,3,2,1,0:T(8,128)(2,1)S(1)}, bf16[1,2,2,96,640]{4,3,2,1,0:T(8,128)(2,1)S(1)}, u32[]{:S(2)}, u32[]{:S(2)}) %collective-permute-start.10) | collective-permute-done | bytes 491552 | tf_op jit(solution)/shard_map/ppermute | solution.py:44
  59.7 6.0 %qkv.1 = (bf16[1024,384]{1,0:T(8,128)(2,1)S(1)}, bf16[2048,384]{1,0:T(8,128)(2,1)S(1)}, bf16[2048,384]{1,0:T(8,128)(2,1)S(1)}) custom-call(bf16[2048,768]{1,0:T(8,128)(2,1)S(1)} %pad_maximum_fusion.x_ref, bf16[768,640]{1,0:T(8,128)(2,1)S(1)} %bitcast.117, bf16[768,640]{1,0:T(8,128)(2,1)S(1)} %bitcast.114), custom_call_target="tpu_custom_call" | custom-call | flops 6899999744 | bytes 1048576 | tf_op jit(solution)/shard_map/qkv/pallas_call | solution.py:468
  79.2 8.3 %attn_fwd.2 = (bf16[512,384]{1,0:T(8,128)(2,1)S(1)}, f32[3,1,1024]{2,1,0:T(1,128)S(1)}) custom-call(s32[8]{0:T(128)S(1)} %compare_select_fusion.ends, bf16[1024,384]{1,0:T(8,128)(2,1)S(1)} %copy-done.48, bf16[2048,384]{1,0:T(8,128)(2,1)S(1)} %get-tuple-element.158.k_ref, bf16[2048,384]{1,0:T(8,128)(2,1)S(1)} %copy-done.45), custom_call_target="tpu_custom_call" | custom-call | flops 11500000256 | bytes 1048576 | tf_op jit(solution)/shard_map/attn_fwd/pallas_call | solution.py:345
  87.9 4.8 %collective-permute-start.18 = (bf16[2,2,1,96,1152]{4,3,2,1,0:T(8,128)(2,1)S(1)}, bf16[2,2,1,96,1152]{4,3,2,1,0:T(8,128)(2,1)S(1)}, u32[]{:S(2)}, u32[]{:S(2)}) collective-permute-start(bf16[2,2,1,96,1152]{4,3,2,1,0:T(8,128)(2,1)S(1)} %pad_maximum_fusion.10), channel_id=1, source_target_pairs={{0,4},{4,0},{1,5},{5,1},{2,6},{6,2},{3,7},{7,3},{8,12},{12,8},{9,1... | collective-permute-start | bytes 2654216 | tf_op jit(solution)/shard_map/ppermute | solution.py:44
  93.1 9.5 %attn_fwd.3 = (bf16[512,384]{1,0:T(8,128)(2,1)S(1)}, f32[3,1,1024]{2,1,0:T(1,128)S(1)}) custom-call(s32[8]{0:T(128)S(1)} %compare_select_fusion.ends, bf16[1024,384]{1,0:T(8,128)(2,1)S(1)} %copy-done.48, bf16[2048,384]{1,0:T(8,128)(2,1)S(1)} %copy-done.42, bf16[2048,384]{1,0:T(8,128)(2,1)S(1)} %copy-done.45), custom_call_target="tpu_custom_call" | custom-call | flops 11500000256 | bytes 1048576 | tf_op jit(solution)/shard_map/attn_fwd/pallas_call | solution.py:345
  102.7 10.2 %collective-permute-done.18 = bf16[2,2,1,96,1152]{4,3,2,1,0:T(8,128)(2,1)S(1)} collective-permute-done((bf16[2,2,1,96,1152]{4,3,2,1,0:T(8,128)(2,1)S(1)}, bf16[2,2,1,96,1152]{4,3,2,1,0:T(8,128)(2,1)S(1)}, u32[]{:S(2)}, u32[]{:S(2)}) %collective-permute-start.18) | collective-permute-done | bytes 884768 | tf_op jit(solution)/shard_map/ppermute | solution.py:44
  121.0 10.1 %feed_forward.1 = (bf16[1024,768]{1,0:T(8,128)(2,1)S(1)}, f32[1024,128]{1,0:T(8,128)S(1)}, bf16[1024,768]{1,0:T(8,128)(2,1)S(1)}, bf16[1024,1536]{1,0:T(8,128)(2,1)S(1)}, bf16[1024,1536]{1,0:T(8,128)(2,1)S(1)}) custom-call(bf16[1024,768]{1,0:T(8,128)(2,1)S(1)} %broadcast_select_fusion.x_ref, bf16[1024,768]{1,0:T(8,128)(2,1)S(1)} %get-tuple-element.172.mine_ref, ...), custom_call_target="tpu_custom_call" | custom-call | flops 16099999744 | bytes 1048576 | tf_op jit(solution)/shard_map/feed_forward/pallas_call | solution.py:619
  135.9 3.4 %ffn_out.1.mine_ref = bf16[1024,768]{1,0:T(8,128)(2,1)S(1)} custom-call(bf16[1024,1536]{1,0:T(8,128)(2,1)S(1)} %get-tuple-element.178.act_ref, bf16[768,768]{1,0:T(8,128)(2,1)S(1)} %bitcast.130, bf16[768,768]{1,0:T(8,128)(2,1)S(1)} %bitcast.128), custom_call_target="tpu_custom_call" | custom-call | flops 3449999872 | bytes 1048576 | tf_op jit(solution)/shard_map/ffn_out/pallas_call | solution.py:642
  139.9 3.0 collective-permute-done.24.got_ref
  142.9 6.2 %middle.1 = (f32[1024,128]{1,0:T(8,128)S(1)}, f32[1024,768]{1,0:T(8,128)S(1)}, bf16[1024,768]{1,0:T(8,128)(2,1)S(1)}, f32[768,128]{1,0:T(8,128)S(1)}, f32[8,768]{1,0:T(8,128)S(1)}) custom-call(bf16[1024,768]{1,0:T(8,128)(2,1)S(1)} %get-tuple-element.174.normed_ref, bf16[1024,768]{1,0:T(8,128)(2,1)S(1)} %ffn_out.1.mine_ref, ...), custom_call_target="tpu_custom_call" | custom-call | flops 5750000128 | bytes 1048576 | tf_op jit(solution)/shard_map/middle/pallas_call | solution.py:688
  149.1 18.1 %ffn_back.1 = (bf16[2,384,768]{2,1,0:T(8,128)(2,1)}, bf16[2,384,768]{2,1,0:T(8,128)(2,1)}, bf16[2,384,768]{2,1,0:T(8,128)(2,1)}, bf16[2,384,768]{2,1,0:T(8,128)(2,1)}, bf16[1024,768]{1,0:T(8,128)(2,1)S(1)}) custom-call(s32[2]{0:T(128)S(1)} %pad_add_fusion.bits, bf16[1024,768]{1,0:T(8,128)(2,1)S(1)} %get-tuple-element.183.g_ref, ...), custom_call_target="tpu_custom_call" | custom-call | flops 19549999104 | bytes 1048576 | tf_op jit(solution)/shard_map/ffn_back/pallas_call | solution.py:778
  170.7 8.2 %first_back.1 = (f32[1024,768]{1,0:T(8,128)}, bf16[1024,384]{1,0:T(8,128)(2,1)S(1)}, bf16[768,384]{1,0:T(8,128)(2,1)S(1)}, bf16[768,256]{1,0:T(8,128)(2,1)S(1)}) custom-call(bf16[1024,768]{1,0:T(8,128)(2,1)S(1)} %get-tuple-element.186.mine_ref, bf16[1024,768]{1,0:T(8,128)(2,1)S(1)} %collective-permute-done.25.got_ref, f32[1024,768]{1,0:T(8,128)} %copy-done.9, ...), custom_call_target="tpu_custom_call" | custom-call | flops 1150000000 | bytes 1048576 | tf_op jit(solution)/shard_map/first_back/pallas_call | solution.py:854
  179.0 4.0 %collective-permute-start.29 = (f32[256,128]{1,0:T(8,128)S(1)}, f32[256,128]{1,0:T(8,128)S(1)}, u32[]{:S(2)}, u32[]{:S(2)}) collective-permute-start(f32[256,128]{1,0:T(8,128)S(1)} %get-tuple-element.332), channel_id=1, source_target_pairs={{0,0},{1,8},{2,1},{3,9},{4,4},{5,12},{6,5},{7,13},{8,2},{9,10},{10... | collective-permute-start | bytes 393224 | tf_op jit(solution)/shard_map/ppermute | solution.py:60
  184.3 18.3 %attn_bwd.1 = (bf16[1024,384]{1,0:T(8,128)(2,1)S(1)}, bf16[2048,384]{1,0:T(8,128)(2,1)S(1)}, bf16[2048,384]{1,0:T(8,128)(2,1)S(1)}) custom-call(s32[8]{0:T(128)S(1)} %compare_select_fusion.ends, bf16[1024,384]{1,0:T(8,128)(2,1)S(1)} %copy-done.49, bf16[1024,384]{1,0:T(8,128)(2,1)S(1)} %get-tuple-element.194.do_ref, bf16[512,384]{1,0:T(8,128)(2,1)S(1)} %copy-done.28, ...), custom_call_target="tpu_custom_call" | custom-call | flops 3449999872 | bytes 1048576 | tf_op jit(solution)/shard_map/attn_bwd/pallas_call | solution.py:389
  206.0 3.4 %token_grads.2 = (bf16[512,768]{1,0:T(8,128)(2,1)}, bf16[512,768]{1,0:T(8,128)(2,1)S(1)}) custom-call(s32[1]{0:T(128)} %bitcast.34.core, bf16[2048,384]{1,0:T(8,128)(2,1)S(1)} %get-tuple-element.215.refs_0_.refs_1_, bf16[2048,384]{1,0:T(8,128)(2,1)S(1)} %get-tuple-element.216.refs_1_.refs_2_, bf16[768,640]{1,0:T(8,128)(2,1)S(1)} %bitcast.118, ...), custom_call_target="tpu_custom_call" | custom-call | flops 575000000 | bytes 1048576 | tf_op jit(solution)/shard_map/token_grads/pallas_call | solution.py:922
  210.3 4.2 %token_grads.3 = (bf16[512,768]{1,0:T(8,128)(2,1)}, bf16[512,768]{1,0:T(8,128)(2,1)S(1)}) custom-call(s32[1]{0:T(128)} %bitcast.34.core, bf16[1024,384]{1,0:T(8,128)(2,1)S(1)} %get-tuple-element.218.refs_0_, bf16[2048,384]{1,0:T(8,128)(2,1)S(1)} %get-tuple-element.215.refs_0_.refs_1_, bf16[2048,384]{1,0:T(8,128)(2,1)S(1)} %get-tuple-element.216.refs_1_.refs_2_, ...), custom_call_target="tpu_custom_call" | custom-call | flops 575000000 | bytes 1048576 | tf_op jit(solution)/shard_map/token_grads/pallas_call | solution.py:922
  216.8 5.0 %collective-permute-start.34 = (bf16[2,1,2,1,96,768]{5,4,2,0,3,1:T(8,128)(2,1)}, bf16[2,1,2,1,96,768]{5,4,2,0,3,1:T(8,128)(2,1)}, u32[]{:S(2)}, u32[]{:S(2)}) collective-permute-start(bf16[2,1,2,1,96,768]{5,4,2,0,3,1:T(8,128)(2,1)} %constant_dynamic-slice_fusion.6), channel_id=1, source_target_pairs={{0,16},{8,24},{16,0},{24,8},{1,17},{9,25},{17,1},{25,9},{2,18},{10... | collective-permute-start | bytes 1769480 | tf_op jit(solution)/shard_map/ppermute | solution.py:44
  226.3 7.5 %head_grads.1 = (bf16[2,768,512]{2,1,0:T(8,128)(2,1)S(1)}, bf16[2,768,256]{2,1,0:T(8,128)(2,1)S(1)}) custom-call(bf16[2048,768]{1,0:T(8,128)(2,1)} %copy-done.2, bf16[1024,384]{1,0:T(8,128)(2,1)S(1)} %copy-done.8, bf16[2048,384]{1,0:T(8,128)(2,1)S(1)} %get-tuple-element.215.refs_0_.refs_1_, bf16[2048,384]{1,0:T(8,128)(2,1)S(1)} %get-tuple-element.216.refs_1_.refs_2_, ...), custom_call_target="tpu_custom_call" | custom-call | flops 575000000 | bytes 1048576 | tf_op jit(solution)/shard_map/head_grads/pallas_call | solution.py:982
  234.6 4.6 %collective-permute-done.33 = bf16[1,2,1,96,256]{4,3,2,1,0:T(8,128)(2,1)S(1)} collective-permute-done((bf16[1,2,1,96,256]{4,3,2,1,0:T(8,128)(2,1)S(1)}, bf16[1,2,1,96,256]{4,3,2,1,0:T(8,128)(2,1)S(1)}, u32[]{:S(2)}, u32[]{:S(2)}) %collective-permute-start.33) | collective-permute-done | bytes 98336 | tf_op jit(solution)/shard_map/ppermute | solution.py:44
  254.5 13.6 %collective-permute-done.39 = bf16[2,2,2,1,96,256]{5,4,3,2,1,0:T(8,128)(2,1)} collective-permute-done((bf16[2,2,2,1,96,256]{5,4,3,2,1,0:T(8,128)(2,1)}, bf16[2,2,2,1,96,256]{5,4,3,2,1,0:T(8,128)(2,1)}, u32[]{:S(2)}, u32[]{:S(2)}) %collective-permute-start.39) | collective-permute-done | bytes 393248 | tf_op jit(solution)/shard_map/ppermute | solution.py:44
  274.3 2.7 collective-permute-start.46
  277.0 3.4 %collective-permute-done.40 = bf16[2,1,2,1,96,512]{5,4,3,2,1,0:T(8,128)(2,1)S(1)} collective-permute-done((bf16[2,1,2,1,96,512]{5,4,3,2,1,0:T(8,128)(2,1)S(1)}, bf16[2,1,2,1,96,512]{5,4,3,2,1,0:T(8,128)(2,1)S(1)}, u32[]{:S(2)}, u32[]{:S(2)}) %collective-permute-start.40) | collective-permute-done | bytes 393248 | tf_op jit(solution)/shard_map/ppermute | solution.py:44
  280.6 2.8 collective-permute-start.42
  285.9 3.4 %collective-permute-start.48 = (bf16[1024,192]{1,0:T(8,128)(2,1)S(1)}, bf16[1024,192]{1,0:T(8,128)(2,1)S(1)}, u32[]{:S(2)}, u32[]{:S(2)}) collective-permute-start(bf16[1024,192]{1,0:T(8,128)(2,1)S(1)} %get-tuple-element.303), channel_id=1, source_target_pairs={{0,2},{1,10},{2,0},{3,8},{4,6},{5,14},{6,4},{7,12},{8,3},{9,11},{1... | collective-permute-start | bytes 1179656 | tf_op jit(solution)/shard_map/ppermute | solution.py:60
  290.5 3.2 collective-permute-start.45
  295.5 3.2 collective-permute-done.47
  298.7 12.2 %collective-permute-done.48 = bf16[1024,192]{1,0:T(8,128)(2,1)S(1)} collective-permute-done((bf16[1024,192]{1,0:T(8,128)(2,1)S(1)}, bf16[1024,192]{1,0:T(8,128)(2,1)S(1)}, u32[]{:S(2)}, u32[]{:S(2)}) %collective-permute-start.48) | collective-permute-done | bytes 393248 | tf_op jit(solution)/shard_map/ppermute | solution.py:60
  310.8 10.4 %collective-permute-done.44.p2 = bf16[96,768]{1,0:T(8,128)(2,1)S(1)} collective-permute-done((bf16[96,768]{1,0:T(8,128)(2,1)S(1)}, bf16[96,768]{1,0:T(8,128)(2,1)S(1)}, u32[]{:S(2)}, u32[]{:S(2)}) %collective-permute-start.44) | collective-permute-done | bytes 147488 | tf_op jit(solution)/shard_map/ppermute | solution.py:44
  324.3 2.8 copy.38
  (328 shorter events, 103.0 us)
Async XLA Ops:
  7.2 61.6 %all-gather.3.cloned.1.call-start = ((), (), s32[]{:S(2)}) async-start(), calls=%async_computation.2 | async-start | bytes 1843200 | tf_op jit(solution)/shard_map/all_gather | solution.py:1073
  10.4 19.5 %collective-permute-start.4 = (bf16[800,768]{1,0:T(8,128)(2,1)}, bf16[800,768]{1,0:T(8,128)(2,1)}, u32[]{:S(2)}, u32[]{:S(2)}) collective-permute-start(bf16[800,768]{1,0:T(8,128)(2,1)} %dynamic-slice_bitcast_fusion.1), channel_id=1, source_target_pairs={{0,4},{2,6},{4,0},{6,2},{9,13},{11,15},{13,9},{15,11},{16,20},{18,... | collective-permute-start | bytes 3686408 | tf_op jit(solution)/shard_map/ppermute | solution.py:60
  12.4 15.6 %collective-permute-start = (bf16[96,640]{1,0:T(8,128)(2,1)S(1)}, bf16[96,640]{1,0:T(8,128)(2,1)S(1)}, u32[]{:S(2)}, u32[]{:S(2)}) collective-permute-start(bf16[96,640]{1,0:T(8,128)(2,1)S(1)} %pack_heads.1), channel_id=1, source_target_pairs={{0,0},{1,1},{2,8},{3,9},{4,4},{5,5},{6,12},{7,13},{8,2},{9,3},{10,... | collective-permute-start | bytes 368648 | tf_op jit(solution)/shard_map/ppermute | solution.py:60
  30.5 259.0 %reduce-scatter.2.cloned.1.call-start = ((), (), s32[]{:S(2)}) async-start(), calls=%async_computation.1 | async-start | bytes 1720320 | tf_op jit(solution)/shard_map/reduce_scatter | solution.py:1231
  44.2 13.0 %collective-permute-start.10 = (bf16[1,2,2,96,640]{4,3,2,1,0:T(8,128)(2,1)S(1)}, bf16[1,2,2,96,640]{4,3,2,1,0:T(8,128)(2,1)S(1)}, u32[]{:S(2)}, u32[]{:S(2)}) collective-permute-start(bf16[1,2,2,96,640]{4,3,2,1,0:T(8,128)(2,1)S(1)} %pad_maximum_fusion.19), channel_id=1, source_target_pairs={{0,16},{8,24},{16,0},{24,8},{1,17},{9,25},{17,1},{25,9},{2,18},{10... | collective-permute-start | bytes 1474568 | tf_op jit(solution)/shard_map/ppermute | solution.py:44
  45.8 12.7 %collective-permute-start.9 = (bf16[2,2,1,96,640]{4,3,2,1,0:T(8,128)(2,1)S(1)}, bf16[2,2,1,96,640]{4,3,2,1,0:T(8,128)(2,1)S(1)}, u32[]{:S(2)}, u32[]{:S(2)}) collective-permute-start(bf16[2,2,1,96,640]{4,3,2,1,0:T(8,128)(2,1)S(1)} %pad_maximum_fusion.18), channel_id=1, source_target_pairs={{0,4},{4,0},{1,5},{5,1},{2,6},{6,2},{3,7},{7,3},{8,12},{12,8},{9,1... | collective-permute-start | bytes 1474568 | tf_op jit(solution)/shard_map/ppermute | solution.py:44
  76.2 11.5 %collective-permute-start.16 = (bf16[1,2,1,96,1152]{4,3,2,1,0:T(8,128)(2,1)S(1)}, bf16[1,2,1,96,1152]{4,3,2,1,0:T(8,128)(2,1)S(1)}, u32[]{:S(2)}, u32[]{:S(2)}) collective-permute-start(bf16[1,2,1,96,1152]{4,3,2,1,0:T(8,128)(2,1)S(1)} %fusion.6), channel_id=1, source_target_pairs={{0,16},{8,24},{16,0},{24,8},{1,17},{9,25},{17,1},{25,9},{2,18},{10... | collective-permute-start | bytes 1327112 | tf_op jit(solution)/shard_map/ppermute | solution.py:44
  76.3 11.4 %collective-permute-start.15 = (bf16[1,2,1,96,1152]{4,3,2,1,0:T(8,128)(2,1)S(1)}, bf16[1,2,1,96,1152]{4,3,2,1,0:T(8,128)(2,1)S(1)}, u32[]{:S(2)}, u32[]{:S(2)}) collective-permute-start(bf16[1,2,1,96,1152]{4,3,2,1,0:T(8,128)(2,1)S(1)} %fusion.7), channel_id=1, source_target_pairs={{0,4},{4,0},{1,5},{5,1},{2,6},{6,2},{3,7},{7,3},{8,12},{12,8},{9,1... | collective-permute-start | bytes 1327112 | tf_op jit(solution)/shard_map/ppermute | solution.py:44
  77.7 25.0 %collective-permute-start.20 = (bf16[1,2,1,96,768]{4,3,2,1,0:T(8,128)(2,1)S(1)}, bf16[1,2,1,96,768]{4,3,2,1,0:T(8,128)(2,1)S(1)}, u32[]{:S(2)}, u32[]{:S(2)}) collective-permute-start(bf16[1,2,1,96,768]{4,3,2,1,0:T(8,128)(2,1)S(1)} %pad_maximum_fusion.20), channel_id=1, source_target_pairs={{0,16},{8,24},{16,0},{24,8},{1,17},{9,25},{17,1},{25,9},{2,18},{10... | collective-permute-start | bytes 884744 | tf_op jit(solution)/shard_map/ppermute | solution.py:44
  78.9 23.7 %collective-permute-start.19 = (bf16[1,2,1,96,768]{4,3,2,1,0:T(8,128)(2,1)S(1)}, bf16[1,2,1,96,768]{4,3,2,1,0:T(8,128)(2,1)S(1)}, u32[]{:S(2)}, u32[]{:S(2)}) collective-permute-start(bf16[1,2,1,96,768]{4,3,2,1,0:T(8,128)(2,1)S(1)} %pad_maximum_fusion.21), channel_id=1, source_target_pairs={{0,4},{4,0},{1,5},{5,1},{2,6},{6,2},{3,7},{7,3},{8,12},{12,8},{9,1... | collective-permute-start | bytes 884744 | tf_op jit(solution)/shard_map/ppermute | solution.py:44
  87.9 25.0 %collective-permute-start.18 = (bf16[2,2,1,96,1152]{4,3,2,1,0:T(8,128)(2,1)S(1)}, bf16[2,2,1,96,1152]{4,3,2,1,0:T(8,128)(2,1)S(1)}, u32[]{:S(2)}, u32[]{:S(2)}) collective-permute-start(bf16[2,2,1,96,1152]{4,3,2,1,0:T(8,128)(2,1)S(1)} %pad_maximum_fusion.10), channel_id=1, source_target_pairs={{0,4},{4,0},{1,5},{5,1},{2,6},{6,2},{3,7},{7,3},{8,12},{12,8},{9,1... | collective-permute-start | bytes 2654216 | tf_op jit(solution)/shard_map/ppermute | solution.py:44
  92.8 20.1 %collective-permute-start.17 = (bf16[1,2,2,96,1152]{4,3,2,1,0:T(8,128)(2,1)S(1)}, bf16[1,2,2,96,1152]{4,3,2,1,0:T(8,128)(2,1)S(1)}, u32[]{:S(2)}, u32[]{:S(2)}) collective-permute-start(bf16[1,2,2,96,1152]{4,3,2,1,0:T(8,128)(2,1)S(1)} %pad_maximum_fusion.9), channel_id=1, source_target_pairs={{0,16},{8,24},{16,0},{24,8},{1,17},{9,25},{17,1},{25,9},{2,18},{10... | collective-permute-start | bytes 2654216 | tf_op jit(solution)/shard_map/ppermute | solution.py:44
  118.1 15.9 %collective-permute-start.23 = (bf16[2,2,1,96,768]{4,3,2,1,0:T(8,128)(2,1)S(1)}, bf16[2,2,1,96,768]{4,3,2,1,0:T(8,128)(2,1)S(1)}, u32[]{:S(2)}, u32[]{:S(2)}) collective-permute-start(bf16[2,2,1,96,768]{4,3,2,1,0:T(8,128)(2,1)S(1)} %pad_maximum_fusion.12), channel_id=1, source_target_pairs={{0,4},{4,0},{1,5},{5,1},{2,6},{6,2},{3,7},{7,3},{8,12},{12,8},{9,1... | collective-permute-start | bytes 1769480 | tf_op jit(solution)/shard_map/ppermute | solution.py:44
  119.0 15.1 %collective-permute-start.22 = (bf16[1,2,2,96,768]{4,3,2,1,0:T(8,128)(2,1)S(1)}, bf16[1,2,2,96,768]{4,3,2,1,0:T(8,128)(2,1)S(1)}, u32[]{:S(2)}, u32[]{:S(2)}) collective-permute-start(bf16[1,2,2,96,768]{4,3,2,1,0:T(8,128)(2,1)S(1)} %pad_maximum_fusion.11), channel_id=1, source_target_pairs={{0,16},{8,24},{16,0},{24,8},{1,17},{9,25},{17,1},{25,9},{2,18},{10... | collective-permute-start | bytes 1769480 | tf_op jit(solution)/shard_map/ppermute | solution.py:44
  167.6 35.0 %collective-permute-start.26 = (bf16[2,384,768]{2,1,0:T(8,128)(2,1)}, bf16[2,384,768]{2,1,0:T(8,128)(2,1)}, u32[]{:S(2)}, u32[]{:S(2)}) collective-permute-start(bf16[2,384,768]{2,1,0:T(8,128)(2,1)} %get-tuple-element.202), channel_id=1, source_target_pairs={{0,4},{4,0},{1,5},{5,1},{2,6},{6,2},{3,7},{7,3},{8,12},{12,8},{9,1... | collective-permute-start | bytes 3538952 | tf_op jit(solution)/shard_map/ppermute | solution.py:44
  168.2 34.4 %collective-permute-start.27 = (bf16[2,384,768]{2,1,0:T(8,128)(2,1)}, bf16[2,384,768]{2,1,0:T(8,128)(2,1)}, u32[]{:S(2)}, u32[]{:S(2)}) collective-permute-start(bf16[2,384,768]{2,1,0:T(8,128)(2,1)} %get-tuple-element.203), channel_id=1, source_target_pairs={{0,16},{8,24},{16,0},{24,8},{1,17},{9,25},{17,1},{25,9},{2,18},{10... | collective-permute-start | bytes 3538952 | tf_op jit(solution)/shard_map/ppermute | solution.py:44
  179.0 23.7 %collective-permute-start.29 = (f32[256,128]{1,0:T(8,128)S(1)}, f32[256,128]{1,0:T(8,128)S(1)}, u32[]{:S(2)}, u32[]{:S(2)}) collective-permute-start(f32[256,128]{1,0:T(8,128)S(1)} %get-tuple-element.332), channel_id=1, source_target_pairs={{0,0},{1,8},{2,1},{3,9},{4,4},{5,12},{6,5},{7,13},{8,2},{9,10},{10... | collective-permute-start | bytes 393224 | tf_op jit(solution)/shard_map/ppermute | solution.py:60
  183.0 19.6 %collective-permute-start.30 = (f32[256,128]{1,0:T(8,128)S(1)}, f32[256,128]{1,0:T(8,128)S(1)}, u32[]{:S(2)}, u32[]{:S(2)}) collective-permute-start(f32[256,128]{1,0:T(8,128)S(1)} %get-tuple-element.331), channel_id=1, source_target_pairs={{0,1},{1,9},{2,0},{3,8},{4,5},{5,13},{6,4},{7,12},{8,3},{9,11},{10... | collective-permute-start | bytes 393224 | tf_op jit(solution)/shard_map/ppermute | solution.py:60
  183.1 19.6 %collective-permute-start.28 = (bf16[1,2,2,96,256]{4,3,2,1,0:T(8,128)(2,1)S(1)}, bf16[1,2,2,96,256]{4,3,2,1,0:T(8,128)(2,1)S(1)}, u32[]{:S(2)}, u32[]{:S(2)}) collective-permute-start(bf16[1,2,2,96,256]{4,3,2,1,0:T(8,128)(2,1)S(1)} %constant_dynamic-slice_fusion.8), channel_id=1, source_target_pairs={{0,16},{8,24},{16,0},{24,8},{1,17},{9,25},{17,1},{25,9},{2,18},{10... | collective-permute-start | bytes 589832 | tf_op jit(solution)/shard_map/ppermute | solution.py:44
  215.4 23.9 %collective-permute-start.31 = (bf16[512,768]{1,0:T(8,128)(2,1)}, bf16[512,768]{1,0:T(8,128)(2,1)}, u32[]{:S(2)}, u32[]{:S(2)}) collective-permute-start(bf16[512,768]{1,0:T(8,128)(2,1)} %get-tuple-element.224), channel_id=1, source_target_pairs={{0,8},{8,0},{16,24},{24,16},{1,9},{9,1},{17,25},{25,17},{2,10},{10... | collective-permute-start | bytes 2359304 | tf_op jit(solution)/shard_map/ppermute | solution.py:44
  215.4 23.9 %collective-permute-start.32 = (bf16[512,768]{1,0:T(8,128)(2,1)}, bf16[512,768]{1,0:T(8,128)(2,1)}, u32[]{:S(2)}, u32[]{:S(2)}) collective-permute-start(bf16[512,768]{1,0:T(8,128)(2,1)} %get-tuple-element.225), channel_id=1, source_target_pairs={{0,8},{8,0},{16,24},{24,16},{1,9},{9,1},{17,25},{25,17},{2,10},{10... | collective-permute-start | bytes 2359304 | tf_op jit(solution)/shard_map/ppermute | solution.py:44
  216.8 22.5 %collective-permute-start.34 = (bf16[2,1,2,1,96,768]{5,4,2,0,3,1:T(8,128)(2,1)}, bf16[2,1,2,1,96,768]{5,4,2,0,3,1:T(8,128)(2,1)}, u32[]{:S(2)}, u32[]{:S(2)}) collective-permute-start(bf16[2,1,2,1,96,768]{5,4,2,0,3,1:T(8,128)(2,1)} %constant_dynamic-slice_fusion.6), channel_id=1, source_target_pairs={{0,16},{8,24},{16,0},{24,8},{1,17},{9,25},{17,1},{25,9},{2,18},{10... | collective-permute-start | bytes 1769480 | tf_op jit(solution)/shard_map/ppermute | solution.py:44
  222.6 16.7 %collective-permute-start.35 = (bf16[2,1,2,1,96,768]{5,4,3,2,0,1:T(8,128)(2,1)}, bf16[2,1,2,1,96,768]{5,4,3,2,0,1:T(8,128)(2,1)}, u32[]{:S(2)}, u32[]{:S(2)}) collective-permute-start(bf16[2,1,2,1,96,768]{5,4,3,2,0,1:T(8,128)(2,1)} %constant_dynamic-slice_fusion.5), channel_id=1, source_target_pairs={{0,4},{4,0},{1,5},{5,1},{2,6},{6,2},{3,7},{7,3},{8,12},{12,8},{9,1... | collective-permute-start | bytes 1769480 | tf_op jit(solution)/shard_map/ppermute | solution.py:44
  223.7 15.6 %collective-permute-start.33 = (bf16[1,2,1,96,256]{4,3,2,1,0:T(8,128)(2,1)S(1)}, bf16[1,2,1,96,256]{4,3,2,1,0:T(8,128)(2,1)S(1)}, u32[]{:S(2)}, u32[]{:S(2)}) collective-permute-start(bf16[1,2,1,96,256]{4,3,2,1,0:T(8,128)(2,1)S(1)} %constant_dynamic-slice_fusion.7), channel_id=1, source_target_pairs={{0,4},{4,0},{1,5},{5,1},{2,6},{6,2},{3,7},{7,3},{8,12},{12,8},{9,1... | collective-permute-start | bytes 294920 | tf_op jit(solution)/shard_map/ppermute | solution.py:44
  241.7 26.4 %collective-permute-start.37 = (bf16[512,768]{1,0:T(8,128)(2,1)}, bf16[512,768]{1,0:T(8,128)(2,1)}, u32[]{:S(2)}, u32[]{:S(2)}) collective-permute-start(bf16[512,768]{1,0:T(8,128)(2,1)} %add_convert_fusion.4), channel_id=1, source_target_pairs={{0,4},{4,0},{1,5},{5,1},{2,6},{6,2},{3,7},{7,3},{8,12},{12,8},{9,1... | collective-permute-start | bytes 2359304 | tf_op jit(solution)/shard_map/ppermute | solution.py:44
  243.9 24.1 %collective-permute-start.38 = (bf16[2,1,2,2,96,512]{5,4,3,2,1,0:T(8,128)(2,1)}, bf16[2,1,2,2,96,512]{5,4,3,2,1,0:T(8,128)(2,1)S(1)}, u32[]{:S(2)}, u32[]{:S(2)}) collective-permute-start(bf16[2,1,2,2,96,512]{5,4,3,2,1,0:T(8,128)(2,1)} %constant_dynamic-slice_fusion.3), channel_id=1, source_target_pairs={{0,16},{8,24},{16,0},{24,8},{1,17},{9,25},{17,1},{25,9},{2,18},{10... | collective-permute-start | bytes 2359304 | tf_op jit(solution)/shard_map/ppermute | solution.py:44
  250.4 17.7 %collective-permute-start.39 = (bf16[2,2,2,1,96,256]{5,4,3,2,1,0:T(8,128)(2,1)}, bf16[2,2,2,1,96,256]{5,4,3,2,1,0:T(8,128)(2,1)}, u32[]{:S(2)}, u32[]{:S(2)}) collective-permute-start(bf16[2,2,2,1,96,256]{5,4,3,2,1,0:T(8,128)(2,1)} %constant_dynamic-slice_fusion.2), channel_id=1, source_target_pairs={{0,4},{4,0},{1,5},{5,1},{2,6},{6,2},{3,7},{7,3},{8,12},{12,8},{9,1... | collective-permute-start | bytes 1179656 | tf_op jit(solution)/shard_map/ppermute | solution.py:44
  284.0 14.7 %collective-permute-start.47 = (bf16[1024,192]{1,0:T(8,128)(2,1)S(1)}, bf16[1024,192]{1,0:T(8,128)(2,1)S(1)}, u32[]{:S(2)}, u32[]{:S(2)}) collective-permute-start(bf16[1024,192]{1,0:T(8,128)(2,1)S(1)} %get-tuple-element.304), channel_id=1, source_target_pairs={{0,0},{1,8},{2,2},{3,10},{4,4},{5,12},{6,6},{7,14},{8,1},{9,9},{10... | collective-permute-start | bytes 1179656 | tf_op jit(solution)/shard_map/ppermute | solution.py:60
  285.9 24.9 %collective-permute-start.48 = (bf16[1024,192]{1,0:T(8,128)(2,1)S(1)}, bf16[1024,192]{1,0:T(8,128)(2,1)S(1)}, u32[]{:S(2)}, u32[]{:S(2)}) collective-permute-start(bf16[1024,192]{1,0:T(8,128)(2,1)S(1)} %get-tuple-element.303), channel_id=1, source_target_pairs={{0,2},{1,10},{2,0},{3,8},{4,6},{5,14},{6,4},{7,12},{8,3},{9,11},{1... | collective-permute-start | bytes 1179656 | tf_op jit(solution)/shard_map/ppermute | solution.py:60
  290.2 20.6 %collective-permute-start.43 = (bf16[96,768]{1,0:T(8,128)(2,1)}, bf16[96,768]{1,0:T(8,128)(2,1)S(1)}, u32[]{:S(2)}, u32[]{:S(2)}) collective-permute-start(bf16[96,768]{1,0:T(8,128)(2,1)} %get-tuple-element.321), channel_id=1, source_target_pairs={{0,1},{1,0},{2,3},{3,2},{4,5},{5,4},{6,7},{7,6},{8,9},{9,8},{10,11... | collective-permute-start | bytes 442376 | tf_op jit(solution)/shard_map/ppermute | solution.py:44
  290.2 31.0 %collective-permute-start.44 = (bf16[96,768]{1,0:T(8,128)(2,1)S(1)}, bf16[96,768]{1,0:T(8,128)(2,1)S(1)}, u32[]{:S(2)}, u32[]{:S(2)}) collective-permute-start(bf16[96,768]{1,0:T(8,128)(2,1)S(1)} %get-tuple-element.320), channel_id=1, source_target_pairs={{0,2},{1,3},{2,0},{3,1},{4,6},{5,7},{6,4},{7,5},{8,10},{9,11},{10,... | collective-permute-start | bytes 442376 | tf_op jit(solution)/shard_map/ppermute | solution.py:44
  290.5 30.7 %collective-permute-start.45 = (bf16[96,768]{1,0:T(8,128)(2,1)S(1)}, bf16[96,768]{1,0:T(8,128)(2,1)S(1)}, u32[]{:S(2)}, u32[]{:S(2)}) collective-permute-start(bf16[96,768]{1,0:T(8,128)(2,1)S(1)} %get-tuple-element.319), channel_id=1, source_target_pairs={{0,3},{1,2},{2,1},{3,0},{4,7},{5,6},{6,5},{7,4},{8,11},{9,10},{10,... | collective-permute-start | bytes 442376 | tf_op jit(solution)/shard_map/ppermute | solution.py:44
  (91 other events, 746.8 us)
Sparse Core Ops, SparseCore 0:
  30.7 35.3 all-gather.2
  254.6 33.4 reduce-scatter.1
